TPU v7x, 128 devices: a whole 4x4x4 slice. The times are simulated.
128 devices in a mesh: island: 8 (over x, y_hi), fsdp: 16 (over z, y_lo, core).
Axes of the slice: x: 4, y: 4 (y_hi: 2, y_lo: 2; y = y_hi * 2 + y_lo), z: 4, core: 2. Of those that a mesh axis runs over, the one named last changes fastest.
Arguments:
- delta: bfloat16 [8, 8192, 8192], P('island', 'fsdp'), may hold values from -24 to 24
- sketch: bfloat16 [8192, 256], P('fsdp'), may hold values from -0.0625 to 0.0625
- params: float32 [8192, 8192], P('fsdp', 'island'), may hold values from -6 to 6
- momentum: float32 [8192, 8192], P('fsdp', 'island'), may hold values from -3 to 3
Outputs:
- new_params: float32 [8192, 8192], P('fsdp', 'island')
- new_momentum: float32 [8192, 8192], P('fsdp', 'island')
All inputs are finite; a program needn't handle non-finite values. Where the computation divides by a largest or mean magnitude, that divisor is 1e-20 or more.
Results may differ from a plain program's by a relative error of at most 0.01.
Values may be sent and summed in bfloat16 or wider, within the bound.
No kernel may reach another device: no remote copies, remote signals or barrier semaphores. Data moves between devices by JAX's collectives and lax.ppermute only.
A program may use at most 128 MiB of HBM per device.

v0:
```python
import jax
import jax.numpy as jnp
from jax import lax
from jax.sharding import PartitionSpec as P

BLK = 128


def compress(values, rank):
    count = values.shape[0]
    blocks = values.reshape(count, rank // BLK, BLK)
    scale = (jnp.max(jnp.abs(blocks), axis=2) + 1e-06).astype(jnp.bfloat16)
    code = (blocks / scale.astype(jnp.float32)[:, :, None]).astype(jnp.bfloat16)
    return (code.reshape(count, rank), scale)


def body(delta, sketch, params, momentum):
    local = delta[0]
    rows = local.shape[0]
    width = local.shape[1]
    rank = sketch.shape[1]
    nblocks = rank // BLK
    sketched = jnp.dot(
        local,
        lax.all_gather(sketch, "fsdp", axis=0, tiled=True),
        preferred_element_type=jnp.float32,
    )
    local_gram = jnp.dot(
        sketched.T, sketched, precision=lax.Precision.HIGHEST, preferred_element_type=jnp.float32
    )
    chol = jnp.linalg.cholesky(lax.psum(local_gram, "fsdp"))
    basis = lax.linalg.triangular_solve(
        chol, sketched, left_side=False, lower=True, transpose_a=True
    )
    basis_b = basis.astype(jnp.bfloat16)
    block = local
    coef = lax.psum(
        jnp.einsum("rc,rk->ck", block, basis_b, preferred_element_type=jnp.float32), "fsdp"
    )
    code_b, scale_b = compress(coef, rank)
    code_q, scale_q = compress(basis, rank)
    islands = lax.axis_size("island")
    owned = width // islands
    got_code, got_scale = (
        lax.all_to_all(
            code_b.reshape(islands, owned, rank), "island", split_axis=0, concat_axis=0, tiled=True
        ),
        lax.all_to_all(
            scale_b.reshape(islands, owned, nblocks),
            "island",
            split_axis=0,
            concat_axis=0,
            tiled=True,
        ),
    )
    total = jnp.zeros((rows, owned), jnp.float32)
    piece_code = lax.all_gather(code_q[None], "island", axis=0, tiled=True)
    piece_scale = lax.all_gather(scale_q[None], "island", axis=0, tiled=True)
    for block in range(nblocks):
        lower = block * BLK
        part = jnp.einsum(
            "nrk,nck->nrc",
            piece_code[:, :, lower : lower + BLK],
            got_code[:, :, lower : lower + BLK],
            preferred_element_type=jnp.float32,
        )
        weight = (
            piece_scale[:, :, block].astype(jnp.float32)[:, :, None]
            * got_scale[:, :, block].astype(jnp.float32)[:, None, :]
        )
        total = total + jnp.sum(weight * part, axis=0)
    average = total / islands
    new_momentum = 0.9 * momentum + average
    new_params = params - 0.7 * (average + 0.9 * new_momentum)
    return (new_params, new_momentum)


def solution(mesh):
    placed = (P("island", "fsdp", None), P("fsdp", None), P("fsdp", "island"), P("fsdp", "island"))
    return jax.shard_map(
        body,
        mesh=mesh,
        in_specs=placed,
        out_specs=(P("fsdp", "island"), P("fsdp", "island")),
        check_vma=False,
    )
```

profile of v0, /device:TPU:1, one launch (start us, length us, event | category | flops | bytes accessed | tf_op | source)
XLA Modules:
  0.0 600.6 jit_solution(12410636656227820253)
XLA Ops:
  7.2 0.0 all-gather.4.cloned.1.call-start
  7.2 0.7 all-gather.4.cloned.1.call-update
  7.9 0.0 all-reduce.4.cloned.1.call-start
  7.9 42.8 %all-gather.4.cloned.1.call-done = bf16[8192,256]{1,0:T(8,128)(2,1)} async-done(((bf16[512,256]{1,0:T(8,128)(2,1)}), bf16[8192,256]{1,0:T(8,128)(2,1)}) %all-gather.4.cloned.1.call-update) | async-done | bytes 4194320 | tf_op jit(solution)/shard_map/all_gather | solution.py:25
  50.8 6.9 %fusion.1 = f32[512,256]{1,0:T(8,128)S(1)} fusion(bf16[8192,256]{1,0:T(8,128)(2,1)} %all-gather.4.cloned.1.call-done, bf16[1,512,8192]{2,1,0:T(8,128)(2,1)} %param.4), kind=kOutput, calls=%fused_computation.7 | convolution fusion | flops 2147483648 | bytes 13107200 | tf_op jit(solution)/shard_map/dot_general | solution.py:23
  57.7 1.7 fusion.24
  59.4 0.0 all-reduce.4.cloned.1.call-update
  59.4 0.2 all-reduce.6.cloned.1.call-start
  59.7 116.2 %all-reduce.4.cloned.1.call-done = f32[256,256]{0,1:T(8,128)} async-done(((f32[256,256]{0,1:T(8,128)}), f32[256,256]{0,1:T(8,128)}) %all-reduce.4.cloned.1.call-update) | async-done | bytes 262160 | tf_op jit(solution)/shard_map/psum | solution.py:31
  175.9 1.1 copy.13
  177.0 1.0 fusion.13
  178.0 11.7 %cholesky.50 = f32[128,128]{1,0:T(8,128)S(1)} custom-call(f32[128,128]{1,0:T(8,128)S(1)} %cholesky.118), custom_call_target="Cholesky" | custom-call | tf_op jit(solution)/shard_map/jit(cholesky)/cholesky | solution.py:31
  189.7 9.8 %custom-call.14 = f32[1,128,128]{1,2,0:T(8,128)S(1)} custom-call(f32[1,128,128]{2,1,0:T(8,128)S(1)} %get-tuple-element.27), custom_call_target="InvertDiagBlocksLowerTriangular" | custom-call | tf_op jit(solution)/shard_map/jit(cholesky)/cholesky | solution.py:31
  199.6 0.2 constant_dynamic-update-slice_fusion.1
  199.8 0.3 convolution_subtract_fusion.1
  200.1 11.7 %cholesky.105 = f32[128,128]{1,0:T(8,128)S(1)} custom-call(f32[128,128]{1,0:T(8,128)S(1)} %convolution_subtract_fusion.1), custom_call_target="Cholesky" | custom-call | tf_op jit(solution)/shard_map/jit(cholesky)/cholesky | solution.py:31
  211.8 0.7 compare_reduce_fusion
  213.9 0.1 triangular_solve.64
  214.0 4.3 while.1
  214.2 0.6 fusion.33
  214.8 1.4 bitcast_dynamic-update-slice_fusion.2
  216.2 0.6 fusion.33
  216.8 1.4 bitcast_dynamic-update-slice_fusion.2
  218.3 19.7 %custom-call.15 = f32[2,128,128]{1,2,0:T(8,128)S(1)} custom-call(f32[2,128,128]{2,1,0:T(8,128)S(1)} %get-tuple-element.9), custom_call_target="InvertDiagBlocksLowerTriangular" | custom-call | tf_op jit(solution)/shard_map/triangular_solve | solution.py:32
  237.9 0.4 fusion.11
  238.4 0.6 convolution_subtract_fusion
  239.0 0.4 fusion.14
  239.4 8.9 %convolution_bitcast_fusion = f32[8192,256]{0,1:T(8,128)} fusion(bf16[1,512,8192]{2,1,0:T(8,128)(2,1)} %param.4, f32[512,128]{0,1:T(8,128)S(1)} %fusion.14, f32[512,128]{0,1:T(8,128)S(1)} %fusion.11), kind=kOutput, calls=%fused_computation.4 | convolution fusion | flops 2148007936 | bytes 17301504 | tf_op jit(solution)/shard_map/rc,rk->ck/dot_general | solution.py:38
  248.3 0.0 all-reduce.6.cloned.1.call-update
  248.4 0.0 all-gather.6.cloned.1.call-start
  248.5 0.8 copy.15
  249.4 0.0 all-gather.6.cloned.1.call-update
  249.4 193.1 %all-reduce.6.cloned.1.call-done = f32[8192,256]{0,1:T(8,128)} async-done(((f32[8192,256]{0,1:T(8,128)}), f32[8192,256]{0,1:T(8,128)}) %all-reduce.6.cloned.1.call-update) | async-done | bytes 8388624 | tf_op jit(solution)/shard_map/psum | solution.py:37
  442.5 3.8 bitcast_reduce_fusion
  446.3 0.7 add_convert_fusion
  447.0 3.1 copy.16
  450.1 16.7 %div.47 = f32[8192,2,128]{2,1,0:T(2,128)} broadcast(f32[8192,2]{1,0:T(8,128)} %copy.16), dimensions={0,1} | broadcast | bytes 8454144 | tf_op jit(solution)/shard_map/div | solution.py:13
  466.8 11.5 %div.48 = f32[8,1024,256]{2,1,0:T(8,128)} reshape(f32[8192,2,128]{2,1,0:T(2,128)} %div.47) | data formatting | bytes 16777216 | tf_op jit(solution)/shard_map/div | solution.py:13
  478.3 6.1 %all-to-all-start = ((bf16[8,1024,2]{1,2,0:T(2,128)(2,1)}), bf16[8,1024,2]{1,2,0:T(2,128)(2,1)S(1)}, u32[]{:S(2)}, u32[]{:S(2)}) async-start(bf16[8,1024,2]{1,2,0:T(2,128)(2,1)} %bitcast.10), calls=%async_computation | async-start | bytes 65536 | tf_op jit(solution)/shard_map/all_to_all | solution.py:48
  484.5 9.0 %copy.19 = f32[8192,256]{1,0:T(8,128)} copy(f32[8192,256]{0,1:T(8,128)} %all-reduce.6.cloned.1.call-done) | data formatting | bytes 16777216 | tf_op jit(solution)/shard_map/reshape | solution.py:11
  493.5 9.0 %divide_convert_fusion = bf16[8,1024,256]{2,1,0:T(8,128)(2,1)} fusion(f32[8,1024,256]{2,1,0:T(8,128)} %bitcast.73, f32[8,1024,256]{2,1,0:T(8,128)} %div.48), kind=kLoop, calls=%fused_computation.9 | loop fusion | flops 4194304 | bytes 20971520 | tf_op jit(solution)/shard_map/convert_element_type | solution.py:13
  502.5 6.6 %all-to-all-start.1 = ((bf16[8,1024,256]{2,1,0:T(8,128)(2,1)}), bf16[8,1024,256]{2,1,0:T(8,128)(2,1)}, u32[]{:S(2)}, u32[]{:S(2)}) async-start(bf16[8,1024,256]{2,1,0:T(8,128)(2,1)} %divide_convert_fusion), calls=%async_computation.1 | async-start | bytes 8388608 | tf_op jit(solution)/shard_map/all_to_all | solution.py:45
  509.1 72.2 %all-gather = bf16[4096,2]{0,1:T(2,128)(2,1)S(1)} all-gather(bf16[512,2]{0,1:T(2,128)(2,1)S(1)} %get-tuple-element.21), channel_id=2, replica_groups=mesh['island'=8,'fsdp'=16] {'island'}, dimensions={0}, use_global_device_ids=true | all-gather | bytes 18432 | tf_op jit(solution)/shard_map/all_gather | solution.py:58
  581.4 0.0 all-gather.6.cloned.1.call-done
  581.5 4.8 multiply_reduce_fusion
  586.2 0.0 copy-start
  586.3 4.7 multiply_reduce_fusion.1
  591.0 3.0 multiply_subtract_fusion
  (24 shorter events, 0.3 us)
Async XLA Ops:
  7.2 43.6 %all-gather.4.cloned.1.call-start = ((), (), s32[]{:S(2)}) async-start(), calls=%async_computation.2 | async-start | bytes 4456448 | tf_op jit(solution)/shard_map/all_gather | solution.py:25
  7.9 168.0 %all-reduce.4.cloned.1.call-start = ((), (), s32[]{:S(2)}) async-start(), calls=%async_computation.3 | async-start | bytes 524288 | tf_op jit(solution)/shard_map/psum | solution.py:31
  59.4 383.1 %all-reduce.6.cloned.1.call-start = ((), (), s32[]{:S(2)}) async-start(), calls=%async_computation.4 | async-start | bytes 16777216 | tf_op jit(solution)/shard_map/psum | solution.py:37
  248.4 333.1 %all-gather.6.cloned.1.call-start = ((), (), s32[]{:S(2)}) async-start(), calls=%async_computation.5 | async-start | bytes 2359296 | tf_op jit(solution)/shard_map/all_gather | solution.py:57
  478.3 24.1 %all-to-all-start = ((bf16[8,1024,2]{1,2,0:T(2,128)(2,1)}), bf16[8,1024,2]{1,2,0:T(2,128)(2,1)S(1)}, u32[]{:S(2)}, u32[]{:S(2)}) async-start(bf16[8,1024,2]{1,2,0:T(2,128)(2,1)} %bitcast.10), calls=%async_computation | async-start | bytes 65536 | tf_op jit(solution)/shard_map/all_to_all | solution.py:48
  502.5 79.0 %all-to-all-start.1 = ((bf16[8,1024,256]{2,1,0:T(8,128)(2,1)}), bf16[8,1024,256]{2,1,0:T(8,128)(2,1)}, u32[]{:S(2)}, u32[]{:S(2)}) async-start(bf16[8,1024,256]{2,1,0:T(8,128)(2,1)} %divide_convert_fusion), calls=%async_computation.1 | async-start | bytes 8388608 | tf_op jit(solution)/shard_map/all_to_all | solution.py:45
  581.4 4.8 copy-start.2
  586.2 4.7 copy-start
  586.3 4.7 copy-start.1
Sparse Core Ops, SparseCore 0:
  9.7 41.0 all-gather.3
  59.5 116.3 all-reduce.3
  248.5 193.9 all-reduce.5
  445.5 54.2 all-gather.5
where the time goes:
time: 611 us; the launch traced here: 601 us
  waiting for transfers between devices  353 us (58%)
  blocking collectives  72.2 us (12%)
  other arithmetic  71.4 us (12%)
  local copies, waits for them, and re-layouts  46.5 us (8%)
  matrix products  28.9 us (5%)
  between operations  15.3 us (3%)
  starting transfers between devices  13.1 us (2%)
    psum x1, waiting for transfers between devices, body(): lax.psum(jnp.einsum('rc,rk->ck', block, basis_b, preferred_element_type=j...  193 us
    psum x1, waiting for transfers between devices, body(): chol = jnp.linalg.cholesky(lax.psum(local_gram, 'fsdp'))  116 us
    all_gather x1, blocking collectives, body(): piece_scale = lax.all_gather(scale_q[None], 'island', axis=0, tiled=True)  72.2 us
    all_gather x1, waiting for transfers between devices, body(): lax.all_gather(sketch, 'fsdp', axis=0, tiled=True)  42.8 us
    another operation x6, other arithmetic, body(): chol = jnp.linalg.cholesky(lax.psum(local_gram, 'fsdp'))  34 us
    div x2, local copies, waits for them, and re-layouts, compress(): code = (blocks / scale.astype(jnp.float32)[:, :, None]).astype(jnp.bfloat16)  28.2 us
    another operation x3, other arithmetic, body(): lax.linalg.triangular_solve(chol, sketched, left_side=False, lower=True,...  19.7 us
  transfers between devices with their start and end apart: 6, of which 3 were waited for; matrix products, arithmetic and copies ran while one was open for 9% of the time, Pallas kernels for 0%

commit v1 on v0

v1 whole, which is shorter than its diff:
```python
import functools

import jax
import jax.numpy as jnp
import numpy as np
from jax import lax
from jax.experimental import pallas as pl
from jax.experimental.pallas import tpu as pltpu
from jax.sharding import Mesh, PartitionSpec as P

BLK = 128
AXES = ("x", "yh", "z", "yl", "core")
SIZES = (4, 2, 4, 2, 2)
ISLANDS = 8
HIGH = lax.Precision.HIGHEST
F32 = jnp.float32
BF16 = jnp.bfloat16


def move(value, where):
    pairs = []
    for c in np.ndindex(*SIZES):
        d = tuple(a % b for a, b in zip(where(*c), SIZES))
        pairs.append((int(np.ravel_multi_index(c, SIZES)), int(np.ravel_multi_index(d, SIZES))))
    return lax.ppermute(value, AXES, pairs)


def shift(value, dx=0, dh=0, dz=0, dl=0, dc=0):
    return move(value, lambda x, h, z, l, c: (x + dx, h + dh, z + dz, l + dl, c + dc))


def recode(values, axis):
    scale = (jnp.max(jnp.abs(values), axis=axis, keepdims=True) + 1e-06).astype(BF16).astype(F32)
    code = (values / scale).astype(BF16)
    return (code.astype(F32) * scale).astype(BF16)


VMEM = pl.BlockSpec(memory_space=pltpu.VMEM)
FAR = pl.BlockSpec(memory_space=pltpu.HBM)
SMEM = pl.BlockSpec(memory_space=pltpu.SMEM)


def call(kernel, outs, flops, name, smem=True, scratch=(), vmem=16, far=()):
    def run(*args):
        args = [
            pltpu.with_memory_space_constraint(a, pltpu.HBM) if n in far else a
            for n, a in enumerate(args)
        ]
        return pl.pallas_call(
            kernel,
            in_specs=[
                SMEM if smem and n == 0 else FAR if n in far else VMEM for n in range(len(args))
            ],
            out_specs=[VMEM] * len(outs),
            out_shape=[jax.ShapeDtypeStruct(*o) if isinstance(o, tuple) else o for o in outs],
            scratch_shapes=list(scratch),
            compiler_params=pltpu.CompilerParams(vmem_limit_bytes=vmem * 1024 * 1024),
            cost_estimate=pl.CostEstimate(
                flops=int(flops), bytes_accessed=4 * 1024 * 1024, transcendentals=0
            ),
            name=name,
        )(*args)

    return run


def columns(ref, start, count):
    return ref.at[:, pl.ds(pl.multiple_of(start, count), count)]


def fetch(delta, starts, held, sems):
    copies = [
        pltpu.make_async_copy(columns(delta, start, held.shape[2]), held.at[n], sems.at[n])
        for n, start in enumerate(starts)
    ]
    for copy in copies:
        copy.start()
    return copies


def add_products(copies, pieces, out, held):
    for n, (piece, copy) in enumerate(zip(pieces, copies)):
        copy.wait()
        value = jnp.dot(held[n], piece[...], preferred_element_type=F32)
        if n == 0:
            out[...] = value
        else:
            out[...] += value


def early_kernel(layout, place, delta, *refs):
    pieces, (out, held, sems) = refs[: len(layout)], refs[len(layout) :]
    copies = fetch(delta, [place[at] for at in layout], held, sems)
    add_products(copies, pieces, out, held)


def late_kernel(layout, place, delta, *refs):
    pieces, part = refs[: len(layout)], refs[len(layout)]
    gram, rounded, turned, out, held, sems = refs[len(layout) + 1 :]
    copies = fetch(delta, [place[at] for at in layout], held, sems)
    add_products(copies, pieces, out, held)
    total = out[...] + part[...]
    flipped = total.T
    gram[...] = jnp.dot(flipped, total, precision=HIGH, preferred_element_type=F32)
    rounded[...] = total.astype(BF16)
    turned[...] = flipped.astype(BF16)


def product_kernel(place, delta, turned, sent, kept, held, sems):
    width = held.shape[2]
    blocks = [
        (out, parity, g)
        for out, parity in ((sent, 1 - place[0]), (kept, place[0]))
        for g in range(4)
    ]
    copies = fetch(delta, [(2 * g + parity) * width for _, parity, g in blocks], held, sems)
    for n, ((out, _, g), copy) in enumerate(zip(blocks, copies)):
        copy.wait()
        for q in range(2):
            tile = jnp.dot(
                turned[...], held[n, :, q * 512 : (q + 1) * 512], preferred_element_type=F32
            ).astype(BF16)
            for u in range(4):
                out[4 * q + u, :, g * BLK : (g + 1) * BLK] = tile[:, u * BLK : (u + 1) * BLK]


def spread_kernel(t0, t1, t2, t3, out):
    rank = t0.shape[0]
    for n in range(out.shape[0]):
        for d, tile in enumerate((t0, t1, t2, t3)):
            out[n, d * rank : (d + 1) * rank] = tile[...]


def inverse_kernel(gram, out, left):
    size, wide = gram.shape[0], 16
    left[...] = gram[...]
    rows = lax.broadcasted_iota(jnp.int32, (size, size), 0)
    cols = lax.broadcasted_iota(jnp.int32, (size, size), 1)
    out[...] = (rows == cols).astype(F32)
    row = lax.broadcasted_iota(jnp.int32, (wide, BLK), 0)
    for k in range(0, size, wide):
        lo = k // BLK * BLK
        hi = lo + BLK
        over = lambda v, width: jnp.concatenate([v] * (width // BLK), 1)
        a, b = left[k : k + wide, lo:size], out[k : k + wide, :hi]
        col = [
            jnp.broadcast_to(left[k : k + wide, k + j : k + j + 1], (wide, BLK))
            for j in range(wide)
        ]
        done = []
        for i in range(wide):
            pivot = col[i][i : i + 1]
            root = lax.rsqrt(pivot)
            root = root * (1.5 - 0.5 * pivot * root * root)
            done.append(b[i : i + 1] * over(root, hi))
            inv = root * root
            factor = jnp.where(row == i, 1.0 - inv, col[i] * inv)
            for j in range(i + 1, wide):
                col[j] = col[j] - factor * col[j][i : i + 1]
            a = a - over(factor, size - lo) * a[i : i + 1]
            b = b - over(factor, hi) * b[i : i + 1]
        out[k : k + wide, :hi] = jnp.concatenate(done, 0)
        if k + wide < size:
            a_rest, b_rest = left[k + wide :, lo:size], out[k + wide :, :hi]
            for j in range(wide):
                c = left[k + wide :, k + j : k + j + 1]
                a_rest = a_rest - c * a[j : j + 1]
                b_rest = b_rest - c * b[j : j + 1]
            left[k + wide :, lo:size] = a_rest
            out[k + wide :, :hi] = b_rest


def coef_kernel(place, inverse, parts, *refs):
    outs, held = refs[:4], refs[4]
    total = parts[0].astype(F32)
    for t in range(1, 8):
        total += parts[t].astype(F32)
    coef = jnp.dot(inverse[...], total, precision=HIGH, preferred_element_type=F32)
    for b in range(2):
        held[b * BLK : (b + 1) * BLK] = recode(coef[b * BLK : (b + 1) * BLK], 0)
    for d in range(4):
        outs[d][...] = columns(held, (place[2] + d) % 4 * BLK, BLK)[...]


def basis_kernel(place, s0, s1, s2, s3, mine, theirs, left):
    for d, sketched in enumerate((s0, s1, s2, s3)):
        for n, yh in enumerate((place[3], 1 - place[3])):
            for core, inverse in ((place[0], mine), (1 - place[0], theirs)):
                basis = lax.dot_general(
                    sketched[yh],
                    inverse[d, yh],
                    (((1,), (1,)), ((), ())),
                    preferred_element_type=F32,
                )
                start = pl.multiple_of((2 * (4 * n + d) + core) * BLK, BLK)
                left[:, pl.ds(start, BLK)] = recode(basis, 1)


def partial_kernel(left, mine, out):
    depth = mine.shape[1]
    for t in range(0, 8, 2):
        right = jnp.concatenate([mine[t], mine[t + 1]], axis=1)
        out[:, t * BLK : (t + 2) * BLK] = jnp.dot(
            left[:, :depth], right, preferred_element_type=F32
        )


def update_kernel(params, momentum, part, left, theirs, new_params, new_momentum):
    right = jnp.concatenate([theirs[0], theirs[1]], axis=1)
    rest = jnp.dot(left[...], right, preferred_element_type=F32)
    average = (part[...] + rest) * (1.0 / ISLANDS)
    new = 0.9 * momentum[...] + average
    new_momentum[...] = new
    new_params[...] = params[...] - 0.7 * (average + 0.9 * new)


def update_call(params, momentum, part, left, theirs):
    rows, width = params.shape
    depth = theirs.shape[1]
    tile = pl.BlockSpec((rows, 2 * BLK), lambda g: (0, g))
    return pl.pallas_call(
        update_kernel,
        grid=(4,),
        in_specs=[
            tile,
            tile,
            tile,
            pl.BlockSpec((rows, depth), lambda g: (0, 1)),
            pl.BlockSpec((2, depth, BLK), lambda g: (g, 0, 0)),
        ],
        out_specs=[tile, tile],
        out_shape=[jax.ShapeDtypeStruct((rows, width), F32)] * 2,
        compiler_params=pltpu.CompilerParams(vmem_limit_bytes=16 * 1024 * 1024),
        cost_estimate=pl.CostEstimate(flops=1100000000, bytes_accessed=14000000, transcendentals=0),
        name="update",
    )(
        pltpu.with_memory_space_constraint(params, pltpu.HBM),
        pltpu.with_memory_space_constraint(momentum, pltpu.HBM),
        part,
        left,
        theirs,
    )


def body(delta, sketch, params, momentum):
    local = delta[0]
    rows, rank = local.shape[0], sketch.shape[1]
    depth = sketch.shape[0]
    x, yh, z, yl, core = (lax.axis_index(a) for a in AXES)
    fence = lax.optimization_barrier

    up = lambda v: move(v, lambda x, h, z, l, c: (x, h + l, z, l + 1, c))
    down = lambda v: move(v, lambda x, h, z, l, c: (x, h + l - 1, z, l - 1, c))
    swap = lambda vs: [shift(v, dc=1) for v in vs]
    near = [z, z - 1, z + 1, z - 2]
    starts = [
        (2 * (2 * (n % 4) + l) + c) * depth
        for c in (core, 1 - core)
        for n, l in ((z, yl), (z - 1, yl), (z + 1, yl), (z, 1 - yl), (z - 2, yl))
    ]
    starts += [
        (2 * (2 * (n % 4) + 1 - yl) + c) * depth
        for c in (core, 1 - core)
        for n in (z - 1, z + 1, z - 2)
    ]
    place = jnp.stack([core, 0, x, (core + yh) % 2] + starts).astype(jnp.int32)
    fetched = lambda count, width: [
        pltpu.VMEM((count, rows, width), BF16),
        pltpu.SemaphoreType.DMA((count,)),
    ]
    with jax.named_scope("gather_sketch"):
        z1, z3 = shift(sketch, dz=1), shift(sketch, dz=-1)
        pieces = [sketch, z1, z3, up(sketch), shift(sketch, dz=2)]
        y1, y3, y2 = up(z1), down(z3), down(pieces[4])
        pieces += swap(pieces)
    part = call(
        functools.partial(early_kernel, range(4, 14)),
        [((rows, rank), F32)],
        1.4e9,
        "sketched_early",
        scratch=fetched(10, depth),
        far=(1,),
    )(place, local, *pieces)[0]
    y1, y3, y2, part = fence((y1, y3, y2, part))
    with jax.named_scope("gather_sketch"):
        pieces = [y1, y3, y2]
        pieces += swap(pieces)
    gram, rounded, turned = call(
        functools.partial(late_kernel, range(14, 20)),
        [((rank, rank), F32), ((rows, rank), BF16), ((rank, rows), BF16)],
        1e9,
        "sketched_late",
        scratch=[pltpu.VMEM((rows, rank), F32)] + fetched(6, depth),
        far=(1,),
    )(place, local, *pieces, part)

    with jax.named_scope("sum_gram"):
        half = rank // 2
        mine = lax.dynamic_slice_in_dim(gram, core * half, half, 0)
        theirs = lax.dynamic_slice_in_dim(gram, (1 - core) * half, half, 0)
        mine = mine + shift(theirs, dc=1)
        mine, turned = fence((mine, turned))
        got = shift(mine, dl=1)
    shares = ((8, rank, 4 * BLK), BF16)
    sent, kept = call(
        product_kernel, [shares] * 2, 2.2e9, "product", vmem=24, scratch=fetched(8, 1024), far=(1,)
    )(place, local, turned)
    got, sent, kept = fence((got, sent, kept))
    with jax.named_scope("sum_cores"):
        kept = (kept.astype(F32) + shift(sent, dc=1).astype(F32)).astype(BF16)
    with jax.named_scope("sum_gram"):
        mine = mine + got
        mine = mine + move(mine, lambda x, h, z, l, c: (x, h, z ^ 1, l, c))
        mine, rounded = fence((mine, rounded))
        got = move(mine, lambda x, h, z, l, c: (x, h, 3 - z, l, c))
        got, kept = fence((got, kept))
        mine = mine + got
    with jax.named_scope("gather_sketched"):
        both = jnp.stack([rounded, shift(rounded, dh=1)])
    kept, mine, both = fence((kept, mine, both))
    with jax.named_scope("gather_sketched"):
        right, left = shift(both, dx=1), shift(both, dx=-1)
    with jax.named_scope("sum_fsdp"):
        parts = lax.all_to_all(kept, ("z", "yl"), 0, 0, tiled=True)

    with jax.named_scope("sum_gram"):
        theirs = shift(mine, dc=1)
        zero = core == 0
        gram = jnp.concatenate([jnp.where(zero, mine, theirs), jnp.where(zero, theirs, mine)], 0)
    inverse = call(
        inverse_kernel, [((rank, rank), F32)], 3e9, "inverse", False, [pltpu.VMEM((rank, rank), F32)]
    )(gram)[0]

    inverse, right, left = fence((inverse, right, left))
    with jax.named_scope("gather_sketched"):
        far = [shift(right[0], dx=1), shift(left[1], dx=-1)]
    with jax.named_scope("gather_inverse"):
        half_inverse = lax.dynamic_slice_in_dim(inverse, core * half, half, 0).astype(BF16)
        pair = jnp.stack([half_inverse, shift(half_inverse, dh=1)])
    parts, pair, *far = fence((parts, pair, *far))
    tiles = call(
        coef_kernel,
        [((rank, BLK), BF16)] * 4,
        4e8,
        "coef",
        scratch=[pltpu.VMEM((rank, 4 * BLK), BF16)],
    )(place, inverse, parts)
    with jax.named_scope("exchange_coef"):
        tiles = [
            move(v, lambda x, h, z, l, c, d=d: (x + d, c, z, l, h)) for d, v in enumerate(tiles)
        ]
    with jax.named_scope("gather_inverse"):
        inverses = jnp.stack([pair] + [shift(pair, dx=d) for d in range(1, 4)])
        other = shift(inverses, dc=1)
    sketches = [both, right, jnp.stack(far), left]
    operand = call(basis_kernel, [((rows, 8 * rank), BF16)], 5.4e8, "basis")(
        place, *sketches, inverses, other
    )[0]

    tiles = call(spread_kernel, [((8, 4 * rank, BLK), BF16)], 0, "spread", False)(*tiles)[0]
    with jax.named_scope("gather_coef"):
        mine, operand = fence((lax.all_to_all(tiles, ("z", "yl"), 0, 0, tiled=True), operand))
        theirs = shift(mine, dc=1)
    part = call(partial_kernel, [((rows, 8 * BLK), F32)], 1.1e9, "partial", False)(operand, mine)[0]
    return tuple(update_call(params, momentum, part, operand, theirs))


def solution(mesh):
    mesh = Mesh(mesh.devices.reshape(SIZES), AXES)
    island, fsdp = AXES[:2], AXES[2:]
    placed = (P(island, fsdp, None), P(fsdp, None), P(fsdp, island), P(fsdp, island))
    return jax.shard_map(
        body,
        mesh=mesh,
        in_specs=placed,
        out_specs=(P(fsdp, island), P(fsdp, island)),
        check_vma=False,
    )
```

time: 611 us -> 155 us (0.25); the launches traced: 601 us -> 154 us
  waiting for transfers between devices: 353 us -> 47.9 us
  blocking collectives: 72.2 us -> 0 us
  other arithmetic: 71.4 us -> 3.25 us
  starting transfers between devices: 13.1 us -> 61.1 us
  local copies, waits for them, and re-layouts: 46.5 us -> 1.83 us
  Pallas kernels: 0 us -> 39.3 us
  matrix products: 28.9 us -> 0 us
  between operations: 15.3 us -> 0.9 us
    psum x2 -> x0, waiting for transfers between devices: 309 us -> none  [the longest x1 193 us: body(): lax.psum(jnp.einsum('rc,rk->ck', block, basis_b, preferred_element_type=j...]
    all_gather x1 -> x0, blocking collectives: 72.2 us -> none  [body(): piece_scale = lax.all_gather(scale_q[None], 'island', axis=0, tiled=True)]
    ppermute x0 -> x36, starting transfers between devices: none -> 53 us  [move(): return lax.ppermute(value, AXES, pairs)]
    another operation x9 -> x4, other arithmetic: 53.7 us -> 1.13 us  [the longest x1 1 us: body(): sketches = [both, right, jnp.stack(far), left]]
    all_gather x2 -> x0, waiting for transfers between devices: 42.9 us -> none  [the longest x1 42.8 us: body(): lax.all_gather(sketch, 'fsdp', axis=0, tiled=True)]
    ppermute x0 -> x36, waiting for transfers between devices: none -> 41.1 us  [move(): return lax.ppermute(value, AXES, pairs)]
    pallas_call x0 -> x9, Pallas kernels: none -> 39.3 us  [the longest x8 33.7 us: run(): pl.pallas_call(kernel, in_specs=[SMEM if smem and n == 0 else FAR if n in...]
    div x2 -> x0, local copies, waits for them, and re-layouts: 28.2 us -> none  [compress(): code = (blocks / scale.astype(jnp.float32)[:, :, None]).astype(jnp.bfloat16)]
  transfers between devices with their start and end apart: 6 -> 38, of which waited for: 3 -> 22; matrix products, arithmetic and copies ran while one was open for 9% -> 2% of each run, Pallas kernels for 0% -> 17%
where the time goes in v1:
time: 155 us; the launch traced here: 154 us
  starting transfers between devices  61.1 us (39%)
  waiting for transfers between devices  47.9 us (31%)
  Pallas kernels  39.3 us (25%)
  other arithmetic  3.25 us (2%)
  local copies, waits for them, and re-layouts  1.83 us (1%)
    ppermute x36, starting transfers between devices, move(): return lax.ppermute(value, AXES, pairs)  53 us
    ppermute x36, waiting for transfers between devices, move(): return lax.ppermute(value, AXES, pairs)  41.1 us
    pallas_call x8, Pallas kernels, run(): pl.pallas_call(kernel, in_specs=[SMEM if smem and n == 0 else FAR if n in...  33.7 us
    all_to_all x1, waiting for transfers between devices, body(): lax.all_to_all(tiles, ('z', 'yl'), 0, 0, tiled=True)  6.84 us
    pallas_call x1, Pallas kernels, update_call(): pl.pallas_call(update_kernel, grid=(4,), in_specs=[tile, tile, tile, pl.B...  5.58 us
    all_to_all x1, starting transfers between devices, body(): lax.all_to_all(tiles, ('z', 'yl'), 0, 0, tiled=True)  4.49 us
    all_to_all x1, starting transfers between devices, body(): parts = lax.all_to_all(kept, ('z', 'yl'), 0, 0, tiled=True)  3.62 us
  transfers between devices with their start and end apart: 38, of which 22 were waited for; matrix products, arithmetic and copies ran while one was open for 2% of the time, Pallas kernels for 17%

profile of v1, /device:TPU:1, one launch (start us, length us, event | category | flops | bytes accessed | tf_op | source)
XLA Modules:
  0.0 154.3 jit_solution(4302322141084711458)
XLA Ops:
  0.6 2.2 %collective-permute-start.6 = (bf16[512,256]{1,0:T(8,128)(2,1)}, bf16[512,256]{1,0:T(8,128)(2,1)S(1)}, u32[]{:S(2)}, u32[]{:S(2)}) collective-permute-start(bf16[512,256]{1,0:T(8,128)(2,1)} %refs_0_.1), channel_id=1, source_target_pairs={{0,2},{1,3},{2,16},{3,17},{4,6},{5,7},{6,20},{7,21},{8,10},{9,11},... | collective-permute-start | bytes 786440 | tf_op jit(solution)/shard_map/gather_sketch/ppermute | solution.py:25
  2.8 3.6 %collective-permute-start.4 = (bf16[512,256]{1,0:T(8,128)(2,1)}, bf16[512,256]{1,0:T(8,128)(2,1)S(1)}, u32[]{:S(2)}, u32[]{:S(2)}) collective-permute-start(bf16[512,256]{1,0:T(8,128)(2,1)} %refs_0_.1), channel_id=1, source_target_pairs={{0,8},{1,9},{2,10},{3,11},{4,12},{5,13},{6,14},{7,15},{8,0},{9,1},... | collective-permute-start | bytes 786440 | tf_op jit(solution)/shard_map/gather_sketch/ppermute | solution.py:25
  6.9 1.0 collective-permute-start
  7.9 1.8 %collective-permute-start.7 = (bf16[512,256]{1,0:T(8,128)(2,1)}, bf16[512,256]{1,0:T(8,128)(2,1)S(1)}, u32[]{:S(2)}, u32[]{:S(2)}) collective-permute-start(bf16[512,256]{1,0:T(8,128)(2,1)} %refs_0_.1), channel_id=1, source_target_pairs={{0,1},{1,0},{2,3},{3,2},{4,5},{5,4},{6,7},{7,6},{8,9},{9,8},{10,11... | collective-permute-start | bytes 786440 | tf_op jit(solution)/shard_map/gather_sketch/ppermute | solution.py:25
  10.4 1.4 collective-permute-start.10
  12.4 2.7 %collective-permute-start.11 = (bf16[512,256]{1,0:T(8,128)(2,1)S(1)}, bf16[512,256]{1,0:T(8,128)(2,1)S(1)}, u32[]{:S(2)}, u32[]{:S(2)}) collective-permute-start(bf16[512,256]{1,0:T(8,128)(2,1)S(1)} %collective-permute-done.4.refs_4_), channel_id=1, source_target_pairs={{0,1},{1,0},{2,3},{3,2},{4,5},{5,4},{6,7},{7,6},{8,9},{9,8},{10,11... | collective-permute-start | bytes 786440 | tf_op jit(solution)/shard_map/gather_sketch/ppermute | solution.py:25
  15.1 3.7 %collective-permute-done.2.refs_2_ = bf16[512,256]{1,0:T(8,128)(2,1)S(1)} collective-permute-done((bf16[512,256]{1,0:T(8,128)(2,1)}, bf16[512,256]{1,0:T(8,128)(2,1)S(1)}, u32[]{:S(2)}, u32[]{:S(2)}) %collective-permute-start.2) | collective-permute-done | bytes 262176 | tf_op jit(solution)/shard_map/gather_sketch/ppermute | solution.py:25
  18.8 1.5 collective-permute-start.9
  20.3 1.6 %collective-permute-start.5 = (bf16[512,256]{1,0:T(8,128)(2,1)S(1)}, bf16[512,256]{1,0:T(8,128)(2,1)S(1)}, u32[]{:S(2)}, u32[]{:S(2)}) collective-permute-start(bf16[512,256]{1,0:T(8,128)(2,1)S(1)} %collective-permute-done.4.refs_4_), channel_id=1, source_target_pairs={{0,18},{1,19},{2,0},{3,1},{4,22},{5,23},{6,4},{7,5},{8,26},{9,27},... | collective-permute-start | bytes 786440 | tf_op jit(solution)/shard_map/gather_sketch/ppermute | solution.py:25
  21.9 1.4 collective-permute-start.3
  24.4 5.0 %sketched_early.1.refs_6_ = f32[512,256]{1,0:T(8,128)S(1)} custom-call(s32[20]{0:T(128)S(1)} %stack.121.place, bf16[512,8192]{1,0:T(8,128)(2,1)} %bitcast.36, bf16[512,256]{1,0:T(8,128)(2,1)S(1)} %copy-done.2, bf16[512,256]{1,0:T(8,128)(2,1)S(1)} %collective-permute-done.refs_1_, bf16[512,256]{1,0:T(8,128)(2,1)S(1)} %collective-permute-done.2.refs_2_, ...), custom_call_target="tpu_custom_call" | custom-call | flops 1400000000 | bytes 4194304 | tf_op jit(solution)/shard_map/sketched_early/pallas_call | solution.py:49
  29.4 4.0 %collective-permute-done.3.refs_1_ = bf16[512,256]{1,0:T(8,128)(2,1)S(1)} collective-permute-done((bf16[512,256]{1,0:T(8,128)(2,1)S(1)}, bf16[512,256]{1,0:T(8,128)(2,1)S(1)}, u32[]{:S(2)}, u32[]{:S(2)}) %collective-permute-start.3) | collective-permute-done | bytes 262176 | tf_op jit(solution)/shard_map/gather_sketch/ppermute | solution.py:25
  33.4 1.3 collective-permute-start.12
  35.2 1.2 collective-permute-done.12.refs_3_
  36.6 4.9 %sketched_late.1 = (f32[256,256]{1,0:T(8,128)S(1)}, bf16[512,256]{1,0:T(8,128)(2,1)S(1)}, bf16[256,512]{1,0:T(8,128)(2,1)S(1)}) custom-call(s32[20]{0:T(128)S(1)} %stack.121.place, bf16[512,8192]{1,0:T(8,128)(2,1)} %bitcast.37, bf16[512,256]{1,0:T(8,128)(2,1)} %collective-permute-done.1.refs_0_, bf16[512,256]{1,0:T(8,128)(2,1)S(1)} %collective-permute-done.3.refs_1_, ...), custom_call_target="tpu_custom_call" | custom-call | flops 1000000000 | bytes 4194304 | tf_op jit(solution)/shard_map/sketched_late/pallas_call | solution.py:49
  42.0 1.0 collective-permute-done.15
  43.0 1.4 collective-permute-start.16
  44.4 5.4 %product.1 = (bf16[8,256,512]{2,1,0:T(8,128)(2,1)S(1)}, bf16[8,256,512]{2,1,0:T(8,128)(2,1)S(1)}) custom-call(s32[20]{0:T(128)S(1)} %stack.121.place, bf16[512,8192]{1,0:T(8,128)(2,1)} %bitcast.38, bf16[256,512]{1,0:T(8,128)(2,1)S(1)} %get-tuple-element.43.turned), custom_call_target="tpu_custom_call" | custom-call | flops 2200000000 | bytes 4194304 | tf_op jit(solution)/shard_map/product/pallas_call | solution.py:49
  51.3 4.5 %collective-permute-done.17 = f32[128,256]{1,0:T(8,128)S(1)} collective-permute-done((f32[128,256]{1,0:T(8,128)S(1)}, f32[128,256]{1,0:T(8,128)S(1)}, u32[]{:S(2)}, u32[]{:S(2)}) %collective-permute-start.17) | collective-permute-done | bytes 131104 | tf_op jit(solution)/shard_map/sum_gram/ppermute | solution.py:25
  55.8 2.7 %collective-permute-start.20 = (bf16[512,256]{1,0:T(8,128)(2,1)S(1)}, bf16[512,256]{1,0:T(8,128)(2,1)S(1)}, u32[]{:S(2)}, u32[]{:S(2)}) collective-permute-start(bf16[512,256]{1,0:T(8,128)(2,1)S(1)} %get-tuple-element.53), channel_id=1, source_target_pairs={{0,16},{1,17},{2,18},{3,19},{4,20},{5,21},{6,22},{7,23},{8,24},{9,... | collective-permute-start | bytes 786440 | tf_op jit(solution)/shard_map/gather_sketched/ppermute | solution.py:25
  58.5 2.3 %collective-permute-start.18 = (f32[128,256]{1,0:T(8,128)S(1)}, f32[128,256]{1,0:T(8,128)S(1)}, u32[]{:S(2)}, u32[]{:S(2)}) collective-permute-start(f32[128,256]{1,0:T(8,128)S(1)} %add.176), channel_id=1, source_target_pairs={{0,12},{1,13},{2,14},{3,15},{4,8},{5,9},{6,10},{7,11},{8,4},{9,5},... | collective-permute-start | bytes 393224 | tf_op jit(solution)/shard_map/sum_gram/ppermute | solution.py:25
  60.8 3.6 %collective-permute-done.20 = bf16[512,256]{1,0:T(8,128)(2,1)S(1)} collective-permute-done((bf16[512,256]{1,0:T(8,128)(2,1)S(1)}, bf16[512,256]{1,0:T(8,128)(2,1)S(1)}, u32[]{:S(2)}, u32[]{:S(2)}) %collective-permute-start.20) | collective-permute-done | bytes 262176 | tf_op jit(solution)/shard_map/gather_sketched/ppermute | solution.py:25
  64.4 2.0 %add_convert_fusion = bf16[8,256,512]{2,1,0:T(8,128)(2,1)} fusion(bf16[8,256,512]{2,1,0:T(8,128)(2,1)S(1)} %collective-permute-done.19, bf16[8,256,512]{2,1,0:T(8,128)(2,1)S(1)} %get-tuple-element.49), kind=kLoop, calls=%fused_computation | loop fusion | flops 4194304 | bytes 6291456 | tf_op jit(solution)/shard_map/sum_cores/convert_element_type | solution.py:310
  66.5 3.6 %all-to-all-start = ((bf16[8,256,512]{2,1,0:T(8,128)(2,1)}), bf16[8,256,512]{2,1,0:T(8,128)(2,1)S(1)}, u32[]{:S(2)}, u32[]{:S(2)}) async-start(bf16[8,256,512]{2,1,0:T(8,128)(2,1)} %add_convert_fusion), calls=%async_computation | async-start | bytes 4194304 | tf_op jit(solution)/shard_map/sum_fsdp/all_to_all | solution.py:324
  70.1 2.0 %collective-permute-start.21 = (f32[128,256]{1,0:T(8,128)S(1)}, f32[128,256]{1,0:T(8,128)S(1)}, u32[]{:S(2)}, u32[]{:S(2)}) collective-permute-start(f32[128,256]{1,0:T(8,128)S(1)} %add.178), channel_id=1, source_target_pairs={{0,1},{1,0},{2,3},{3,2},{4,5},{5,4},{6,7},{7,6},{8,9},{9,8},{10,11... | collective-permute-start | bytes 393224 | tf_op jit(solution)/shard_map/sum_gram/ppermute | solution.py:25
  72.1 2.5 %collective-permute-start.23 = (bf16[2,512,256]{2,1,0:T(8,128)(2,1)S(1)}, bf16[2,512,256]{2,1,0:T(8,128)(2,1)S(1)}, u32[]{:S(2)}, u32[]{:S(2)}) collective-permute-start(bf16[2,512,256]{2,1,0:T(8,128)(2,1)S(1)} %pad_maximum_fusion.s0), channel_id=1, source_target_pairs={{0,96},{1,97},{2,98},{3,99},{4,100},{5,101},{6,102},{7,103},{8,104... | collective-permute-start | bytes 1572872 | tf_op jit(solution)/shard_map/gather_sketched/ppermute | solution.py:25
  74.6 10.0 %inverse.1 = f32[256,256]{1,0:T(8,128)S(1)} custom-call(f32[256,256]{1,0:T(8,128)S(1)} %pad_maximum_fusion.3.gram), custom_call_target="tpu_custom_call" | custom-call | flops 3000000000 | bytes 4194304 | tf_op jit(solution)/shard_map/inverse/pallas_call | solution.py:49
  84.7 1.2 collective-permute-done.23.s3
  85.8 3.1 %collective-permute-done.22.s1 = bf16[2,512,256]{2,1,0:T(8,128)(2,1)S(1)} collective-permute-done((bf16[2,512,256]{2,1,0:T(8,128)(2,1)S(1)}, bf16[2,512,256]{2,1,0:T(8,128)(2,1)S(1)}, u32[]{:S(2)}, u32[]{:S(2)}) %collective-permute-start.22) | collective-permute-done | bytes 524320 | tf_op jit(solution)/shard_map/gather_sketched/ppermute | solution.py:25
  89.4 1.2 collective-permute-start.25
  90.6 2.9 %collective-permute-start.24 = (bf16[128,256]{1,0:T(8,128)(2,1)S(1)}, bf16[128,256]{1,0:T(8,128)(2,1)S(1)}, u32[]{:S(2)}, u32[]{:S(2)}) collective-permute-start(bf16[128,256]{1,0:T(8,128)(2,1)S(1)} %dynamic-slice_convert_fusion), channel_id=1, source_target_pairs={{0,16},{1,17},{2,18},{3,19},{4,20},{5,21},{6,22},{7,23},{8,24},{9,... | collective-permute-start | bytes 196616 | tf_op jit(solution)/shard_map/gather_inverse/ppermute | solution.py:25
  93.5 3.0 %collective-permute-done.24 = bf16[128,256]{1,0:T(8,128)(2,1)S(1)} collective-permute-done((bf16[128,256]{1,0:T(8,128)(2,1)S(1)}, bf16[128,256]{1,0:T(8,128)(2,1)S(1)}, u32[]{:S(2)}, u32[]{:S(2)}) %collective-permute-start.24) | collective-permute-done | bytes 65568 | tf_op jit(solution)/shard_map/gather_inverse/ppermute | solution.py:25
  97.4 1.5 coef.1
  98.9 6.5 %collective-permute-start.27 = (bf16[256,128]{1,0:T(8,128)(2,1)S(1)}, bf16[256,128]{1,0:T(8,128)(2,1)S(1)}, u32[]{:S(2)}, u32[]{:S(2)}) collective-permute-start(bf16[256,128]{1,0:T(8,128)(2,1)S(1)} %get-tuple-element.61), channel_id=1, source_target_pairs={{0,0},{1,16},{2,2},{3,18},{4,4},{5,20},{6,6},{7,22},{8,8},{9,24},{... | collective-permute-start | bytes 196616 | tf_op jit(solution)/shard_map/exchange_coef/ppermute | solution.py:25
  105.7 5.4 %collective-permute-start.29 = (bf16[256,128]{1,0:T(8,128)(2,1)S(1)}, bf16[256,128]{1,0:T(8,128)(2,1)S(1)}, u32[]{:S(2)}, u32[]{:S(2)}) collective-permute-start(bf16[256,128]{1,0:T(8,128)(2,1)S(1)} %get-tuple-element.63), channel_id=1, source_target_pairs={{0,64},{1,80},{2,66},{3,82},{4,68},{5,84},{6,70},{7,86},{8,72},{9,... | collective-permute-start | bytes 196616 | tf_op jit(solution)/shard_map/exchange_coef/ppermute | solution.py:25
  113.8 3.5 %collective-permute-done.30.t3 = bf16[256,128]{1,0:T(8,128)(2,1)S(1)} collective-permute-done((bf16[256,128]{1,0:T(8,128)(2,1)S(1)}, bf16[256,128]{1,0:T(8,128)(2,1)S(1)}, u32[]{:S(2)}, u32[]{:S(2)}) %collective-permute-start.30) | collective-permute-done | bytes 65568 | tf_op jit(solution)/shard_map/exchange_coef/ppermute | solution.py:25
  117.3 1.6 %spread.1 = bf16[8,1024,128]{2,1,0:T(8,128)(2,1)} custom-call(bf16[256,128]{1,0:T(8,128)(2,1)S(1)} %collective-permute-done.27.t0, bf16[256,128]{1,0:T(8,128)(2,1)S(1)} %collective-permute-done.28.t1, bf16[256,128]{1,0:T(8,128)(2,1)S(1)} %collective-permute-done.29.t2, bf16[256,128]{1,0:T(8,128)(2,1)S(1)} %collective-permute-done.30.t3), custom_call_target="tpu_custom_call" | custom-call | bytes 4194304 | tf_op jit(solution)/shard_map/spread/pallas_call | solution.py:49
  118.9 4.5 %all-to-all-start.1 = ((bf16[8,1024,128]{2,1,0:T(8,128)(2,1)}), bf16[8,1024,128]{2,1,0:T(8,128)(2,1)}, u32[]{:S(2)}, u32[]{:S(2)}) async-start(bf16[8,1024,128]{2,1,0:T(8,128)(2,1)} %spread.1), calls=%async_computation.1 | async-start | bytes 4194304 | tf_op jit(solution)/shard_map/gather_coef/all_to_all | solution.py:362
  123.4 2.4 %collective-permute-start.33 = (bf16[2,128,256]{2,1,0:T(8,128)(2,1)S(1)}, bf16[2,128,256]{2,1,0:T(8,128)(2,1)S(1)}, u32[]{:S(2)}, u32[]{:S(2)}) collective-permute-start(bf16[2,128,256]{2,1,0:T(8,128)(2,1)S(1)} %pad_maximum_fusion.4), channel_id=1, source_target_pairs={{0,96},{1,97},{2,98},{3,99},{4,100},{5,101},{6,102},{7,103},{8,104... | collective-permute-start | bytes 393224 | tf_op jit(solution)/shard_map/gather_inverse/ppermute | solution.py:25
  126.5 2.6 %collective-permute-done.33 = bf16[2,128,256]{2,1,0:T(8,128)(2,1)S(1)} collective-permute-done((bf16[2,128,256]{2,1,0:T(8,128)(2,1)S(1)}, bf16[2,128,256]{2,1,0:T(8,128)(2,1)S(1)}, u32[]{:S(2)}, u32[]{:S(2)}) %collective-permute-start.33) | collective-permute-done | bytes 131104 | tf_op jit(solution)/shard_map/gather_inverse/ppermute | solution.py:25
  129.2 2.4 %collective-permute-done.32 = bf16[2,128,256]{2,1,0:T(8,128)(2,1)S(1)} collective-permute-done((bf16[2,128,256]{2,1,0:T(8,128)(2,1)S(1)}, bf16[2,128,256]{2,1,0:T(8,128)(2,1)S(1)}, u32[]{:S(2)}, u32[]{:S(2)}) %collective-permute-start.32) | collective-permute-done | bytes 131104 | tf_op jit(solution)/shard_map/gather_inverse/ppermute | solution.py:25
  131.6 1.3 collective-permute-done.31
  133.1 1.0 pad_maximum_fusion.1.s2
  135.0 2.5 %basis.1.left = bf16[512,2048]{1,0:T(8,128)(2,1)S(1)} custom-call(s32[20]{0:T(128)S(1)} %stack.121.place, bf16[2,512,256]{2,1,0:T(8,128)(2,1)S(1)} %pad_maximum_fusion.s0, bf16[2,512,256]{2,1,0:T(8,128)(2,1)S(1)} %copy-done.1, bf16[2,512,256]{2,1,0:T(8,128)(2,1)S(1)} %pad_maximum_fusion.1.s2, bf16[2,512,256]{2,1,0:T(8,128)(2,1)S(1)} %collective-permute-done.23.s3, ...), custom_call_target="tpu_custom_call" | custom-call | flops 540000000 | bytes 4194304 | tf_op jit(solution)/shard_map/basis/pallas_call | solution.py:49
  137.5 6.8 %all-to-all-done.1.mine = bf16[8,1024,128]{2,1,0:T(8,128)(2,1)} async-done(((bf16[8,1024,128]{2,1,0:T(8,128)(2,1)}), bf16[8,1024,128]{2,1,0:T(8,128)(2,1)}, u32[]{:S(2)}, u32[]{:S(2)}) %all-to-all-start.1) | async-done | bytes 2097184 | tf_op jit(solution)/shard_map/gather_coef/all_to_all | solution.py:362
  144.4 2.8 %partial.1.part = f32[512,1024]{1,0:T(8,128)S(1)} custom-call(bf16[512,2048]{1,0:T(8,128)(2,1)S(1)} %basis.1.left, bf16[8,1024,128]{2,1,0:T(8,128)(2,1)} %all-to-all-done.1.mine), custom_call_target="tpu_custom_call" | custom-call | flops 1100000000 | bytes 4194304 | tf_op jit(solution)/shard_map/partial/pallas_call | solution.py:49
  147.2 1.5 collective-permute-done.35.theirs
  148.7 5.6 %update.1 = (f32[512,1024]{1,0:T(8,128)}, f32[512,1024]{1,0:T(8,128)}) custom-call(f32[512,1024]{1,0:T(8,128)} %params.1, f32[512,1024]{1,0:T(8,128)} %momentum.1, f32[512,1024]{1,0:T(8,128)S(1)} %partial.1.part, bf16[512,2048]{1,0:T(8,128)(2,1)S(1)} %basis.1.left, bf16[8,1024,128]{2,1,0:T(8,128)(2,1)S(1)} %collective-permute-done.35.theirs), custom_call_target="tpu_custom_call" | custom-call | flops 1100000000 | bytes 14000000 | tf_op jit(solution)/shard_map/update/pallas_call | solution.py:221
  (64 shorter events, 11.6 us)
Async XLA Ops:
  0.6 9.7 %collective-permute-start.6 = (bf16[512,256]{1,0:T(8,128)(2,1)}, bf16[512,256]{1,0:T(8,128)(2,1)S(1)}, u32[]{:S(2)}, u32[]{:S(2)}) collective-permute-start(bf16[512,256]{1,0:T(8,128)(2,1)} %refs_0_.1), channel_id=1, source_target_pairs={{0,2},{1,3},{2,16},{3,17},{4,6},{5,7},{6,20},{7,21},{8,10},{9,11},... | collective-permute-start | bytes 786440 | tf_op jit(solution)/shard_map/gather_sketch/ppermute | solution.py:25
  2.8 9.6 %collective-permute-start.4 = (bf16[512,256]{1,0:T(8,128)(2,1)}, bf16[512,256]{1,0:T(8,128)(2,1)S(1)}, u32[]{:S(2)}, u32[]{:S(2)}) collective-permute-start(bf16[512,256]{1,0:T(8,128)(2,1)} %refs_0_.1), channel_id=1, source_target_pairs={{0,8},{1,9},{2,10},{3,11},{4,12},{5,13},{6,14},{7,15},{8,0},{9,1},... | collective-permute-start | bytes 786440 | tf_op jit(solution)/shard_map/gather_sketch/ppermute | solution.py:25
  6.4 12.4 %collective-permute-start.2 = (bf16[512,256]{1,0:T(8,128)(2,1)}, bf16[512,256]{1,0:T(8,128)(2,1)S(1)}, u32[]{:S(2)}, u32[]{:S(2)}) collective-permute-start(bf16[512,256]{1,0:T(8,128)(2,1)} %refs_0_.1), channel_id=1, source_target_pairs={{0,12},{1,13},{2,14},{3,15},{4,0},{5,1},{6,2},{7,3},{8,4},{9,5},{1... | collective-permute-start | bytes 786440 | tf_op jit(solution)/shard_map/gather_sketch/ppermute | solution.py:25
  6.9 13.4 %collective-permute-start = (bf16[512,256]{1,0:T(8,128)(2,1)}, bf16[512,256]{1,0:T(8,128)(2,1)S(1)}, u32[]{:S(2)}, u32[]{:S(2)}) collective-permute-start(bf16[512,256]{1,0:T(8,128)(2,1)} %refs_0_.1), channel_id=1, source_target_pairs={{0,4},{1,5},{2,6},{3,7},{4,8},{5,9},{6,10},{7,11},{8,12},{9,13},{1... | collective-permute-start | bytes 786440 | tf_op jit(solution)/shard_map/gather_sketch/ppermute | solution.py:25
  7.9 12.4 %collective-permute-start.7 = (bf16[512,256]{1,0:T(8,128)(2,1)}, bf16[512,256]{1,0:T(8,128)(2,1)S(1)}, u32[]{:S(2)}, u32[]{:S(2)}) collective-permute-start(bf16[512,256]{1,0:T(8,128)(2,1)} %refs_0_.1), channel_id=1, source_target_pairs={{0,1},{1,0},{2,3},{3,2},{4,5},{5,4},{6,7},{7,6},{8,9},{9,8},{10,11... | collective-permute-start | bytes 786440 | tf_op jit(solution)/shard_map/gather_sketch/ppermute | solution.py:25
  10.4 11.5 %collective-permute-start.10 = (bf16[512,256]{1,0:T(8,128)(2,1)S(1)}, bf16[512,256]{1,0:T(8,128)(2,1)S(1)}, u32[]{:S(2)}, u32[]{:S(2)}) collective-permute-start(bf16[512,256]{1,0:T(8,128)(2,1)S(1)} %collective-permute-done.6.refs_3_), channel_id=1, source_target_pairs={{0,1},{1,0},{2,3},{3,2},{4,5},{5,4},{6,7},{7,6},{8,9},{9,8},{10,11... | collective-permute-start | bytes 786440 | tf_op jit(solution)/shard_map/gather_sketch/ppermute | solution.py:25
  12.4 10.9 %collective-permute-start.11 = (bf16[512,256]{1,0:T(8,128)(2,1)S(1)}, bf16[512,256]{1,0:T(8,128)(2,1)S(1)}, u32[]{:S(2)}, u32[]{:S(2)}) collective-permute-start(bf16[512,256]{1,0:T(8,128)(2,1)S(1)} %collective-permute-done.4.refs_4_), channel_id=1, source_target_pairs={{0,1},{1,0},{2,3},{3,2},{4,5},{5,4},{6,7},{7,6},{8,9},{9,8},{10,11... | collective-permute-start | bytes 786440 | tf_op jit(solution)/shard_map/gather_sketch/ppermute | solution.py:25
  18.8 4.7 %collective-permute-start.9 = (bf16[512,256]{1,0:T(8,128)(2,1)S(1)}, bf16[512,256]{1,0:T(8,128)(2,1)S(1)}, u32[]{:S(2)}, u32[]{:S(2)}) collective-permute-start(bf16[512,256]{1,0:T(8,128)(2,1)S(1)} %collective-permute-done.2.refs_2_), channel_id=1, source_target_pairs={{0,1},{1,0},{2,3},{3,2},{4,5},{5,4},{6,7},{7,6},{8,9},{9,8},{10,11... | collective-permute-start | bytes 786440 | tf_op jit(solution)/shard_map/gather_sketch/ppermute | solution.py:25
  20.3 3.2 %collective-permute-start.8 = (bf16[512,256]{1,0:T(8,128)(2,1)S(1)}, bf16[512,256]{1,0:T(8,128)(2,1)S(1)}, u32[]{:S(2)}, u32[]{:S(2)}) collective-permute-start(bf16[512,256]{1,0:T(8,128)(2,1)S(1)} %collective-permute-done.refs_1_), channel_id=1, source_target_pairs={{0,1},{1,0},{2,3},{3,2},{4,5},{5,4},{6,7},{7,6},{8,9},{9,8},{10,11... | collective-permute-start | bytes 786440 | tf_op jit(solution)/shard_map/gather_sketch/ppermute | solution.py:25
  20.3 9.1 %collective-permute-start.5 = (bf16[512,256]{1,0:T(8,128)(2,1)S(1)}, bf16[512,256]{1,0:T(8,128)(2,1)S(1)}, u32[]{:S(2)}, u32[]{:S(2)}) collective-permute-start(bf16[512,256]{1,0:T(8,128)(2,1)S(1)} %collective-permute-done.4.refs_4_), channel_id=1, source_target_pairs={{0,18},{1,19},{2,0},{3,1},{4,22},{5,23},{6,4},{7,5},{8,26},{9,27},... | collective-permute-start | bytes 786440 | tf_op jit(solution)/shard_map/gather_sketch/ppermute | solution.py:25
  21.9 11.5 %collective-permute-start.3 = (bf16[512,256]{1,0:T(8,128)(2,1)S(1)}, bf16[512,256]{1,0:T(8,128)(2,1)S(1)}, u32[]{:S(2)}, u32[]{:S(2)}) collective-permute-start(bf16[512,256]{1,0:T(8,128)(2,1)S(1)} %collective-permute-done.2.refs_2_), channel_id=1, source_target_pairs={{0,18},{1,19},{2,0},{3,1},{4,22},{5,23},{6,4},{7,5},{8,26},{9,27},... | collective-permute-start | bytes 786440 | tf_op jit(solution)/shard_map/gather_sketch/ppermute | solution.py:25
  23.3 10.2 %collective-permute-start.1 = (bf16[512,256]{1,0:T(8,128)(2,1)S(1)}, bf16[512,256]{1,0:T(8,128)(2,1)}, u32[]{:S(2)}, u32[]{:S(2)}) collective-permute-start(bf16[512,256]{1,0:T(8,128)(2,1)S(1)} %collective-permute-done.refs_1_), channel_id=1, source_target_pairs={{0,2},{1,3},{2,16},{3,17},{4,6},{5,7},{6,20},{7,21},{8,10},{9,11},... | collective-permute-start | bytes 786440 | tf_op jit(solution)/shard_map/gather_sketch/ppermute | solution.py:25
  23.5 1.0 copy-start.2
  33.4 3.0 %collective-permute-start.12 = (bf16[512,256]{1,0:T(8,128)(2,1)}, bf16[512,256]{1,0:T(8,128)(2,1)S(1)}, u32[]{:S(2)}, u32[]{:S(2)}) collective-permute-start(bf16[512,256]{1,0:T(8,128)(2,1)} %collective-permute-done.1.refs_0_), channel_id=1, source_target_pairs={{0,1},{1,0},{2,3},{3,2},{4,5},{5,4},{6,7},{7,6},{8,9},{9,8},{10,11... | collective-permute-start | bytes 786440 | tf_op jit(solution)/shard_map/gather_sketch/ppermute | solution.py:25
  34.7 1.7 %collective-permute-start.13 = (bf16[512,256]{1,0:T(8,128)(2,1)S(1)}, bf16[512,256]{1,0:T(8,128)(2,1)S(1)}, u32[]{:S(2)}, u32[]{:S(2)}) collective-permute-start(bf16[512,256]{1,0:T(8,128)(2,1)S(1)} %collective-permute-done.3.refs_1_), channel_id=1, source_target_pairs={{0,1},{1,0},{2,3},{3,2},{4,5},{5,4},{6,7},{7,6},{8,9},{9,8},{10,11... | collective-permute-start | bytes 786440 | tf_op jit(solution)/shard_map/gather_sketch/ppermute | solution.py:25
  34.7 1.9 %collective-permute-start.14 = (bf16[512,256]{1,0:T(8,128)(2,1)S(1)}, bf16[512,256]{1,0:T(8,128)(2,1)S(1)}, u32[]{:S(2)}, u32[]{:S(2)}) collective-permute-start(bf16[512,256]{1,0:T(8,128)(2,1)S(1)} %collective-permute-done.5.refs_2_), channel_id=1, source_target_pairs={{0,1},{1,0},{2,3},{3,2},{4,5},{5,4},{6,7},{7,6},{8,9},{9,8},{10,11... | collective-permute-start | bytes 786440 | tf_op jit(solution)/shard_map/gather_sketch/ppermute | solution.py:25
  41.6 1.4 collective-permute-start.15
  43.0 6.8 %collective-permute-start.16 = (f32[128,256]{1,0:T(8,128)S(1)}, f32[128,256]{1,0:T(8,128)S(1)}, u32[]{:S(2)}, u32[]{:S(2)}) collective-permute-start(f32[128,256]{1,0:T(8,128)S(1)} %dynamic-slice_add_fusion), channel_id=1, source_target_pairs={{0,2},{1,3},{2,0},{3,1},{4,6},{5,7},{6,4},{7,5},{8,10},{9,11},{10,... | collective-permute-start | bytes 393224 | tf_op jit(solution)/shard_map/sum_gram/ppermute | solution.py:25
  49.8 14.6 %collective-permute-start.19 = (bf16[8,256,512]{2,1,0:T(8,128)(2,1)S(1)}, bf16[8,256,512]{2,1,0:T(8,128)(2,1)S(1)}, u32[]{:S(2)}, u32[]{:S(2)}) collective-permute-start(bf16[8,256,512]{2,1,0:T(8,128)(2,1)S(1)} %get-tuple-element.50), channel_id=1, source_target_pairs={{0,1},{1,0},{2,3},{3,2},{4,5},{5,4},{6,7},{7,6},{8,9},{9,8},{10,11... | collective-permute-start | bytes 6291464 | tf_op jit(solution)/shard_map/sum_cores/ppermute | solution.py:25
  50.5 5.2 %collective-permute-start.17 = (f32[128,256]{1,0:T(8,128)S(1)}, f32[128,256]{1,0:T(8,128)S(1)}, u32[]{:S(2)}, u32[]{:S(2)}) collective-permute-start(f32[128,256]{1,0:T(8,128)S(1)} %add.175), channel_id=1, source_target_pairs={{0,4},{1,5},{2,6},{3,7},{4,0},{5,1},{6,2},{7,3},{8,12},{9,13},{10,... | collective-permute-start | bytes 393224 | tf_op jit(solution)/shard_map/sum_gram/ppermute | solution.py:25
  55.8 8.6 %collective-permute-start.20 = (bf16[512,256]{1,0:T(8,128)(2,1)S(1)}, bf16[512,256]{1,0:T(8,128)(2,1)S(1)}, u32[]{:S(2)}, u32[]{:S(2)}) collective-permute-start(bf16[512,256]{1,0:T(8,128)(2,1)S(1)} %get-tuple-element.53), channel_id=1, source_target_pairs={{0,16},{1,17},{2,18},{3,19},{4,20},{5,21},{6,22},{7,23},{8,24},{9,... | collective-permute-start | bytes 786440 | tf_op jit(solution)/shard_map/gather_sketched/ppermute | solution.py:25
  58.5 8.0 %collective-permute-start.18 = (f32[128,256]{1,0:T(8,128)S(1)}, f32[128,256]{1,0:T(8,128)S(1)}, u32[]{:S(2)}, u32[]{:S(2)}) collective-permute-start(f32[128,256]{1,0:T(8,128)S(1)} %add.176), channel_id=1, source_target_pairs={{0,12},{1,13},{2,14},{3,15},{4,8},{5,9},{6,10},{7,11},{8,4},{9,5},... | collective-permute-start | bytes 393224 | tf_op jit(solution)/shard_map/sum_gram/ppermute | solution.py:25
  66.5 30.9 %all-to-all-start = ((bf16[8,256,512]{2,1,0:T(8,128)(2,1)}), bf16[8,256,512]{2,1,0:T(8,128)(2,1)S(1)}, u32[]{:S(2)}, u32[]{:S(2)}) async-start(bf16[8,256,512]{2,1,0:T(8,128)(2,1)} %add_convert_fusion), calls=%async_computation | async-start | bytes 4194304 | tf_op jit(solution)/shard_map/sum_fsdp/all_to_all | solution.py:324
  70.1 4.5 %collective-permute-start.21 = (f32[128,256]{1,0:T(8,128)S(1)}, f32[128,256]{1,0:T(8,128)S(1)}, u32[]{:S(2)}, u32[]{:S(2)}) collective-permute-start(f32[128,256]{1,0:T(8,128)S(1)} %add.178), channel_id=1, source_target_pairs={{0,1},{1,0},{2,3},{3,2},{4,5},{5,4},{6,7},{7,6},{8,9},{9,8},{10,11... | collective-permute-start | bytes 393224 | tf_op jit(solution)/shard_map/sum_gram/ppermute | solution.py:25
  72.1 13.8 %collective-permute-start.23 = (bf16[2,512,256]{2,1,0:T(8,128)(2,1)S(1)}, bf16[2,512,256]{2,1,0:T(8,128)(2,1)S(1)}, u32[]{:S(2)}, u32[]{:S(2)}) collective-permute-start(bf16[2,512,256]{2,1,0:T(8,128)(2,1)S(1)} %pad_maximum_fusion.s0), channel_id=1, source_target_pairs={{0,96},{1,97},{2,98},{3,99},{4,100},{5,101},{6,102},{7,103},{8,104... | collective-permute-start | bytes 1572872 | tf_op jit(solution)/shard_map/gather_sketched/ppermute | solution.py:25
  74.6 14.4 %collective-permute-start.22 = (bf16[2,512,256]{2,1,0:T(8,128)(2,1)S(1)}, bf16[2,512,256]{2,1,0:T(8,128)(2,1)S(1)}, u32[]{:S(2)}, u32[]{:S(2)}) collective-permute-start(bf16[2,512,256]{2,1,0:T(8,128)(2,1)S(1)} %pad_maximum_fusion.s0), channel_id=1, source_target_pairs={{0,32},{1,33},{2,34},{3,35},{4,36},{5,37},{6,38},{7,39},{8,40},{9,... | collective-permute-start | bytes 1572872 | tf_op jit(solution)/shard_map/gather_sketched/ppermute | solution.py:25
  88.9 7.7 %copy-start = (bf16[2,512,256]{2,1,0:T(8,128)(2,1)}, bf16[2,512,256]{2,1,0:T(8,128)(2,1)S(1)}, u32[]{:S(2)}) copy-start(bf16[2,512,256]{2,1,0:T(8,128)(2,1)S(1)} %collective-permute-done.22.s1) | copy-start | bytes 1572868
  89.0 7.6 %collective-permute-start.26 = (bf16[512,256]{1,0:T(8,128)(2,1)S(1)}, bf16[512,256]{1,0:T(8,128)(2,1)S(1)}, u32[]{:S(2)}, u32[]{:S(2)}) collective-permute-start(bf16[512,256]{1,0:T(8,128)(2,1)S(1)} %slice_bitcast_fusion), channel_id=1, source_target_pairs={{0,96},{1,97},{2,98},{3,99},{4,100},{5,101},{6,102},{7,103},{8,104... | collective-permute-start | bytes 786440 | tf_op jit(solution)/shard_map/gather_sketched/ppermute | solution.py:25
  89.4 8.0 %collective-permute-start.25 = (bf16[512,256]{1,0:T(8,128)(2,1)S(1)}, bf16[512,256]{1,0:T(8,128)(2,1)}, u32[]{:S(2)}, u32[]{:S(2)}) collective-permute-start(bf16[512,256]{1,0:T(8,128)(2,1)S(1)} %slice_bitcast_fusion.1), channel_id=1, source_target_pairs={{0,32},{1,33},{2,34},{3,35},{4,36},{5,37},{6,38},{7,39},{8,40},{9,... | collective-permute-start | bytes 786440 | tf_op jit(solution)/shard_map/gather_sketched/ppermute | solution.py:25
  90.6 6.0 %collective-permute-start.24 = (bf16[128,256]{1,0:T(8,128)(2,1)S(1)}, bf16[128,256]{1,0:T(8,128)(2,1)S(1)}, u32[]{:S(2)}, u32[]{:S(2)}) collective-permute-start(bf16[128,256]{1,0:T(8,128)(2,1)S(1)} %dynamic-slice_convert_fusion), channel_id=1, source_target_pairs={{0,16},{1,17},{2,18},{3,19},{4,20},{5,21},{6,22},{7,23},{8,24},{9,... | collective-permute-start | bytes 196616 | tf_op jit(solution)/shard_map/gather_inverse/ppermute | solution.py:25
  96.6 0.7 copy-start.3
  98.9 13.0 %collective-permute-start.27 = (bf16[256,128]{1,0:T(8,128)(2,1)S(1)}, bf16[256,128]{1,0:T(8,128)(2,1)S(1)}, u32[]{:S(2)}, u32[]{:S(2)}) collective-permute-start(bf16[256,128]{1,0:T(8,128)(2,1)S(1)} %get-tuple-element.61), channel_id=1, source_target_pairs={{0,0},{1,16},{2,2},{3,18},{4,4},{5,20},{6,6},{7,22},{8,8},{9,24},{... | collective-permute-start | bytes 196616 | tf_op jit(solution)/shard_map/exchange_coef/ppermute | solution.py:25
  105.4 7.4 %collective-permute-start.28 = (bf16[256,128]{1,0:T(8,128)(2,1)S(1)}, bf16[256,128]{1,0:T(8,128)(2,1)S(1)}, u32[]{:S(2)}, u32[]{:S(2)}) collective-permute-start(bf16[256,128]{1,0:T(8,128)(2,1)S(1)} %get-tuple-element.62), channel_id=1, source_target_pairs={{0,32},{1,48},{2,34},{3,50},{4,36},{5,52},{6,38},{7,54},{8,40},{9,... | collective-permute-start | bytes 196616 | tf_op jit(solution)/shard_map/exchange_coef/ppermute | solution.py:25
  105.7 8.1 %collective-permute-start.29 = (bf16[256,128]{1,0:T(8,128)(2,1)S(1)}, bf16[256,128]{1,0:T(8,128)(2,1)S(1)}, u32[]{:S(2)}, u32[]{:S(2)}) collective-permute-start(bf16[256,128]{1,0:T(8,128)(2,1)S(1)} %get-tuple-element.63), channel_id=1, source_target_pairs={{0,64},{1,80},{2,66},{3,82},{4,68},{5,84},{6,70},{7,86},{8,72},{9,... | collective-permute-start | bytes 196616 | tf_op jit(solution)/shard_map/exchange_coef/ppermute | solution.py:25
  111.1 6.2 %collective-permute-start.30 = (bf16[256,128]{1,0:T(8,128)(2,1)S(1)}, bf16[256,128]{1,0:T(8,128)(2,1)S(1)}, u32[]{:S(2)}, u32[]{:S(2)}) collective-permute-start(bf16[256,128]{1,0:T(8,128)(2,1)S(1)} %get-tuple-element.64), channel_id=1, source_target_pairs={{0,96},{1,112},{2,98},{3,114},{4,100},{5,116},{6,102},{7,118},{8,1... | collective-permute-start | bytes 196616 | tf_op jit(solution)/shard_map/exchange_coef/ppermute | solution.py:25
  118.9 14.2 %copy-start.4 = (bf16[512,256]{1,0:T(8,128)(2,1)S(1)}, bf16[512,256]{1,0:T(8,128)(2,1)}, u32[]{:S(2)}) copy-start(bf16[512,256]{1,0:T(8,128)(2,1)} %copy-done.3) | copy-start | bytes 786436
  118.9 25.5 %all-to-all-start.1 = ((bf16[8,1024,128]{2,1,0:T(8,128)(2,1)}), bf16[8,1024,128]{2,1,0:T(8,128)(2,1)}, u32[]{:S(2)}, u32[]{:S(2)}) async-start(bf16[8,1024,128]{2,1,0:T(8,128)(2,1)} %spread.1), calls=%async_computation.1 | async-start | bytes 4194304 | tf_op jit(solution)/shard_map/gather_coef/all_to_all | solution.py:362
  123.4 11.6 %copy-start.1 = (bf16[2,512,256]{2,1,0:T(8,128)(2,1)S(1)}, bf16[2,512,256]{2,1,0:T(8,128)(2,1)}, u32[]{:S(2)}) copy-start(bf16[2,512,256]{2,1,0:T(8,128)(2,1)} %copy-done) | copy-start | bytes 1572868
  123.4 5.8 %collective-permute-start.33 = (bf16[2,128,256]{2,1,0:T(8,128)(2,1)S(1)}, bf16[2,128,256]{2,1,0:T(8,128)(2,1)S(1)}, u32[]{:S(2)}, u32[]{:S(2)}) collective-permute-start(bf16[2,128,256]{2,1,0:T(8,128)(2,1)S(1)} %pad_maximum_fusion.4), channel_id=1, source_target_pairs={{0,96},{1,97},{2,98},{3,99},{4,100},{5,101},{6,102},{7,103},{8,104... | collective-permute-start | bytes 393224 | tf_op jit(solution)/shard_map/gather_inverse/ppermute | solution.py:25
  125.8 5.8 %collective-permute-start.32 = (bf16[2,128,256]{2,1,0:T(8,128)(2,1)S(1)}, bf16[2,128,256]{2,1,0:T(8,128)(2,1)S(1)}, u32[]{:S(2)}, u32[]{:S(2)}) collective-permute-start(bf16[2,128,256]{2,1,0:T(8,128)(2,1)S(1)} %pad_maximum_fusion.4), channel_id=1, source_target_pairs={{0,64},{1,65},{2,66},{3,67},{4,68},{5,69},{6,70},{7,71},{8,72},{9,... | collective-permute-start | bytes 393224 | tf_op jit(solution)/shard_map/gather_inverse/ppermute | solution.py:25
  126.1 6.8 %collective-permute-start.31 = (bf16[2,128,256]{2,1,0:T(8,128)(2,1)S(1)}, bf16[2,128,256]{2,1,0:T(8,128)(2,1)S(1)}, u32[]{:S(2)}, u32[]{:S(2)}) collective-permute-start(bf16[2,128,256]{2,1,0:T(8,128)(2,1)S(1)} %pad_maximum_fusion.4), channel_id=1, source_target_pairs={{0,32},{1,33},{2,34},{3,35},{4,36},{5,37},{6,38},{7,39},{8,40},{9,... | collective-permute-start | bytes 393224 | tf_op jit(solution)/shard_map/gather_inverse/ppermute | solution.py:25
  133.0 2.0 %collective-permute-start.34 = (bf16[4,2,128,256]{3,2,1,0:T(8,128)(2,1)S(1)}, bf16[4,2,128,256]{3,2,1,0:T(8,128)(2,1)S(1)}, u32[]{:S(2)}, u32[]{:S(2)}) collective-permute-start(bf16[4,2,128,256]{3,2,1,0:T(8,128)(2,1)S(1)} %pad_maximum_fusion.2.mine), channel_id=1, source_target_pairs={{0,1},{1,0},{2,3},{3,2},{4,5},{5,4},{6,7},{7,6},{8,9},{9,8},{10,11... | collective-permute-start | bytes 1572872 | tf_op jit(solution)/shard_map/gather_inverse/ppermute | solution.py:25
  144.4 4.4 %collective-permute-start.35 = (bf16[8,1024,128]{2,1,0:T(8,128)(2,1)}, bf16[8,1024,128]{2,1,0:T(8,128)(2,1)S(1)}, u32[]{:S(2)}, u32[]{:S(2)}) collective-permute-start(bf16[8,1024,128]{2,1,0:T(8,128)(2,1)} %all-to-all-done.1.mine), channel_id=1, source_target_pairs={{0,1},{1,0},{2,3},{3,2},{4,5},{5,4},{6,7},{7,6},{8,9},{9,8},{10,11... | collective-permute-start | bytes 6291464 | tf_op jit(solution)/shard_map/gather_coef/ppermute | solution.py:25

commit v2 on v1

--- a/solution.py
+++ b/solution.py
@@ -68,20 +68,29 @@
     return ref.at[:, pl.ds(pl.multiple_of(start, count), count)]
 
 
-def fetch(delta, starts, held, sems):
-    copies = [
-        pltpu.make_async_copy(columns(delta, start, held.shape[2]), held.at[n], sems.at[n])
-        for n, start in enumerate(starts)
-    ]
+def fetch(delta, starts, held, sems, pieces=(), near=None):
+    copies = []
+    for n, start in enumerate(starts):
+        pairs = [(columns(delta, start, held.shape[2]), held.at[n])]
+        if pieces:
+            pairs.append((pieces[n], near.at[n]))
+        copies.append(
+            [pltpu.make_async_copy(a, b, sems.at[m, n]) for m, (a, b) in enumerate(pairs)]
+        )
+        for copy in copies[-1]:
+            copy.start()
+    return copies
+
+
+def wait(copies):
     for copy in copies:
-        copy.start()
-    return copies
-
-
-def add_products(copies, pieces, out, held):
-    for n, (piece, copy) in enumerate(zip(pieces, copies)):
         copy.wait()
-        value = jnp.dot(held[n], piece[...], preferred_element_type=F32)
+
+
+def add_products(copies, out, held, near):
+    for n, pair in enumerate(copies):
+        wait(pair)
+        value = jnp.dot(held[n], near[n][...], preferred_element_type=F32)
         if n == 0:
             out[...] = value
         else:
@@ -89,21 +98,29 @@
 
 
 def early_kernel(layout, place, delta, *refs):
-    pieces, (out, held, sems) = refs[: len(layout)], refs[len(layout) :]
-    copies = fetch(delta, [place[at] for at in layout], held, sems)
-    add_products(copies, pieces, out, held)
+    pieces, (out, held, near, sems) = refs[: len(layout)], refs[len(layout) :]
+    copies = fetch(delta, [place[at] for at in layout], held, sems, pieces, near)
+    add_products(copies, out, held, [near.at[n] for n in range(len(layout))])
 
 
 def late_kernel(layout, place, delta, *refs):
     pieces, part = refs[: len(layout)], refs[len(layout)]
-    gram, rounded, turned, out, held, sems = refs[len(layout) + 1 :]
+    mine, theirs, sketched, turned, out, held, sems = refs[len(layout) + 1 :]
     copies = fetch(delta, [place[at] for at in layout], held, sems)
-    add_products(copies, pieces, out, held)
+    add_products(copies, out, held, pieces)
     total = out[...] + part[...]
     flipped = total.T
-    gram[...] = jnp.dot(flipped, total, precision=HIGH, preferred_element_type=F32)
-    rounded[...] = total.astype(BF16)
+    gram = jnp.dot(flipped, total, precision=HIGH, preferred_element_type=F32)
+    sketched[...] = total
     turned[...] = flipped.astype(BF16)
+    for core, to in ((0, (mine, theirs)), (1, (theirs, mine))):
+
+        @pl.when(place[0] == core)
+        def _(to=to):
+            for n in range(2):
+                at = n * BLK
+                to[n][:BLK] = gram[at : at + BLK, at : at + BLK]
+                to[n][BLK:] = gram[BLK + at // 2 : BLK + at // 2 + BLK // 2, :BLK]
 
 
 def product_kernel(place, delta, turned, sent, kept, held, sems):
@@ -114,8 +131,8 @@
         for g in range(4)
     ]
     copies = fetch(delta, [(2 * g + parity) * width for _, parity, g in blocks], held, sems)
-    for n, ((out, _, g), copy) in enumerate(zip(blocks, copies)):
-        copy.wait()
+    for n, ((out, _, g), pair) in enumerate(zip(blocks, copies)):
+        wait(pair)
         for q in range(2):
             tile = jnp.dot(
                 turned[...], held[n, :, q * 512 : (q + 1) * 512], preferred_element_type=F32
@@ -131,9 +148,19 @@
             out[n, d * rank : (d + 1) * rank] = tile[...]
 
 
-def inverse_kernel(gram, out, left):
-    size, wide = gram.shape[0], 16
-    left[...] = gram[...]
+def inverse_kernel(place, mine, theirs, out, left):
+    size, wide = out.shape[0], 16
+    half = BLK // 2
+    for core, parts in ((0, (mine, theirs)), (1, (theirs, mine))):
+
+        @pl.when(place[0] == core)
+        def _(parts=parts):
+            for n in range(2):
+                at = n * BLK
+                left[at : at + BLK, at : at + BLK] = parts[n][:BLK]
+                left[BLK + n * half : BLK + (n + 1) * half, :BLK] = parts[n][BLK:]
+
+    left[:BLK, BLK:] = left[BLK:, :BLK].T
     rows = lax.broadcasted_iota(jnp.int32, (size, size), 0)
     cols = lax.broadcasted_iota(jnp.int32, (size, size), 1)
     out[...] = (rows == cols).astype(F32)
@@ -182,18 +209,23 @@
         outs[d][...] = columns(held, (place[2] + d) % 4 * BLK, BLK)[...]
 
 
-def basis_kernel(place, s0, s1, s2, s3, mine, theirs, left):
-    for d, sketched in enumerate((s0, s1, s2, s3)):
-        for n, yh in enumerate((place[3], 1 - place[3])):
-            for core, inverse in ((place[0], mine), (1 - place[0], theirs)):
-                basis = lax.dot_general(
-                    sketched[yh],
-                    inverse[d, yh],
-                    (((1,), (1,)), ((), ())),
-                    preferred_element_type=F32,
-                )
-                start = pl.multiple_of((2 * (4 * n + d) + core) * BLK, BLK)
-                left[:, pl.ds(start, BLK)] = recode(basis, 1)
+def basis_kernel(sketched, inverse, out):
+    basis = lax.dot_general(
+        sketched[...],
+        inverse[...],
+        (((1,), (1,)), ((), ())),
+        precision=HIGH,
+        preferred_element_type=F32,
+    )
+    for b in range(2):
+        out[:, b * BLK : (b + 1) * BLK] = recode(basis[:, b * BLK : (b + 1) * BLK], 1)
+
+
+def lay_kernel(place, q0, q1, q2, q3, left):
+    rank = q0.shape[2]
+    for d, q in enumerate((q0, q1, q2, q3)):
+        left[:, d * rank : (d + 1) * rank] = q[place[3]]
+        left[:, (4 + d) * rank : (5 + d) * rank] = q[1 - place[3]]
 
 
 def partial_kernel(left, mine, out):
@@ -256,88 +288,103 @@
     starts = [
         (2 * (2 * (n % 4) + l) + c) * depth
         for c in (core, 1 - core)
-        for n, l in ((z, yl), (z - 1, yl), (z + 1, yl), (z, 1 - yl), (z - 2, yl))
+        for n, l in ((z, yl), (z - 1, yl), (z + 1, yl), (z, 1 - yl), (z - 2, yl), (z - 2, 1 - yl))
     ]
     starts += [
-        (2 * (2 * (n % 4) + 1 - yl) + c) * depth
-        for c in (core, 1 - core)
-        for n in (z - 1, z + 1, z - 2)
+        (2 * (2 * (n % 4) + 1 - yl) + c) * depth for c in (core, 1 - core) for n in (z - 1, z + 1)
     ]
     place = jnp.stack([core, 0, x, (core + yh) % 2] + starts).astype(jnp.int32)
-    fetched = lambda count, width: [
-        pltpu.VMEM((count, rows, width), BF16),
-        pltpu.SemaphoreType.DMA((count,)),
+    fetched = lambda count: [
+        pltpu.VMEM((count, rows, depth), BF16),
+        pltpu.VMEM((count, depth, rank), BF16),
+        pltpu.SemaphoreType.DMA((2, count)),
     ]
+    mid = depth // 2
     with jax.named_scope("gather_sketch"):
+        z2 = shift(sketch, dz=2)
         z1, z3 = shift(sketch, dz=1), shift(sketch, dz=-1)
-        pieces = [sketch, z1, z3, up(sketch), shift(sketch, dz=2)]
-        y1, y3, y2 = up(z1), down(z3), down(pieces[4])
+        pieces = [sketch, z1, z3, up(sketch), z2]
+        y2 = [up(z2[:mid]), down(z2[mid:])]
+        z1, z3, *y2 = fence((z1, z3, *y2))
+        y1, y3 = up(z1), down(z3)
+        pieces.append(jnp.concatenate(y2, 0))
         pieces += swap(pieces)
     part = call(
-        functools.partial(early_kernel, range(4, 14)),
+        functools.partial(early_kernel, range(4, 16)),
         [((rows, rank), F32)],
-        1.4e9,
+        1.6e9,
         "sketched_early",
-        scratch=fetched(10, depth),
-        far=(1,),
+        scratch=fetched(12),
+        far=range(1, 14),
     )(place, local, *pieces)[0]
-    y1, y3, y2, part = fence((y1, y3, y2, part))
+    y1, y3, part = fence((y1, y3, part))
     with jax.named_scope("gather_sketch"):
-        pieces = [y1, y3, y2]
+        pieces = [y1, y3]
         pieces += swap(pieces)
-    gram, rounded, turned = call(
-        functools.partial(late_kernel, range(14, 20)),
-        [((rank, rank), F32), ((rows, rank), BF16), ((rank, rows), BF16)],
-        1e9,
+    gram_part = ((BLK + BLK // 2, BLK), F32)
+    mine, theirs, sketched, turned = call(
+        functools.partial(late_kernel, range(16, 20)),
+        [gram_part, gram_part, ((rows, rank), F32), ((rank, rows), BF16)],
+        8e8,
         "sketched_late",
-        scratch=[pltpu.VMEM((rows, rank), F32)] + fetched(6, depth),
+        scratch=[
+            pltpu.VMEM((rows, rank), F32),
+            pltpu.VMEM((4, rows, depth), BF16),
+            pltpu.SemaphoreType.DMA((1, 4)),
+        ],
         far=(1,),
     )(place, local, *pieces, part)
 
     with jax.named_scope("sum_gram"):
-        half = rank // 2
-        mine = lax.dynamic_slice_in_dim(gram, core * half, half, 0)
-        theirs = lax.dynamic_slice_in_dim(gram, (1 - core) * half, half, 0)
         mine = mine + shift(theirs, dc=1)
         mine, turned = fence((mine, turned))
         got = shift(mine, dl=1)
     shares = ((8, rank, 4 * BLK), BF16)
     sent, kept = call(
-        product_kernel, [shares] * 2, 2.2e9, "product", vmem=24, scratch=fetched(8, 1024), far=(1,)
+        product_kernel,
+        [shares] * 2,
+        2.2e9,
+        "product",
+        vmem=24,
+        scratch=[pltpu.VMEM((8, rows, 1024), BF16), pltpu.SemaphoreType.DMA((1, 8))],
+        far=(1,),
     )(place, local, turned)
     got, sent, kept = fence((got, sent, kept))
-    with jax.named_scope("sum_cores"):
-        kept = (kept.astype(F32) + shift(sent, dc=1).astype(F32)).astype(BF16)
     with jax.named_scope("sum_gram"):
         mine = mine + got
-        mine = mine + move(mine, lambda x, h, z, l, c: (x, h, z ^ 1, l, c))
-        mine, rounded = fence((mine, rounded))
+        got = move(mine, lambda x, h, z, l, c: (x, h, z ^ 1, l, c))
+    with jax.named_scope("sum_cores"):
+        other = shift(sent, dc=1)
+    kept, other, mine = fence((kept, other, mine + got))
+    with jax.named_scope("sum_cores"):
+        kept = (kept.astype(F32) + other.astype(F32)).astype(BF16)
+    with jax.named_scope("sum_gram"):
         got = move(mine, lambda x, h, z, l, c: (x, h, 3 - z, l, c))
         got, kept = fence((got, kept))
         mine = mine + got
-    with jax.named_scope("gather_sketched"):
-        both = jnp.stack([rounded, shift(rounded, dh=1)])
-    kept, mine, both = fence((kept, mine, both))
-    with jax.named_scope("gather_sketched"):
-        right, left = shift(both, dx=1), shift(both, dx=-1)
+    mine, kept = fence((mine, kept))
     with jax.named_scope("sum_fsdp"):
         parts = lax.all_to_all(kept, ("z", "yl"), 0, 0, tiled=True)
 
     with jax.named_scope("sum_gram"):
         theirs = shift(mine, dc=1)
-        zero = core == 0
-        gram = jnp.concatenate([jnp.where(zero, mine, theirs), jnp.where(zero, theirs, mine)], 0)
     inverse = call(
-        inverse_kernel, [((rank, rank), F32)], 3e9, "inverse", False, [pltpu.VMEM((rank, rank), F32)]
-    )(gram)[0]
-
-    inverse, right, left = fence((inverse, right, left))
-    with jax.named_scope("gather_sketched"):
-        far = [shift(right[0], dx=1), shift(left[1], dx=-1)]
-    with jax.named_scope("gather_inverse"):
-        half_inverse = lax.dynamic_slice_in_dim(inverse, core * half, half, 0).astype(BF16)
-        pair = jnp.stack([half_inverse, shift(half_inverse, dh=1)])
-    parts, pair, *far = fence((parts, pair, *far))
+        inverse_kernel,
+        [((rank, rank), F32)],
+        3e9,
+        "inverse",
+        scratch=[pltpu.VMEM((rank, rank), F32)],
+    )(place, mine, theirs)[0]
+    basis = call(basis_kernel, [((rows, rank), BF16)], 4e8, "basis", False)(sketched, inverse)[0]
+    with jax.named_scope("gather_basis"):
+        both = jnp.stack([basis, shift(basis, dh=1)])
+    parts, both = fence((parts, both))
+    with jax.named_scope("gather_basis"):
+        right, left = shift(both, dx=1), shift(both, dx=-1)
+        far = jnp.stack([shift(right[0], dx=1), shift(left[1], dx=-1)])
+    operand = call(lay_kernel, [((rows, 8 * rank), BF16)], 1e8, "lay")(
+        place, both, right, far, left
+    )[0]
     tiles = call(
         coef_kernel,
         [((rank, BLK), BF16)] * 4,
@@ -349,15 +396,7 @@
         tiles = [
             move(v, lambda x, h, z, l, c, d=d: (x + d, c, z, l, h)) for d, v in enumerate(tiles)
         ]
-    with jax.named_scope("gather_inverse"):
-        inverses = jnp.stack([pair] + [shift(pair, dx=d) for d in range(1, 4)])
-        other = shift(inverses, dc=1)
-    sketches = [both, right, jnp.stack(far), left]
-    operand = call(basis_kernel, [((rows, 8 * rank), BF16)], 5.4e8, "basis")(
-        place, *sketches, inverses, other
-    )[0]
-
-    tiles = call(spread_kernel, [((8, 4 * rank, BLK), BF16)], 0, "spread", False)(*tiles)[0]
+    tiles = call(spread_kernel, [pltpu.VMEM((8, 4 * rank, BLK), BF16)], 0, "spread", False)(*tiles)[0]
     with jax.named_scope("gather_coef"):
         mine, operand = fence((lax.all_to_all(tiles, ("z", "yl"), 0, 0, tiled=True), operand))
         theirs = shift(mine, dc=1)

time: 155 us -> 149 us (0.961)
  starting transfers between devices: 61.1 us -> 59.3 us
  waiting for transfers between devices: 47.9 us -> 46.1 us
    all_to_all x1, waiting for transfers between devices: 6.84 us -> 0.93 us  [body(): lax.all_to_all(tiles, ('z', 'yl'), 0, 0, tiled=True)]
    ppermute x36 -> x32, starting transfers between devices: 53 us -> 48.6 us  [move(): return lax.ppermute(value, AXES, pairs)]
    ppermute x36 -> x32, waiting for transfers between devices: 41.1 us -> 45.2 us  [move(): return lax.ppermute(value, AXES, pairs)]
    all_to_all x1, starting transfers between devices: 3.62 us -> 5.56 us  [body(): parts = lax.all_to_all(kept, ('z', 'yl'), 0, 0, tiled=True)]
    pallas_call x8 -> x9, Pallas kernels: 33.7 us -> 33.9 us  [run(): pl.pallas_call(kernel, in_specs=[SMEM if smem and n == 0 else FAR if n in...]
  transfers between devices with their start and end apart: 38 -> 34, of which waited for: 22 -> 16; matrix products, arithmetic and copies ran while one was open for 2% -> 2% of each run, Pallas kernels for 17% -> 18%
where the time goes in v2:
time: 149 us
  starting transfers between devices  59.3 us (40%)
  waiting for transfers between devices  46.1 us (31%)
  Pallas kernels  39.5 us (27%)
  other arithmetic  2.12 us (1%)
    ppermute x32, starting transfers between devices, move(): return lax.ppermute(value, AXES, pairs)  48.6 us
    ppermute x32, waiting for transfers between devices, move(): return lax.ppermute(value, AXES, pairs)  45.2 us
    pallas_call x9, Pallas kernels, run(): pl.pallas_call(kernel, in_specs=[SMEM if smem and n == 0 else FAR if n in...  33.9 us
    pallas_call x1, Pallas kernels, update_call(): pl.pallas_call(update_kernel, grid=(4,), in_specs=[tile, tile, tile, pl.B...  5.58 us
    all_to_all x1, starting transfers between devices, body(): parts = lax.all_to_all(kept, ('z', 'yl'), 0, 0, tiled=True)  5.56 us
    all_to_all x1, starting transfers between devices, body(): lax.all_to_all(tiles, ('z', 'yl'), 0, 0, tiled=True)  5.1 us
  transfers between devices with their start and end apart: 34, of which 16 were waited for; matrix products, arithmetic and copies ran while one was open for 2% of the time, Pallas kernels for 18%

profile of v2, /device:TPU:1, one launch (start us, length us, event | category | flops | bytes accessed | tf_op | source)
XLA Modules:
  0.0 149.0 jit_solution(6409642313668458525)
XLA Ops:
  0.6 4.5 %collective-permute-start.2 = (bf16[512,256]{1,0:T(8,128)(2,1)}, bf16[512,256]{1,0:T(8,128)(2,1)S(1)}, u32[]{:S(2)}, u32[]{:S(2)}) collective-permute-start(bf16[512,256]{1,0:T(8,128)(2,1)} %refs_0_.1), channel_id=1, source_target_pairs={{0,8},{1,9},{2,10},{3,11},{4,12},{5,13},{6,14},{7,15},{8,0},{9,1},... | collective-permute-start | bytes 786440 | tf_op jit(solution)/shard_map/gather_sketch/ppermute | solution.py:25
  5.1 1.3 collective-permute-start.7
  6.9 1.0 collective-permute-start
  7.9 3.5 %collective-permute-done.2.refs_4_ = bf16[512,256]{1,0:T(8,128)(2,1)S(1)} collective-permute-done((bf16[512,256]{1,0:T(8,128)(2,1)}, bf16[512,256]{1,0:T(8,128)(2,1)S(1)}, u32[]{:S(2)}, u32[]{:S(2)}) %collective-permute-start.2) | collective-permute-done | bytes 262176 | tf_op jit(solution)/shard_map/gather_sketch/ppermute | solution.py:25
  11.4 2.8 %collective-permute-start.4 = (bf16[256,256]{1,0:T(8,128)(2,1)S(1)}, bf16[256,256]{1,0:T(8,128)(2,1)S(1)}, u32[]{:S(2)}, u32[]{:S(2)}) collective-permute-start(bf16[256,256]{1,0:T(8,128)(2,1)S(1)} %get-tuple-element.68), channel_id=1, source_target_pairs={{0,18},{1,19},{2,0},{3,1},{4,22},{5,23},{6,4},{7,5},{8,26},{9,27},... | collective-permute-start | bytes 393224 | tf_op jit(solution)/shard_map/gather_sketch/ppermute | solution.py:25
  14.2 2.4 %collective-permute-start.8 = (bf16[512,256]{1,0:T(8,128)(2,1)}, bf16[512,256]{1,0:T(8,128)(2,1)S(1)}, u32[]{:S(2)}, u32[]{:S(2)}) collective-permute-start(bf16[512,256]{1,0:T(8,128)(2,1)} %refs_0_.1), channel_id=1, source_target_pairs={{0,1},{1,0},{2,3},{3,2},{4,5},{5,4},{6,7},{7,6},{8,9},{9,8},{10,11... | collective-permute-start | bytes 786440 | tf_op jit(solution)/shard_map/gather_sketch/ppermute | solution.py:25
  16.7 0.9 collective-permute-done.1.refs_2_
  17.6 1.4 collective-permute-start.12
  19.5 3.2 %collective-permute-start.9 = (bf16[512,256]{1,0:T(8,128)(2,1)S(1)}, bf16[512,256]{1,0:T(8,128)(2,1)S(1)}, u32[]{:S(2)}, u32[]{:S(2)}) collective-permute-start(bf16[512,256]{1,0:T(8,128)(2,1)S(1)} %collective-permute-done.refs_1_), channel_id=1, source_target_pairs={{0,1},{1,0},{2,3},{3,2},{4,5},{5,4},{6,7},{7,6},{8,9},{9,8},{10,11... | collective-permute-start | bytes 786440 | tf_op jit(solution)/shard_map/gather_sketch/ppermute | solution.py:25
  23.0 2.6 %collective-permute-start.6 = (bf16[512,256]{1,0:T(8,128)(2,1)S(1)}, bf16[512,256]{1,0:T(8,128)(2,1)S(1)}, u32[]{:S(2)}, u32[]{:S(2)}) collective-permute-start(bf16[512,256]{1,0:T(8,128)(2,1)S(1)} %collective-permute-done.1.refs_2_), channel_id=1, source_target_pairs={{0,18},{1,19},{2,0},{3,1},{4,22},{5,23},{6,4},{7,5},{8,26},{9,27},... | collective-permute-start | bytes 786440 | tf_op jit(solution)/shard_map/gather_sketch/ppermute | solution.py:25
  25.9 0.6 copy-done.8
  26.7 5.8 %sketched_early.1.refs_4_ = f32[512,256]{1,0:T(8,128)S(1)} custom-call(s32[20]{0:T(128)S(1)} %stack.97.place, bf16[512,8192]{1,0:T(8,128)(2,1)} %bitcast.29, bf16[512,256]{1,0:T(8,128)(2,1)} %refs_0_.1, bf16[512,256]{1,0:T(8,128)(2,1)} %copy-done.4, bf16[512,256]{1,0:T(8,128)(2,1)} %copy-done.2, bf16[512,256]{1,0:T(8,128)(2,1)} %copy-done.3, ...), custom_call_target="tpu_custom_call" | custom-call | flops 1600000000 | bytes 4194304 | tf_op jit(solution)/shard_map/sketched_early/pallas_call | solution.py:49
  32.5 1.1 collective-permute-start.14
  33.6 1.1 collective-permute-done.14.refs_2_
  35.1 3.9 %sketched_late.1 = (f32[192,128]{1,0:T(8,128)S(1)}, f32[192,128]{1,0:T(8,128)S(1)}, f32[512,256]{1,0:T(8,128)S(1)}, bf16[256,512]{1,0:T(8,128)(2,1)S(1)}) custom-call(s32[20]{0:T(128)S(1)} %stack.97.place, bf16[512,8192]{1,0:T(8,128)(2,1)} %bitcast.30, bf16[512,256]{1,0:T(8,128)(2,1)S(1)} %collective-permute-done.5.refs_0_, ...), custom_call_target="tpu_custom_call" | custom-call | flops 800000000 | bytes 4194304 | tf_op jit(solution)/shard_map/sketched_late/pallas_call | solution.py:49
  39.0 0.4 collective-permute-start.16
  39.4 0.9 collective-permute-done.16
  40.5 5.4 %product.1 = (bf16[8,256,512]{2,1,0:T(8,128)(2,1)S(1)}, bf16[8,256,512]{2,1,0:T(8,128)(2,1)S(1)}) custom-call(s32[20]{0:T(128)S(1)} %stack.97.place, bf16[512,8192]{1,0:T(8,128)(2,1)} %bitcast.31, bf16[256,512]{1,0:T(8,128)(2,1)S(1)} %get-tuple-element.46.turned), custom_call_target="tpu_custom_call" | custom-call | flops 2200000000 | bytes 4194304 | tf_op jit(solution)/shard_map/product/pallas_call | solution.py:49
  46.3 1.6 %collective-permute-start.19 = (f32[192,128]{1,0:T(8,128)S(1)}, f32[192,128]{1,0:T(8,128)S(1)}, u32[]{:S(2)}, u32[]{:S(2)}) collective-permute-start(f32[192,128]{1,0:T(8,128)S(1)} %add.166), channel_id=1, source_target_pairs={{0,4},{1,5},{2,6},{3,7},{4,0},{5,1},{6,2},{7,3},{8,12},{9,13},{10,... | collective-permute-start | bytes 294920 | tf_op jit(solution)/shard_map/sum_gram/ppermute | solution.py:25
  47.9 2.9 %collective-permute-done.19 = f32[192,128]{1,0:T(8,128)S(1)} collective-permute-done((f32[192,128]{1,0:T(8,128)S(1)}, f32[192,128]{1,0:T(8,128)S(1)}, u32[]{:S(2)}, u32[]{:S(2)}) %collective-permute-start.19) | collective-permute-done | bytes 98336 | tf_op jit(solution)/shard_map/sum_gram/ppermute | solution.py:25
  50.8 3.5 %collective-permute-start.20 = (f32[192,128]{1,0:T(8,128)S(1)}, f32[192,128]{1,0:T(8,128)S(1)}, u32[]{:S(2)}, u32[]{:S(2)}) collective-permute-start(f32[192,128]{1,0:T(8,128)S(1)} %add.167), channel_id=1, source_target_pairs={{0,12},{1,13},{2,14},{3,15},{4,8},{5,9},{6,10},{7,11},{8,4},{9,5},... | collective-permute-start | bytes 294920 | tf_op jit(solution)/shard_map/sum_gram/ppermute | solution.py:25
  54.3 2.0 %add_convert_fusion = bf16[8,256,512]{2,1,0:T(8,128)(2,1)} fusion(bf16[8,256,512]{2,1,0:T(8,128)(2,1)S(1)} %collective-permute-done.18, bf16[8,256,512]{2,1,0:T(8,128)(2,1)S(1)} %get-tuple-element.53), kind=kLoop, calls=%fused_computation | loop fusion | flops 4194304 | bytes 6291456 | tf_op jit(solution)/shard_map/sum_cores/convert_element_type | solution.py:360
  56.4 5.6 %all-to-all-start = ((bf16[8,256,512]{2,1,0:T(8,128)(2,1)}), bf16[8,256,512]{2,1,0:T(8,128)(2,1)S(1)}, u32[]{:S(2)}, u32[]{:S(2)}) async-start(bf16[8,256,512]{2,1,0:T(8,128)(2,1)} %add_convert_fusion), calls=%async_computation | async-start | bytes 4194304 | tf_op jit(solution)/shard_map/sum_fsdp/all_to_all | solution.py:367
  61.9 2.2 %collective-permute-start.21 = (f32[192,128]{1,0:T(8,128)S(1)}, f32[192,128]{1,0:T(8,128)S(1)}, u32[]{:S(2)}, u32[]{:S(2)}) collective-permute-start(f32[192,128]{1,0:T(8,128)S(1)} %add.169.mine), channel_id=1, source_target_pairs={{0,1},{1,0},{2,3},{3,2},{4,5},{5,4},{6,7},{7,6},{8,9},{9,8},{10,11... | collective-permute-start | bytes 294920 | tf_op jit(solution)/shard_map/sum_gram/ppermute | solution.py:25
  64.2 0.9 collective-permute-done.21.theirs
  65.1 11.3 %inverse.1 = f32[256,256]{1,0:T(8,128)S(1)} custom-call(s32[20]{0:T(128)S(1)} %stack.97.place, f32[192,128]{1,0:T(8,128)S(1)} %add.169.mine, f32[192,128]{1,0:T(8,128)S(1)} %collective-permute-done.21.theirs), custom_call_target="tpu_custom_call" | custom-call | flops 3000000000 | bytes 4194304 | tf_op jit(solution)/shard_map/inverse/pallas_call | solution.py:49
  76.4 0.7 basis.1
  77.2 2.4 %collective-permute-start.22 = (bf16[512,256]{1,0:T(8,128)(2,1)S(1)}, bf16[512,256]{1,0:T(8,128)(2,1)S(1)}, u32[]{:S(2)}, u32[]{:S(2)}) collective-permute-start(bf16[512,256]{1,0:T(8,128)(2,1)S(1)} %basis.1), channel_id=1, source_target_pairs={{0,16},{1,17},{2,18},{3,19},{4,20},{5,21},{6,22},{7,23},{8,24},{9,... | collective-permute-start | bytes 786440 | tf_op jit(solution)/shard_map/gather_basis/ppermute | solution.py:25
  79.6 11.6 %collective-permute-done.22 = bf16[512,256]{1,0:T(8,128)(2,1)S(1)} collective-permute-done((bf16[512,256]{1,0:T(8,128)(2,1)S(1)}, bf16[512,256]{1,0:T(8,128)(2,1)S(1)}, u32[]{:S(2)}, u32[]{:S(2)}) %collective-permute-start.22) | collective-permute-done | bytes 262176 | tf_op jit(solution)/shard_map/gather_basis/ppermute | solution.py:25
  91.3 1.5 %coef.1 = (bf16[256,128]{1,0:T(8,128)(2,1)S(1)}, bf16[256,128]{1,0:T(8,128)(2,1)S(1)}, bf16[256,128]{1,0:T(8,128)(2,1)S(1)}, bf16[256,128]{1,0:T(8,128)(2,1)S(1)}) custom-call(s32[20]{0:T(128)S(1)} %stack.97.place, f32[256,256]{1,0:T(8,128)S(1)} %inverse.1, bf16[8,256,512]{2,1,0:T(8,128)(2,1)S(1)} %all-to-all-done.parts), custom_call_target="tpu_custom_call" | custom-call | flops 400000000 | bytes 4194304 | tf_op jit(solution)/shard_map/coef/pallas_call | solution.py:49
  92.8 5.5 %collective-permute-start.23 = (bf16[256,128]{1,0:T(8,128)(2,1)S(1)}, bf16[256,128]{1,0:T(8,128)(2,1)S(1)}, u32[]{:S(2)}, u32[]{:S(2)}) collective-permute-start(bf16[256,128]{1,0:T(8,128)(2,1)S(1)} %get-tuple-element.61), channel_id=1, source_target_pairs={{0,0},{1,16},{2,2},{3,18},{4,4},{5,20},{6,6},{7,22},{8,8},{9,24},{... | collective-permute-start | bytes 196616 | tf_op jit(solution)/shard_map/exchange_coef/ppermute | solution.py:25
  98.3 1.0 collective-permute-start.24
  99.3 5.4 %collective-permute-start.25 = (bf16[256,128]{1,0:T(8,128)(2,1)S(1)}, bf16[256,128]{1,0:T(8,128)(2,1)S(1)}, u32[]{:S(2)}, u32[]{:S(2)}) collective-permute-start(bf16[256,128]{1,0:T(8,128)(2,1)S(1)} %get-tuple-element.63), channel_id=1, source_target_pairs={{0,64},{1,80},{2,66},{3,82},{4,68},{5,84},{6,70},{7,86},{8,72},{9,... | collective-permute-start | bytes 196616 | tf_op jit(solution)/shard_map/exchange_coef/ppermute | solution.py:25
  104.7 0.9 collective-permute-start.26
  105.7 1.7 %collective-permute-done.25.t2 = bf16[256,128]{1,0:T(8,128)(2,1)S(1)} collective-permute-done((bf16[256,128]{1,0:T(8,128)(2,1)S(1)}, bf16[256,128]{1,0:T(8,128)(2,1)S(1)}, u32[]{:S(2)}, u32[]{:S(2)}) %collective-permute-start.25) | collective-permute-done | bytes 65568 | tf_op jit(solution)/shard_map/exchange_coef/ppermute | solution.py:25
  107.4 4.0 %collective-permute-done.26.t3 = bf16[256,128]{1,0:T(8,128)(2,1)S(1)} collective-permute-done((bf16[256,128]{1,0:T(8,128)(2,1)S(1)}, bf16[256,128]{1,0:T(8,128)(2,1)S(1)}, u32[]{:S(2)}, u32[]{:S(2)}) %collective-permute-start.26) | collective-permute-done | bytes 65568 | tf_op jit(solution)/shard_map/exchange_coef/ppermute | solution.py:25
  111.4 1.6 %spread.1 = bf16[8,1024,128]{2,1,0:T(8,128)(2,1)} custom-call(bf16[256,128]{1,0:T(8,128)(2,1)S(1)} %collective-permute-done.23.t0, bf16[256,128]{1,0:T(8,128)(2,1)S(1)} %collective-permute-done.24.t1, bf16[256,128]{1,0:T(8,128)(2,1)S(1)} %collective-permute-done.25.t2, bf16[256,128]{1,0:T(8,128)(2,1)S(1)} %collective-permute-done.26.t3), custom_call_target="tpu_custom_call" | custom-call | bytes 4194304 | tf_op jit(solution)/shard_map/spread/pallas_call | solution.py:49
  113.0 5.1 %all-to-all-start.1 = ((bf16[8,1024,128]{2,1,0:T(8,128)(2,1)}), bf16[8,1024,128]{2,1,0:T(8,128)(2,1)}, u32[]{:S(2)}, u32[]{:S(2)}) async-start(bf16[8,1024,128]{2,1,0:T(8,128)(2,1)} %spread.1), calls=%async_computation.1 | async-start | bytes 4194304 | tf_op jit(solution)/shard_map/gather_coef/all_to_all | solution.py:401
  118.1 1.9 %collective-permute-start.29 = (bf16[2,512,256]{2,1,0:T(8,128)(2,1)S(1)}, bf16[2,512,256]{2,1,0:T(8,128)(2,1)S(1)}, u32[]{:S(2)}, u32[]{:S(2)}) collective-permute-start(bf16[2,512,256]{2,1,0:T(8,128)(2,1)S(1)} %pad_maximum_fusion.q0), channel_id=1, source_target_pairs={{0,96},{1,97},{2,98},{3,99},{4,100},{5,101},{6,102},{7,103},{8,104... | collective-permute-start | bytes 1572872 | tf_op jit(solution)/shard_map/gather_basis/ppermute | solution.py:25
  119.9 9.1 %collective-permute-done.29.q3 = bf16[2,512,256]{2,1,0:T(8,128)(2,1)S(1)} collective-permute-done((bf16[2,512,256]{2,1,0:T(8,128)(2,1)S(1)}, bf16[2,512,256]{2,1,0:T(8,128)(2,1)S(1)}, u32[]{:S(2)}, u32[]{:S(2)}) %collective-permute-start.29) | collective-permute-done | bytes 524320 | tf_op jit(solution)/shard_map/gather_basis/ppermute | solution.py:25
  129.1 1.6 %collective-permute-start.30 = (bf16[512,256]{1,0:T(8,128)(2,1)S(1)}, bf16[512,256]{1,0:T(8,128)(2,1)S(1)}, u32[]{:S(2)}, u32[]{:S(2)}) collective-permute-start(bf16[512,256]{1,0:T(8,128)(2,1)S(1)} %slice_bitcast_fusion), channel_id=1, source_target_pairs={{0,96},{1,97},{2,98},{3,99},{4,100},{5,101},{6,102},{7,103},{8,104... | collective-permute-start | bytes 786440 | tf_op jit(solution)/shard_map/gather_basis/ppermute | solution.py:25
  130.8 3.6 %collective-permute-done.30 = bf16[512,256]{1,0:T(8,128)(2,1)S(1)} collective-permute-done((bf16[512,256]{1,0:T(8,128)(2,1)S(1)}, bf16[512,256]{1,0:T(8,128)(2,1)S(1)}, u32[]{:S(2)}, u32[]{:S(2)}) %collective-permute-start.30) | collective-permute-done | bytes 262176 | tf_op jit(solution)/shard_map/gather_basis/ppermute | solution.py:25
  134.4 2.8 %collective-permute-done.28 = bf16[512,256]{1,0:T(8,128)(2,1)S(1)} collective-permute-done((bf16[512,256]{1,0:T(8,128)(2,1)S(1)}, bf16[512,256]{1,0:T(8,128)(2,1)S(1)}, u32[]{:S(2)}, u32[]{:S(2)}) %collective-permute-start.28) | collective-permute-done | bytes 262176 | tf_op jit(solution)/shard_map/gather_basis/ppermute | solution.py:25
  137.3 0.8 lay.1.left
  138.1 0.9 all-to-all-done.1.mine
  139.0 2.9 %partial.1.part = f32[512,1024]{1,0:T(8,128)S(1)} custom-call(bf16[512,2048]{1,0:T(8,128)(2,1)S(1)} %lay.1.left, bf16[8,1024,128]{2,1,0:T(8,128)(2,1)} %all-to-all-done.1.mine), custom_call_target="tpu_custom_call" | custom-call | flops 1100000000 | bytes 4194304 | tf_op jit(solution)/shard_map/partial/pallas_call | solution.py:49
  141.9 1.5 %collective-permute-done.31.theirs = bf16[8,1024,128]{2,1,0:T(8,128)(2,1)S(1)} collective-permute-done((bf16[8,1024,128]{2,1,0:T(8,128)(2,1)}, bf16[8,1024,128]{2,1,0:T(8,128)(2,1)S(1)}, u32[]{:S(2)}, u32[]{:S(2)}) %collective-permute-start.31) | collective-permute-done | bytes 2097184 | tf_op jit(solution)/shard_map/gather_coef/ppermute | solution.py:25
  143.4 5.6 %update.1 = (f32[512,1024]{1,0:T(8,128)}, f32[512,1024]{1,0:T(8,128)}) custom-call(f32[512,1024]{1,0:T(8,128)} %params.1, f32[512,1024]{1,0:T(8,128)} %momentum.1, f32[512,1024]{1,0:T(8,128)S(1)} %partial.1.part, bf16[512,2048]{1,0:T(8,128)(2,1)S(1)} %lay.1.left, bf16[8,1024,128]{2,1,0:T(8,128)(2,1)S(1)} %collective-permute-done.31.theirs), custom_call_target="tpu_custom_call" | custom-call | flops 1100000000 | bytes 14000000 | tf_op jit(solution)/shard_map/update/pallas_call | solution.py:253
  (65 shorter events, 2.9 us)
Async XLA Ops:
  0.6 10.8 %collective-permute-start.2 = (bf16[512,256]{1,0:T(8,128)(2,1)}, bf16[512,256]{1,0:T(8,128)(2,1)S(1)}, u32[]{:S(2)}, u32[]{:S(2)}) collective-permute-start(bf16[512,256]{1,0:T(8,128)(2,1)} %refs_0_.1), channel_id=1, source_target_pairs={{0,8},{1,9},{2,10},{3,11},{4,12},{5,13},{6,14},{7,15},{8,0},{9,1},... | collective-permute-start | bytes 786440 | tf_op jit(solution)/shard_map/gather_sketch/ppermute | solution.py:25
  5.1 9.1 %collective-permute-start.7 = (bf16[512,256]{1,0:T(8,128)(2,1)}, bf16[512,256]{1,0:T(8,128)(2,1)S(1)}, u32[]{:S(2)}, u32[]{:S(2)}) collective-permute-start(bf16[512,256]{1,0:T(8,128)(2,1)} %refs_0_.1), channel_id=1, source_target_pairs={{0,2},{1,3},{2,16},{3,17},{4,6},{5,7},{6,20},{7,21},{8,10},{9,11},... | collective-permute-start | bytes 786440 | tf_op jit(solution)/shard_map/gather_sketch/ppermute | solution.py:25
  6.4 11.1 %collective-permute-start.1 = (bf16[512,256]{1,0:T(8,128)(2,1)}, bf16[512,256]{1,0:T(8,128)(2,1)S(1)}, u32[]{:S(2)}, u32[]{:S(2)}) collective-permute-start(bf16[512,256]{1,0:T(8,128)(2,1)} %refs_0_.1), channel_id=1, source_target_pairs={{0,12},{1,13},{2,14},{3,15},{4,0},{5,1},{6,2},{7,3},{8,4},{9,5},{1... | collective-permute-start | bytes 786440 | tf_op jit(solution)/shard_map/gather_sketch/ppermute | solution.py:25
  6.9 12.1 %collective-permute-start = (bf16[512,256]{1,0:T(8,128)(2,1)}, bf16[512,256]{1,0:T(8,128)(2,1)S(1)}, u32[]{:S(2)}, u32[]{:S(2)}) collective-permute-start(bf16[512,256]{1,0:T(8,128)(2,1)} %refs_0_.1), channel_id=1, source_target_pairs={{0,4},{1,5},{2,6},{3,7},{4,8},{5,9},{6,10},{7,11},{8,12},{9,13},{1... | collective-permute-start | bytes 786440 | tf_op jit(solution)/shard_map/gather_sketch/ppermute | solution.py:25
  11.4 14.5 %copy-start = (bf16[512,256]{1,0:T(8,128)(2,1)}, bf16[512,256]{1,0:T(8,128)(2,1)S(1)}, u32[]{:S(2)}) copy-start(bf16[512,256]{1,0:T(8,128)(2,1)S(1)} %collective-permute-done.2.refs_4_) | copy-start | bytes 786436
  11.4 7.7 %collective-permute-start.4 = (bf16[256,256]{1,0:T(8,128)(2,1)S(1)}, bf16[256,256]{1,0:T(8,128)(2,1)S(1)}, u32[]{:S(2)}, u32[]{:S(2)}) collective-permute-start(bf16[256,256]{1,0:T(8,128)(2,1)S(1)} %get-tuple-element.68), channel_id=1, source_target_pairs={{0,18},{1,19},{2,0},{3,1},{4,22},{5,23},{6,4},{7,5},{8,26},{9,27},... | collective-permute-start | bytes 393224 | tf_op jit(solution)/shard_map/gather_sketch/ppermute | solution.py:25
  14.2 5.3 %collective-permute-start.3 = (bf16[256,256]{1,0:T(8,128)(2,1)S(1)}, bf16[256,256]{1,0:T(8,128)(2,1)S(1)}, u32[]{:S(2)}, u32[]{:S(2)}) collective-permute-start(bf16[256,256]{1,0:T(8,128)(2,1)S(1)} %get-tuple-element.69), channel_id=1, source_target_pairs={{0,2},{1,3},{2,16},{3,17},{4,6},{5,7},{6,20},{7,21},{8,10},{9,11},... | collective-permute-start | bytes 393224 | tf_op jit(solution)/shard_map/gather_sketch/ppermute | solution.py:25
  14.2 11.6 %copy-start.3 = (bf16[512,256]{1,0:T(8,128)(2,1)}, bf16[512,256]{1,0:T(8,128)(2,1)S(1)}, u32[]{:S(2)}) copy-start(bf16[512,256]{1,0:T(8,128)(2,1)S(1)} %collective-permute-done.7.refs_3_) | copy-start | bytes 786436
  14.2 8.6 %collective-permute-start.8 = (bf16[512,256]{1,0:T(8,128)(2,1)}, bf16[512,256]{1,0:T(8,128)(2,1)S(1)}, u32[]{:S(2)}, u32[]{:S(2)}) collective-permute-start(bf16[512,256]{1,0:T(8,128)(2,1)} %refs_0_.1), channel_id=1, source_target_pairs={{0,1},{1,0},{2,3},{3,2},{4,5},{5,4},{6,7},{7,6},{8,9},{9,8},{10,11... | collective-permute-start | bytes 786440 | tf_op jit(solution)/shard_map/gather_sketch/ppermute | solution.py:25
  17.6 8.3 %copy-start.2 = (bf16[512,256]{1,0:T(8,128)(2,1)}, bf16[512,256]{1,0:T(8,128)(2,1)S(1)}, u32[]{:S(2)}) copy-start(bf16[512,256]{1,0:T(8,128)(2,1)S(1)} %collective-permute-done.1.refs_2_) | copy-start | bytes 786436
  17.6 5.5 %collective-permute-start.12 = (bf16[512,256]{1,0:T(8,128)(2,1)S(1)}, bf16[512,256]{1,0:T(8,128)(2,1)S(1)}, u32[]{:S(2)}, u32[]{:S(2)}) collective-permute-start(bf16[512,256]{1,0:T(8,128)(2,1)S(1)} %collective-permute-done.2.refs_4_), channel_id=1, source_target_pairs={{0,1},{1,0},{2,3},{3,2},{4,5},{5,4},{6,7},{7,6},{8,9},{9,8},{10,11... | collective-permute-start | bytes 786440 | tf_op jit(solution)/shard_map/gather_sketch/ppermute | solution.py:25
  19.0 6.9 %copy-start.4 = (bf16[512,256]{1,0:T(8,128)(2,1)}, bf16[512,256]{1,0:T(8,128)(2,1)S(1)}, u32[]{:S(2)}) copy-start(bf16[512,256]{1,0:T(8,128)(2,1)S(1)} %collective-permute-done.refs_1_) | copy-start | bytes 786436
  19.0 3.9 %collective-permute-start.11 = (bf16[512,256]{1,0:T(8,128)(2,1)S(1)}, bf16[512,256]{1,0:T(8,128)(2,1)S(1)}, u32[]{:S(2)}, u32[]{:S(2)}) collective-permute-start(bf16[512,256]{1,0:T(8,128)(2,1)S(1)} %collective-permute-done.7.refs_3_), channel_id=1, source_target_pairs={{0,1},{1,0},{2,3},{3,2},{4,5},{5,4},{6,7},{7,6},{8,9},{9,8},{10,11... | collective-permute-start | bytes 786440 | tf_op jit(solution)/shard_map/gather_sketch/ppermute | solution.py:25
  19.1 6.7 %collective-permute-start.10 = (bf16[512,256]{1,0:T(8,128)(2,1)S(1)}, bf16[512,256]{1,0:T(8,128)(2,1)S(1)}, u32[]{:S(2)}, u32[]{:S(2)}) collective-permute-start(bf16[512,256]{1,0:T(8,128)(2,1)S(1)} %collective-permute-done.1.refs_2_), channel_id=1, source_target_pairs={{0,1},{1,0},{2,3},{3,2},{4,5},{5,4},{6,7},{7,6},{8,9},{9,8},{10,11... | collective-permute-start | bytes 786440 | tf_op jit(solution)/shard_map/gather_sketch/ppermute | solution.py:25
  19.5 6.3 %collective-permute-start.9 = (bf16[512,256]{1,0:T(8,128)(2,1)S(1)}, bf16[512,256]{1,0:T(8,128)(2,1)S(1)}, u32[]{:S(2)}, u32[]{:S(2)}) collective-permute-start(bf16[512,256]{1,0:T(8,128)(2,1)S(1)} %collective-permute-done.refs_1_), channel_id=1, source_target_pairs={{0,1},{1,0},{2,3},{3,2},{4,5},{5,4},{6,7},{7,6},{8,9},{9,8},{10,11... | collective-permute-start | bytes 786440 | tf_op jit(solution)/shard_map/gather_sketch/ppermute | solution.py:25
  22.8 3.1 %copy-start.1 = (bf16[512,256]{1,0:T(8,128)(2,1)}, bf16[512,256]{1,0:T(8,128)(2,1)S(1)}, u32[]{:S(2)}) copy-start(bf16[512,256]{1,0:T(8,128)(2,1)S(1)} %constant_dynamic-update-slice_fusion.refs_5_) | copy-start | bytes 786436
  22.8 3.1 %copy-start.5 = (bf16[512,256]{1,0:T(8,128)(2,1)}, bf16[512,256]{1,0:T(8,128)(2,1)S(1)}, u32[]{:S(2)}) copy-start(bf16[512,256]{1,0:T(8,128)(2,1)S(1)} %collective-permute-done.8.refs_6_) | copy-start | bytes 786436
  22.8 3.0 %collective-permute-start.13 = (bf16[512,256]{1,0:T(8,128)(2,1)S(1)}, bf16[512,256]{1,0:T(8,128)(2,1)S(1)}, u32[]{:S(2)}, u32[]{:S(2)}) collective-permute-start(bf16[512,256]{1,0:T(8,128)(2,1)S(1)} %constant_dynamic-update-slice_fusion.refs_5_), channel_id=1, source_target_pairs={{0,1},{1,0},{2,3},{3,2},{4,5},{5,4},{6,7},{7,6},{8,9},{9,8},{10,11... | collective-permute-start | bytes 786440 | tf_op jit(solution)/shard_map/gather_sketch/ppermute | solution.py:25
  22.9 3.0 %copy-start.7 = (bf16[512,256]{1,0:T(8,128)(2,1)}, bf16[512,256]{1,0:T(8,128)(2,1)S(1)}, u32[]{:S(2)}) copy-start(bf16[512,256]{1,0:T(8,128)(2,1)S(1)} %collective-permute-done.11.refs_9_) | copy-start | bytes 786436
  22.9 9.5 %collective-permute-start.5 = (bf16[512,256]{1,0:T(8,128)(2,1)S(1)}, bf16[512,256]{1,0:T(8,128)(2,1)S(1)}, u32[]{:S(2)}, u32[]{:S(2)}) collective-permute-start(bf16[512,256]{1,0:T(8,128)(2,1)S(1)} %collective-permute-done.refs_1_), channel_id=1, source_target_pairs={{0,2},{1,3},{2,16},{3,17},{4,6},{5,7},{6,20},{7,21},{8,10},{9,11},... | collective-permute-start | bytes 786440 | tf_op jit(solution)/shard_map/gather_sketch/ppermute | solution.py:25
  23.0 2.9 %copy-start.6 = (bf16[512,256]{1,0:T(8,128)(2,1)}, bf16[512,256]{1,0:T(8,128)(2,1)S(1)}, u32[]{:S(2)}) copy-start(bf16[512,256]{1,0:T(8,128)(2,1)S(1)} %collective-permute-done.12.refs_10_) | copy-start | bytes 786436
  23.0 9.4 %collective-permute-start.6 = (bf16[512,256]{1,0:T(8,128)(2,1)S(1)}, bf16[512,256]{1,0:T(8,128)(2,1)S(1)}, u32[]{:S(2)}, u32[]{:S(2)}) collective-permute-start(bf16[512,256]{1,0:T(8,128)(2,1)S(1)} %collective-permute-done.1.refs_2_), channel_id=1, source_target_pairs={{0,18},{1,19},{2,0},{3,1},{4,22},{5,23},{6,4},{7,5},{8,26},{9,27},... | collective-permute-start | bytes 786440 | tf_op jit(solution)/shard_map/gather_sketch/ppermute | solution.py:25
  25.8 0.7 copy-start.8
  25.8 0.8 copy-start.9
  25.8 0.9 copy-start.10
  32.5 2.2 %collective-permute-start.14 = (bf16[512,256]{1,0:T(8,128)(2,1)S(1)}, bf16[512,256]{1,0:T(8,128)(2,1)S(1)}, u32[]{:S(2)}, u32[]{:S(2)}) collective-permute-start(bf16[512,256]{1,0:T(8,128)(2,1)S(1)} %collective-permute-done.5.refs_0_), channel_id=1, source_target_pairs={{0,1},{1,0},{2,3},{3,2},{4,5},{5,4},{6,7},{7,6},{8,9},{9,8},{10,11... | collective-permute-start | bytes 786440 | tf_op jit(solution)/shard_map/gather_sketch/ppermute | solution.py:25
  33.5 1.5 %collective-permute-start.15 = (bf16[512,256]{1,0:T(8,128)(2,1)S(1)}, bf16[512,256]{1,0:T(8,128)(2,1)S(1)}, u32[]{:S(2)}, u32[]{:S(2)}) collective-permute-start(bf16[512,256]{1,0:T(8,128)(2,1)S(1)} %collective-permute-done.6.refs_1_), channel_id=1, source_target_pairs={{0,1},{1,0},{2,3},{3,2},{4,5},{5,4},{6,7},{7,6},{8,9},{9,8},{10,11... | collective-permute-start | bytes 786440 | tf_op jit(solution)/shard_map/gather_sketch/ppermute | solution.py:25
  39.0 1.4 collective-permute-start.16
  40.4 5.5 %collective-permute-start.17 = (f32[192,128]{1,0:T(8,128)S(1)}, f32[192,128]{1,0:T(8,128)S(1)}, u32[]{:S(2)}, u32[]{:S(2)}) collective-permute-start(f32[192,128]{1,0:T(8,128)S(1)} %add.165), channel_id=1, source_target_pairs={{0,2},{1,3},{2,0},{3,1},{4,6},{5,7},{6,4},{7,5},{8,10},{9,11},{10,... | collective-permute-start | bytes 294920 | tf_op jit(solution)/shard_map/sum_gram/ppermute | solution.py:25
  45.9 5.0 %collective-permute-start.18 = (bf16[8,256,512]{2,1,0:T(8,128)(2,1)S(1)}, bf16[8,256,512]{2,1,0:T(8,128)(2,1)S(1)}, u32[]{:S(2)}, u32[]{:S(2)}) collective-permute-start(bf16[8,256,512]{2,1,0:T(8,128)(2,1)S(1)} %get-tuple-element.50), channel_id=1, source_target_pairs={{0,1},{1,0},{2,3},{3,2},{4,5},{5,4},{6,7},{7,6},{8,9},{9,8},{10,11... | collective-permute-start | bytes 6291464 | tf_op jit(solution)/shard_map/sum_cores/ppermute | solution.py:25
  46.3 4.5 %collective-permute-start.19 = (f32[192,128]{1,0:T(8,128)S(1)}, f32[192,128]{1,0:T(8,128)S(1)}, u32[]{:S(2)}, u32[]{:S(2)}) collective-permute-start(f32[192,128]{1,0:T(8,128)S(1)} %add.166), channel_id=1, source_target_pairs={{0,4},{1,5},{2,6},{3,7},{4,0},{5,1},{6,2},{7,3},{8,12},{9,13},{10,... | collective-permute-start | bytes 294920 | tf_op jit(solution)/shard_map/sum_gram/ppermute | solution.py:25
  50.8 5.5 %collective-permute-start.20 = (f32[192,128]{1,0:T(8,128)S(1)}, f32[192,128]{1,0:T(8,128)S(1)}, u32[]{:S(2)}, u32[]{:S(2)}) collective-permute-start(f32[192,128]{1,0:T(8,128)S(1)} %add.167), channel_id=1, source_target_pairs={{0,12},{1,13},{2,14},{3,15},{4,8},{5,9},{6,10},{7,11},{8,4},{9,5},... | collective-permute-start | bytes 294920 | tf_op jit(solution)/shard_map/sum_gram/ppermute | solution.py:25
  56.4 34.9 %all-to-all-start = ((bf16[8,256,512]{2,1,0:T(8,128)(2,1)}), bf16[8,256,512]{2,1,0:T(8,128)(2,1)S(1)}, u32[]{:S(2)}, u32[]{:S(2)}) async-start(bf16[8,256,512]{2,1,0:T(8,128)(2,1)} %add_convert_fusion), calls=%async_computation | async-start | bytes 4194304 | tf_op jit(solution)/shard_map/sum_fsdp/all_to_all | solution.py:367
  61.9 3.2 %collective-permute-start.21 = (f32[192,128]{1,0:T(8,128)S(1)}, f32[192,128]{1,0:T(8,128)S(1)}, u32[]{:S(2)}, u32[]{:S(2)}) collective-permute-start(f32[192,128]{1,0:T(8,128)S(1)} %add.169.mine), channel_id=1, source_target_pairs={{0,1},{1,0},{2,3},{3,2},{4,5},{5,4},{6,7},{7,6},{8,9},{9,8},{10,11... | collective-permute-start | bytes 294920 | tf_op jit(solution)/shard_map/sum_gram/ppermute | solution.py:25
  77.2 14.0 %collective-permute-start.22 = (bf16[512,256]{1,0:T(8,128)(2,1)S(1)}, bf16[512,256]{1,0:T(8,128)(2,1)S(1)}, u32[]{:S(2)}, u32[]{:S(2)}) collective-permute-start(bf16[512,256]{1,0:T(8,128)(2,1)S(1)} %basis.1), channel_id=1, source_target_pairs={{0,16},{1,17},{2,18},{3,19},{4,20},{5,21},{6,22},{7,23},{8,24},{9,... | collective-permute-start | bytes 786440 | tf_op jit(solution)/shard_map/gather_basis/ppermute | solution.py:25
  92.8 12.8 %collective-permute-start.23 = (bf16[256,128]{1,0:T(8,128)(2,1)S(1)}, bf16[256,128]{1,0:T(8,128)(2,1)S(1)}, u32[]{:S(2)}, u32[]{:S(2)}) collective-permute-start(bf16[256,128]{1,0:T(8,128)(2,1)S(1)} %get-tuple-element.61), channel_id=1, source_target_pairs={{0,0},{1,16},{2,2},{3,18},{4,4},{5,20},{6,6},{7,22},{8,8},{9,24},{... | collective-permute-start | bytes 196616 | tf_op jit(solution)/shard_map/exchange_coef/ppermute | solution.py:25
  98.3 7.4 %collective-permute-start.24 = (bf16[256,128]{1,0:T(8,128)(2,1)S(1)}, bf16[256,128]{1,0:T(8,128)(2,1)S(1)}, u32[]{:S(2)}, u32[]{:S(2)}) collective-permute-start(bf16[256,128]{1,0:T(8,128)(2,1)S(1)} %get-tuple-element.62), channel_id=1, source_target_pairs={{0,32},{1,48},{2,34},{3,50},{4,36},{5,52},{6,38},{7,54},{8,40},{9,... | collective-permute-start | bytes 196616 | tf_op jit(solution)/shard_map/exchange_coef/ppermute | solution.py:25
  99.3 8.1 %collective-permute-start.25 = (bf16[256,128]{1,0:T(8,128)(2,1)S(1)}, bf16[256,128]{1,0:T(8,128)(2,1)S(1)}, u32[]{:S(2)}, u32[]{:S(2)}) collective-permute-start(bf16[256,128]{1,0:T(8,128)(2,1)S(1)} %get-tuple-element.63), channel_id=1, source_target_pairs={{0,64},{1,80},{2,66},{3,82},{4,68},{5,84},{6,70},{7,86},{8,72},{9,... | collective-permute-start | bytes 196616 | tf_op jit(solution)/shard_map/exchange_coef/ppermute | solution.py:25
  104.7 6.7 %collective-permute-start.26 = (bf16[256,128]{1,0:T(8,128)(2,1)S(1)}, bf16[256,128]{1,0:T(8,128)(2,1)S(1)}, u32[]{:S(2)}, u32[]{:S(2)}) collective-permute-start(bf16[256,128]{1,0:T(8,128)(2,1)S(1)} %get-tuple-element.64), channel_id=1, source_target_pairs={{0,96},{1,112},{2,98},{3,114},{4,100},{5,116},{6,102},{7,118},{8,1... | collective-permute-start | bytes 196616 | tf_op jit(solution)/shard_map/exchange_coef/ppermute | solution.py:25
  113.0 26.0 %all-to-all-start.1 = ((bf16[8,1024,128]{2,1,0:T(8,128)(2,1)}), bf16[8,1024,128]{2,1,0:T(8,128)(2,1)}, u32[]{:S(2)}, u32[]{:S(2)}) async-start(bf16[8,1024,128]{2,1,0:T(8,128)(2,1)} %spread.1), calls=%async_computation.1 | async-start | bytes 4194304 | tf_op jit(solution)/shard_map/gather_coef/all_to_all | solution.py:401
  118.1 11.0 %collective-permute-start.29 = (bf16[2,512,256]{2,1,0:T(8,128)(2,1)S(1)}, bf16[2,512,256]{2,1,0:T(8,128)(2,1)S(1)}, u32[]{:S(2)}, u32[]{:S(2)}) collective-permute-start(bf16[2,512,256]{2,1,0:T(8,128)(2,1)S(1)} %pad_maximum_fusion.q0), channel_id=1, source_target_pairs={{0,96},{1,97},{2,98},{3,99},{4,100},{5,101},{6,102},{7,103},{8,104... | collective-permute-start | bytes 1572872 | tf_op jit(solution)/shard_map/gather_basis/ppermute | solution.py:25
  119.9 10.7 %collective-permute-start.27 = (bf16[2,512,256]{2,1,0:T(8,128)(2,1)S(1)}, bf16[2,512,256]{2,1,0:T(8,128)(2,1)S(1)}, u32[]{:S(2)}, u32[]{:S(2)}) collective-permute-start(bf16[2,512,256]{2,1,0:T(8,128)(2,1)S(1)} %pad_maximum_fusion.q0), channel_id=1, source_target_pairs={{0,32},{1,33},{2,34},{3,35},{4,36},{5,37},{6,38},{7,39},{8,40},{9,... | collective-permute-start | bytes 1572872 | tf_op jit(solution)/shard_map/gather_basis/ppermute | solution.py:25
  129.1 5.3 %collective-permute-start.30 = (bf16[512,256]{1,0:T(8,128)(2,1)S(1)}, bf16[512,256]{1,0:T(8,128)(2,1)S(1)}, u32[]{:S(2)}, u32[]{:S(2)}) collective-permute-start(bf16[512,256]{1,0:T(8,128)(2,1)S(1)} %slice_bitcast_fusion), channel_id=1, source_target_pairs={{0,96},{1,97},{2,98},{3,99},{4,100},{5,101},{6,102},{7,103},{8,104... | collective-permute-start | bytes 786440 | tf_op jit(solution)/shard_map/gather_basis/ppermute | solution.py:25
  130.7 6.5 %collective-permute-start.28 = (bf16[512,256]{1,0:T(8,128)(2,1)S(1)}, bf16[512,256]{1,0:T(8,128)(2,1)S(1)}, u32[]{:S(2)}, u32[]{:S(2)}) collective-permute-start(bf16[512,256]{1,0:T(8,128)(2,1)S(1)} %slice_bitcast_fusion.1), channel_id=1, source_target_pairs={{0,32},{1,33},{2,34},{3,35},{4,36},{5,37},{6,38},{7,39},{8,40},{9,... | collective-permute-start | bytes 786440 | tf_op jit(solution)/shard_map/gather_basis/ppermute | solution.py:25
  139.0 4.4 %collective-permute-start.31 = (bf16[8,1024,128]{2,1,0:T(8,128)(2,1)}, bf16[8,1024,128]{2,1,0:T(8,128)(2,1)S(1)}, u32[]{:S(2)}, u32[]{:S(2)}) collective-permute-start(bf16[8,1024,128]{2,1,0:T(8,128)(2,1)} %all-to-all-done.1.mine), channel_id=1, source_target_pairs={{0,1},{1,0},{2,3},{3,2},{4,5},{5,4},{6,7},{7,6},{8,9},{9,8},{10,11... | collective-permute-start | bytes 6291464 | tf_op jit(solution)/shard_map/gather_coef/ppermute | solution.py:25

commit v3 on v2

--- a/solution.py
+++ b/solution.py
@@ -40,17 +40,11 @@
 SMEM = pl.BlockSpec(memory_space=pltpu.SMEM)
 
 
-def call(kernel, outs, flops, name, smem=True, scratch=(), vmem=16, far=()):
+def call(kernel, outs, flops, name, smem=True, scratch=(), vmem=16):
     def run(*args):
-        args = [
-            pltpu.with_memory_space_constraint(a, pltpu.HBM) if n in far else a
-            for n, a in enumerate(args)
-        ]
         return pl.pallas_call(
             kernel,
-            in_specs=[
-                SMEM if smem and n == 0 else FAR if n in far else VMEM for n in range(len(args))
-            ],
+            in_specs=[SMEM] * smem + [VMEM] * (len(args) - smem),
             out_specs=[VMEM] * len(outs),
             out_shape=[jax.ShapeDtypeStruct(*o) if isinstance(o, tuple) else o for o in outs],
             scratch_shapes=list(scratch),
@@ -68,29 +62,11 @@
     return ref.at[:, pl.ds(pl.multiple_of(start, count), count)]
 
 
-def fetch(delta, starts, held, sems, pieces=(), near=None):
-    copies = []
-    for n, start in enumerate(starts):
-        pairs = [(columns(delta, start, held.shape[2]), held.at[n])]
-        if pieces:
-            pairs.append((pieces[n], near.at[n]))
-        copies.append(
-            [pltpu.make_async_copy(a, b, sems.at[m, n]) for m, (a, b) in enumerate(pairs)]
+def add_products(layout, place, delta, pieces, out):
+    for n, (piece, at) in enumerate(zip(pieces, layout)):
+        value = jnp.dot(
+            columns(delta, place[at], piece.shape[0])[...], piece[...], preferred_element_type=F32
         )
-        for copy in copies[-1]:
-            copy.start()
-    return copies
-
-
-def wait(copies):
-    for copy in copies:
-        copy.wait()
-
-
-def add_products(copies, out, held, near):
-    for n, pair in enumerate(copies):
-        wait(pair)
-        value = jnp.dot(held[n], near[n][...], preferred_element_type=F32)
         if n == 0:
             out[...] = value
         else:
@@ -98,16 +74,13 @@
 
 
 def early_kernel(layout, place, delta, *refs):
-    pieces, (out, held, near, sems) = refs[: len(layout)], refs[len(layout) :]
-    copies = fetch(delta, [place[at] for at in layout], held, sems, pieces, near)
-    add_products(copies, out, held, [near.at[n] for n in range(len(layout))])
+    add_products(layout, place, delta, refs[: len(layout)], refs[-1])
 
 
 def late_kernel(layout, place, delta, *refs):
     pieces, part = refs[: len(layout)], refs[len(layout)]
-    mine, theirs, sketched, turned, out, held, sems = refs[len(layout) + 1 :]
-    copies = fetch(delta, [place[at] for at in layout], held, sems)
-    add_products(copies, out, held, pieces)
+    mine, theirs, sketched, turned, out = refs[len(layout) + 1 :]
+    add_products(layout, place, delta, pieces, out)
     total = out[...] + part[...]
     flipped = total.T
     gram = jnp.dot(flipped, total, precision=HIGH, preferred_element_type=F32)
@@ -123,22 +96,17 @@
                 to[n][BLK:] = gram[BLK + at // 2 : BLK + at // 2 + BLK // 2, :BLK]
 
 
-def product_kernel(place, delta, turned, sent, kept, held, sems):
-    width = held.shape[2]
-    blocks = [
-        (out, parity, g)
-        for out, parity in ((sent, 1 - place[0]), (kept, place[0]))
-        for g in range(4)
-    ]
-    copies = fetch(delta, [(2 * g + parity) * width for _, parity, g in blocks], held, sems)
-    for n, ((out, _, g), pair) in enumerate(zip(blocks, copies)):
-        wait(pair)
-        for q in range(2):
-            tile = jnp.dot(
-                turned[...], held[n, :, q * 512 : (q + 1) * 512], preferred_element_type=F32
-            ).astype(BF16)
-            for u in range(4):
-                out[4 * q + u, :, g * BLK : (g + 1) * BLK] = tile[:, u * BLK : (u + 1) * BLK]
+def product_kernel(place, delta, turned, sent, kept):
+    for out, parity in ((sent, 1 - place[0]), (kept, place[0])):
+        for g in range(4):
+            for q in range(2):
+                tile = jnp.dot(
+                    turned[...],
+                    columns(delta, (2 * g + parity) * 1024 + q * 512, 512)[...],
+                    preferred_element_type=F32,
+                ).astype(BF16)
+                for u in range(4):
+                    out[4 * q + u, :, g * BLK : (g + 1) * BLK] = tile[:, u * BLK : (u + 1) * BLK]
 
 
 def spread_kernel(t0, t1, t2, t3, out):
@@ -294,11 +262,6 @@
         (2 * (2 * (n % 4) + 1 - yl) + c) * depth for c in (core, 1 - core) for n in (z - 1, z + 1)
     ]
     place = jnp.stack([core, 0, x, (core + yh) % 2] + starts).astype(jnp.int32)
-    fetched = lambda count: [
-        pltpu.VMEM((count, rows, depth), BF16),
-        pltpu.VMEM((count, depth, rank), BF16),
-        pltpu.SemaphoreType.DMA((2, count)),
-    ]
     mid = depth // 2
     with jax.named_scope("gather_sketch"):
         z2 = shift(sketch, dz=2)
@@ -314,8 +277,6 @@
         [((rows, rank), F32)],
         1.6e9,
         "sketched_early",
-        scratch=fetched(12),
-        far=range(1, 14),
     )(place, local, *pieces)[0]
     y1, y3, part = fence((y1, y3, part))
     with jax.named_scope("gather_sketch"):
@@ -327,12 +288,7 @@
         [gram_part, gram_part, ((rows, rank), F32), ((rank, rows), BF16)],
         8e8,
         "sketched_late",
-        scratch=[
-            pltpu.VMEM((rows, rank), F32),
-            pltpu.VMEM((4, rows, depth), BF16),
-            pltpu.SemaphoreType.DMA((1, 4)),
-        ],
-        far=(1,),
+        scratch=[pltpu.VMEM((rows, rank), F32)],
     )(place, local, *pieces, part)
 
     with jax.named_scope("sum_gram"):
@@ -345,23 +301,16 @@
         [shares] * 2,
         2.2e9,
         "product",
-        vmem=24,
-        scratch=[pltpu.VMEM((8, rows, 1024), BF16), pltpu.SemaphoreType.DMA((1, 8))],
-        far=(1,),
+        vmem=20,
     )(place, local, turned)
     got, sent, kept = fence((got, sent, kept))
     with jax.named_scope("sum_gram"):
         mine = mine + got
-        got = move(mine, lambda x, h, z, l, c: (x, h, z ^ 1, l, c))
+        got = [shift(mine, dz=d) for d in (2, 1, 3)]
     with jax.named_scope("sum_cores"):
-        other = shift(sent, dc=1)
-    kept, other, mine = fence((kept, other, mine + got))
-    with jax.named_scope("sum_cores"):
-        kept = (kept.astype(F32) + other.astype(F32)).astype(BF16)
-    with jax.named_scope("sum_gram"):
-        got = move(mine, lambda x, h, z, l, c: (x, h, 3 - z, l, c))
-        got, kept = fence((got, kept))
-        mine = mine + got
+        kept = (kept.astype(F32) + shift(sent, dc=1).astype(F32)).astype(BF16)
+    *got, kept = fence((*got, kept))
+    mine = (mine + got[0]) + (got[1] + got[2])
     mine, kept = fence((mine, kept))
     with jax.named_scope("sum_fsdp"):
         parts = lax.all_to_all(kept, ("z", "yl"), 0, 0, tiled=True)
@@ -377,14 +326,7 @@
     )(place, mine, theirs)[0]
     basis = call(basis_kernel, [((rows, rank), BF16)], 4e8, "basis", False)(sketched, inverse)[0]
     with jax.named_scope("gather_basis"):
-        both = jnp.stack([basis, shift(basis, dh=1)])
-    parts, both = fence((parts, both))
-    with jax.named_scope("gather_basis"):
-        right, left = shift(both, dx=1), shift(both, dx=-1)
-        far = jnp.stack([shift(right[0], dx=1), shift(left[1], dx=-1)])
-    operand = call(lay_kernel, [((rows, 8 * rank), BF16)], 1e8, "lay")(
-        place, both, right, far, left
-    )[0]
+        across = shift(basis, dh=1)
     tiles = call(
         coef_kernel,
         [((rank, BLK), BF16)] * 4,
@@ -392,6 +334,14 @@
         "coef",
         scratch=[pltpu.VMEM((rank, 4 * BLK), BF16)],
     )(place, inverse, parts)
+    *tiles, across = fence((*tiles, across))
+    both = jnp.stack([basis, across])
+    with jax.named_scope("gather_basis"):
+        right, left = shift(both, dx=1), shift(both, dx=-1)
+        far = jnp.stack([shift(right[0], dx=1), shift(left[1], dx=-1)])
+    operand = call(lay_kernel, [((rows, 8 * rank), BF16)], 1e8, "lay")(
+        place, both, right, far, left
+    )[0]
     with jax.named_scope("exchange_coef"):
         tiles = [
             move(v, lambda x, h, z, l, c, d=d: (x + d, c, z, l, h)) for d, v in enumerate(tiles)

time: 149 us -> 146 us (0.980)
  Pallas kernels: 39.5 us -> 32.2 us
  local copies, waits for them, and re-layouts: 0.97 us -> 4.5 us
    all_to_all x1, waiting for transfers between devices: 0.01 us -> 10.1 us  [body(): parts = lax.all_to_all(kept, ('z', 'yl'), 0, 0, tiled=True)]
    ppermute x32 -> x33, waiting for transfers between devices: 45.2 us -> 36.9 us  [move(): return lax.ppermute(value, AXES, pairs)]
    pallas_call x9, Pallas kernels: 33.9 us -> 26.7 us  [run(): pl.pallas_call(kernel, in_specs=[SMEM] * smem + [VMEM] * (len(args) - sme...]
    unnamed x23 -> x7, local copies, waits for them, and re-layouts: 0.82 us -> 4.34 us
    all_to_all x1, starting transfers between devices: 5.56 us -> 3.62 us  [body(): parts = lax.all_to_all(kept, ('z', 'yl'), 0, 0, tiled=True)]
    ppermute x32 -> x33, starting transfers between devices: 48.6 us -> 48.8 us  [move(): return lax.ppermute(value, AXES, pairs)]
  transfers between devices with their start and end apart: 34 -> 35, of which waited for: 16 -> 17; matrix products, arithmetic and copies ran while one was open for 2% -> 2% of each run, Pallas kernels for 18% -> 16%
where the time goes in v3:
time: 146 us; the launch traced here: 145 us
  starting transfers between devices  57.9 us (40%)
  waiting for transfers between devices  47.3 us (32%)
  Pallas kernels  32.2 us (22%)
  local copies, waits for them, and re-layouts  4.5 us (3%)
  other arithmetic  2.11 us (1%)
    ppermute x33, starting transfers between devices, move(): return lax.ppermute(value, AXES, pairs)  48.8 us
    ppermute x33, waiting for transfers between devices, move(): return lax.ppermute(value, AXES, pairs)  36.9 us
    pallas_call x9, Pallas kernels, run(): pl.pallas_call(kernel, in_specs=[SMEM] * smem + [VMEM] * (len(args) - sme...  26.7 us
    all_to_all x1, waiting for transfers between devices, body(): parts = lax.all_to_all(kept, ('z', 'yl'), 0, 0, tiled=True)  10.1 us
    pallas_call x1, Pallas kernels, update_call(): pl.pallas_call(update_kernel, grid=(4,), in_specs=[tile, tile, tile, pl.B...  5.58 us
    all_to_all x1, starting transfers between devices, body(): lax.all_to_all(tiles, ('z', 'yl'), 0, 0, tiled=True)  5.51 us
    unnamed x7, local copies, waits for them, and re-layouts  4.34 us
    all_to_all x1, starting transfers between devices, body(): parts = lax.all_to_all(kept, ('z', 'yl'), 0, 0, tiled=True)  3.62 us
  transfers between devices with their start and end apart: 35, of which 17 were waited for; matrix products, arithmetic and copies ran while one was open for 2% of the time, Pallas kernels for 16%

profile of v3, /device:TPU:1, one launch (start us, length us, event | category | flops | bytes accessed | tf_op | source)
XLA Modules:
  0.0 144.9 jit_solution(8923587704648724973)
XLA Ops:
  0.6 4.5 %collective-permute-start.2 = (bf16[512,256]{1,0:T(8,128)(2,1)}, bf16[512,256]{1,0:T(8,128)(2,1)S(1)}, u32[]{:S(2)}, u32[]{:S(2)}) collective-permute-start(bf16[512,256]{1,0:T(8,128)(2,1)} %refs_0_.1), channel_id=1, source_target_pairs={{0,8},{1,9},{2,10},{3,11},{4,12},{5,13},{6,14},{7,15},{8,0},{9,1},... | collective-permute-start | bytes 786440 | tf_op jit(solution)/shard_map/gather_sketch/ppermute | solution.py:25
  5.1 1.3 collective-permute-start.7
  6.9 1.0 collective-permute-start
  7.9 3.5 %collective-permute-done.2.refs_4_ = bf16[512,256]{1,0:T(8,128)(2,1)S(1)} collective-permute-done((bf16[512,256]{1,0:T(8,128)(2,1)}, bf16[512,256]{1,0:T(8,128)(2,1)S(1)}, u32[]{:S(2)}, u32[]{:S(2)}) %collective-permute-start.2) | collective-permute-done | bytes 262176 | tf_op jit(solution)/shard_map/gather_sketch/ppermute | solution.py:25
  11.4 2.8 %collective-permute-start.4 = (bf16[256,256]{1,0:T(8,128)(2,1)S(1)}, bf16[256,256]{1,0:T(8,128)(2,1)S(1)}, u32[]{:S(2)}, u32[]{:S(2)}) collective-permute-start(bf16[256,256]{1,0:T(8,128)(2,1)S(1)} %get-tuple-element.72), channel_id=1, source_target_pairs={{0,18},{1,19},{2,0},{3,1},{4,22},{5,23},{6,4},{7,5},{8,26},{9,27},... | collective-permute-start | bytes 393224 | tf_op jit(solution)/shard_map/gather_sketch/ppermute | solution.py:25
  14.2 2.3 %collective-permute-start.8 = (bf16[512,256]{1,0:T(8,128)(2,1)}, bf16[512,256]{1,0:T(8,128)(2,1)S(1)}, u32[]{:S(2)}, u32[]{:S(2)}) collective-permute-start(bf16[512,256]{1,0:T(8,128)(2,1)} %refs_0_.1), channel_id=1, source_target_pairs={{0,1},{1,0},{2,3},{3,2},{4,5},{5,4},{6,7},{7,6},{8,9},{9,8},{10,11... | collective-permute-start | bytes 786440 | tf_op jit(solution)/shard_map/gather_sketch/ppermute | solution.py:25
  16.6 1.0 collective-permute-done.1.refs_2_
  17.6 1.4 %collective-permute-start.12 = (bf16[512,256]{1,0:T(8,128)(2,1)S(1)}, bf16[512,256]{1,0:T(8,128)(2,1)S(1)}, u32[]{:S(2)}, u32[]{:S(2)}) collective-permute-start(bf16[512,256]{1,0:T(8,128)(2,1)S(1)} %collective-permute-done.2.refs_4_), channel_id=1, source_target_pairs={{0,1},{1,0},{2,3},{3,2},{4,5},{5,4},{6,7},{7,6},{8,9},{9,8},{10,11... | collective-permute-start | bytes 786440 | tf_op jit(solution)/shard_map/gather_sketch/ppermute | solution.py:25
  19.5 3.2 %collective-permute-start.9 = (bf16[512,256]{1,0:T(8,128)(2,1)S(1)}, bf16[512,256]{1,0:T(8,128)(2,1)S(1)}, u32[]{:S(2)}, u32[]{:S(2)}) collective-permute-start(bf16[512,256]{1,0:T(8,128)(2,1)S(1)} %collective-permute-done.refs_1_), channel_id=1, source_target_pairs={{0,1},{1,0},{2,3},{3,2},{4,5},{5,4},{6,7},{7,6},{8,9},{9,8},{10,11... | collective-permute-start | bytes 786440 | tf_op jit(solution)/shard_map/gather_sketch/ppermute | solution.py:25
  23.0 2.7 %collective-permute-start.6 = (bf16[512,256]{1,0:T(8,128)(2,1)S(1)}, bf16[512,256]{1,0:T(8,128)(2,1)S(1)}, u32[]{:S(2)}, u32[]{:S(2)}) collective-permute-start(bf16[512,256]{1,0:T(8,128)(2,1)S(1)} %collective-permute-done.1.refs_2_), channel_id=1, source_target_pairs={{0,18},{1,19},{2,0},{3,1},{4,22},{5,23},{6,4},{7,5},{8,26},{9,27},... | collective-permute-start | bytes 786440 | tf_op jit(solution)/shard_map/gather_sketch/ppermute | solution.py:25
  25.8 3.4 %copy-done = bf16[1,512,8192]{2,1,0:T(8,128)(2,1)S(1)} copy-done((bf16[1,512,8192]{2,1,0:T(8,128)(2,1)S(1)}, bf16[1,512,8192]{2,1,0:T(8,128)(2,1)}, u32[]{:S(2)}) %copy-start) | copy-done | bytes 8388632
  29.2 0.9 copy-done.2
  30.1 2.4 %sketched_early.1.refs_4_ = f32[512,256]{1,0:T(8,128)S(1)} custom-call(s32[20]{0:T(128)S(1)} %stack.97.place, bf16[512,8192]{1,0:T(8,128)(2,1)S(1)} %bitcast.28, bf16[512,256]{1,0:T(8,128)(2,1)S(1)} %copy-done.2, bf16[512,256]{1,0:T(8,128)(2,1)S(1)} %collective-permute-done.refs_1_, bf16[512,256]{1,0:T(8,128)(2,1)S(1)} %collective-permute-done.1.refs_2_, ...), custom_call_target="tpu_custom_call" | custom-call | flops 1600000000 | bytes 4194304 | tf_op jit(solution)/shard_map/sketched_early/pallas_call | solution.py:45
  32.5 1.1 collective-permute-start.14
  33.7 1.1 collective-permute-done.14.refs_2_
  35.1 2.6 %sketched_late.1 = (f32[192,128]{1,0:T(8,128)S(1)}, f32[192,128]{1,0:T(8,128)S(1)}, f32[512,256]{1,0:T(8,128)S(1)}, bf16[256,512]{1,0:T(8,128)(2,1)S(1)}) custom-call(s32[20]{0:T(128)S(1)} %stack.97.place, bf16[512,8192]{1,0:T(8,128)(2,1)S(1)} %bitcast.29, bf16[512,256]{1,0:T(8,128)(2,1)S(1)} %collective-permute-done.5.refs_0_, ...), custom_call_target="tpu_custom_call" | custom-call | flops 800000000 | bytes 4194304 | tf_op jit(solution)/shard_map/sketched_late/pallas_call | solution.py:45
  38.1 0.9 collective-permute-done.16
  39.2 2.9 %product.1 = (bf16[8,256,512]{2,1,0:T(8,128)(2,1)S(1)}, bf16[8,256,512]{2,1,0:T(8,128)(2,1)S(1)}) custom-call(s32[20]{0:T(128)S(1)} %stack.97.place, bf16[512,8192]{1,0:T(8,128)(2,1)S(1)} %bitcast.30, bf16[256,512]{1,0:T(8,128)(2,1)S(1)} %get-tuple-element.48.turned), custom_call_target="tpu_custom_call" | custom-call | flops 2200000000 | bytes 4194304 | tf_op jit(solution)/shard_map/product/pallas_call | solution.py:45
  42.1 1.1 collective-permute-done.17
  43.2 1.2 collective-permute-start.21
  44.4 3.5 %collective-permute-start.20 = (f32[192,128]{1,0:T(8,128)S(1)}, f32[192,128]{1,0:T(8,128)S(1)}, u32[]{:S(2)}, u32[]{:S(2)}) collective-permute-start(f32[192,128]{1,0:T(8,128)S(1)} %add.169), channel_id=1, source_target_pairs={{0,12},{1,13},{2,14},{3,15},{4,0},{5,1},{6,2},{7,3},{8,4},{9,5},{1... | collective-permute-start | bytes 294920 | tf_op jit(solution)/shard_map/sum_gram/ppermute | solution.py:25
  47.9 1.3 collective-permute-start.18
  49.3 2.0 %add_convert_fusion = bf16[8,256,512]{2,1,0:T(8,128)(2,1)} fusion(bf16[8,256,512]{2,1,0:T(8,128)(2,1)S(1)} %collective-permute-done.21, bf16[8,256,512]{2,1,0:T(8,128)(2,1)S(1)} %get-tuple-element.52), kind=kLoop, calls=%fused_computation | loop fusion | flops 4194304 | bytes 6291456 | tf_op jit(solution)/shard_map/sum_cores/convert_element_type | solution.py:311
  51.2 4.3 %collective-permute-done.19 = f32[192,128]{1,0:T(8,128)S(1)} collective-permute-done((f32[192,128]{1,0:T(8,128)S(1)}, f32[192,128]{1,0:T(8,128)S(1)}, u32[]{:S(2)}, u32[]{:S(2)}) %collective-permute-start.19) | collective-permute-done | bytes 98336 | tf_op jit(solution)/shard_map/sum_gram/ppermute | solution.py:25
  55.6 3.6 %all-to-all-start = ((bf16[8,256,512]{2,1,0:T(8,128)(2,1)}), bf16[8,256,512]{2,1,0:T(8,128)(2,1)S(1)}, u32[]{:S(2)}, u32[]{:S(2)}) async-start(bf16[8,256,512]{2,1,0:T(8,128)(2,1)} %add_convert_fusion), calls=%async_computation | async-start | bytes 4194304 | tf_op jit(solution)/shard_map/sum_fsdp/all_to_all | solution.py:316
  59.2 1.0 collective-permute-start.22
  60.2 0.9 collective-permute-done.22.theirs
  61.1 11.3 %inverse.1 = f32[256,256]{1,0:T(8,128)S(1)} custom-call(s32[20]{0:T(128)S(1)} %stack.97.place, f32[192,128]{1,0:T(8,128)S(1)} %add_add_fusion.mine, f32[192,128]{1,0:T(8,128)S(1)} %collective-permute-done.22.theirs), custom_call_target="tpu_custom_call" | custom-call | flops 3000000000 | bytes 4194304 | tf_op jit(solution)/shard_map/inverse/pallas_call | solution.py:45
  73.1 2.0 %collective-permute-start.23 = (bf16[512,256]{1,0:T(8,128)(2,1)S(1)}, bf16[512,256]{1,0:T(8,128)(2,1)S(1)}, u32[]{:S(2)}, u32[]{:S(2)}) collective-permute-start(bf16[512,256]{1,0:T(8,128)(2,1)S(1)} %basis.1), channel_id=1, source_target_pairs={{0,16},{1,17},{2,18},{3,19},{4,20},{5,21},{6,22},{7,23},{8,24},{9,... | collective-permute-start | bytes 786440 | tf_op jit(solution)/shard_map/gather_basis/ppermute | solution.py:25
  75.2 10.1 %all-to-all-done.parts = bf16[8,256,512]{2,1,0:T(8,128)(2,1)S(1)} async-done(((bf16[8,256,512]{2,1,0:T(8,128)(2,1)}), bf16[8,256,512]{2,1,0:T(8,128)(2,1)S(1)}, u32[]{:S(2)}, u32[]{:S(2)}) %all-to-all-start) | async-done | bytes 2097184 | tf_op jit(solution)/shard_map/sum_fsdp/all_to_all | solution.py:316
  85.3 1.5 %coef.1 = (bf16[256,128]{1,0:T(8,128)(2,1)S(1)}, bf16[256,128]{1,0:T(8,128)(2,1)S(1)}, bf16[256,128]{1,0:T(8,128)(2,1)S(1)}, bf16[256,128]{1,0:T(8,128)(2,1)S(1)}) custom-call(s32[20]{0:T(128)S(1)} %stack.97.place, f32[256,256]{1,0:T(8,128)S(1)} %inverse.1, bf16[8,256,512]{2,1,0:T(8,128)(2,1)S(1)} %all-to-all-done.parts), custom_call_target="tpu_custom_call" | custom-call | flops 400000000 | bytes 4194304 | tf_op jit(solution)/shard_map/coef/pallas_call | solution.py:45
  86.8 2.8 %collective-permute-done.23 = bf16[512,256]{1,0:T(8,128)(2,1)S(1)} collective-permute-done((bf16[512,256]{1,0:T(8,128)(2,1)S(1)}, bf16[512,256]{1,0:T(8,128)(2,1)S(1)}, u32[]{:S(2)}, u32[]{:S(2)}) %collective-permute-start.23) | collective-permute-done | bytes 262176 | tf_op jit(solution)/shard_map/gather_basis/ppermute | solution.py:25
  89.7 4.5 %collective-permute-start.24 = (bf16[256,128]{1,0:T(8,128)(2,1)S(1)}, bf16[256,128]{1,0:T(8,128)(2,1)S(1)}, u32[]{:S(2)}, u32[]{:S(2)}) collective-permute-start(bf16[256,128]{1,0:T(8,128)(2,1)S(1)} %get-tuple-element.65), channel_id=1, source_target_pairs={{0,0},{1,16},{2,2},{3,18},{4,4},{5,20},{6,6},{7,22},{8,8},{9,24},{... | collective-permute-start | bytes 196616 | tf_op jit(solution)/shard_map/exchange_coef/ppermute | solution.py:25
  94.2 1.7 %collective-permute-start.25 = (bf16[256,128]{1,0:T(8,128)(2,1)S(1)}, bf16[256,128]{1,0:T(8,128)(2,1)S(1)}, u32[]{:S(2)}, u32[]{:S(2)}) collective-permute-start(bf16[256,128]{1,0:T(8,128)(2,1)S(1)} %get-tuple-element.66), channel_id=1, source_target_pairs={{0,32},{1,48},{2,34},{3,50},{4,36},{5,52},{6,38},{7,54},{8,40},{9,... | collective-permute-start | bytes 196616 | tf_op jit(solution)/shard_map/exchange_coef/ppermute | solution.py:25
  95.8 4.8 %collective-permute-start.26 = (bf16[256,128]{1,0:T(8,128)(2,1)S(1)}, bf16[256,128]{1,0:T(8,128)(2,1)S(1)}, u32[]{:S(2)}, u32[]{:S(2)}) collective-permute-start(bf16[256,128]{1,0:T(8,128)(2,1)S(1)} %get-tuple-element.67), channel_id=1, source_target_pairs={{0,64},{1,80},{2,66},{3,82},{4,68},{5,84},{6,70},{7,86},{8,72},{9,... | collective-permute-start | bytes 196616 | tf_op jit(solution)/shard_map/exchange_coef/ppermute | solution.py:25
  100.6 1.5 %collective-permute-start.27 = (bf16[256,128]{1,0:T(8,128)(2,1)S(1)}, bf16[256,128]{1,0:T(8,128)(2,1)S(1)}, u32[]{:S(2)}, u32[]{:S(2)}) collective-permute-start(bf16[256,128]{1,0:T(8,128)(2,1)S(1)} %get-tuple-element.68), channel_id=1, source_target_pairs={{0,96},{1,112},{2,98},{3,114},{4,100},{5,116},{6,102},{7,118},{8,1... | collective-permute-start | bytes 196616 | tf_op jit(solution)/shard_map/exchange_coef/ppermute | solution.py:25
  102.1 1.3 collective-permute-done.26.t2
  103.4 3.3 %collective-permute-done.27.t3 = bf16[256,128]{1,0:T(8,128)(2,1)S(1)} collective-permute-done((bf16[256,128]{1,0:T(8,128)(2,1)S(1)}, bf16[256,128]{1,0:T(8,128)(2,1)S(1)}, u32[]{:S(2)}, u32[]{:S(2)}) %collective-permute-start.27) | collective-permute-done | bytes 65568 | tf_op jit(solution)/shard_map/exchange_coef/ppermute | solution.py:25
  106.7 1.6 %spread.1 = bf16[8,1024,128]{2,1,0:T(8,128)(2,1)} custom-call(bf16[256,128]{1,0:T(8,128)(2,1)S(1)} %collective-permute-done.24.t0, bf16[256,128]{1,0:T(8,128)(2,1)S(1)} %collective-permute-done.25.t1, bf16[256,128]{1,0:T(8,128)(2,1)S(1)} %collective-permute-done.26.t2, bf16[256,128]{1,0:T(8,128)(2,1)S(1)} %collective-permute-done.27.t3), custom_call_target="tpu_custom_call" | custom-call | bytes 4194304 | tf_op jit(solution)/shard_map/spread/pallas_call | solution.py:45
  108.3 5.5 %all-to-all-start.1 = ((bf16[8,1024,128]{2,1,0:T(8,128)(2,1)}), bf16[8,1024,128]{2,1,0:T(8,128)(2,1)}, u32[]{:S(2)}, u32[]{:S(2)}) async-start(bf16[8,1024,128]{2,1,0:T(8,128)(2,1)} %spread.1), calls=%async_computation.1 | async-start | bytes 4194304 | tf_op jit(solution)/shard_map/gather_coef/all_to_all | solution.py:351
  113.8 2.5 %collective-permute-start.30 = (bf16[2,512,256]{2,1,0:T(8,128)(2,1)S(1)}, bf16[2,512,256]{2,1,0:T(8,128)(2,1)S(1)}, u32[]{:S(2)}, u32[]{:S(2)}) collective-permute-start(bf16[2,512,256]{2,1,0:T(8,128)(2,1)S(1)} %pad_maximum_fusion.q0), channel_id=1, source_target_pairs={{0,96},{1,97},{2,98},{3,99},{4,100},{5,101},{6,102},{7,103},{8,104... | collective-permute-start | bytes 1572872 | tf_op jit(solution)/shard_map/gather_basis/ppermute | solution.py:25
  116.3 8.4 %collective-permute-done.30.q3 = bf16[2,512,256]{2,1,0:T(8,128)(2,1)S(1)} collective-permute-done((bf16[2,512,256]{2,1,0:T(8,128)(2,1)S(1)}, bf16[2,512,256]{2,1,0:T(8,128)(2,1)S(1)}, u32[]{:S(2)}, u32[]{:S(2)}) %collective-permute-start.30) | collective-permute-done | bytes 524320 | tf_op jit(solution)/shard_map/gather_basis/ppermute | solution.py:25
  124.7 2.7 %collective-permute-start.31 = (bf16[512,256]{1,0:T(8,128)(2,1)S(1)}, bf16[512,256]{1,0:T(8,128)(2,1)S(1)}, u32[]{:S(2)}, u32[]{:S(2)}) collective-permute-start(bf16[512,256]{1,0:T(8,128)(2,1)S(1)} %slice_bitcast_fusion), channel_id=1, source_target_pairs={{0,96},{1,97},{2,98},{3,99},{4,100},{5,101},{6,102},{7,103},{8,104... | collective-permute-start | bytes 786440 | tf_op jit(solution)/shard_map/gather_basis/ppermute | solution.py:25
  127.5 3.2 %collective-permute-done.31 = bf16[512,256]{1,0:T(8,128)(2,1)S(1)} collective-permute-done((bf16[512,256]{1,0:T(8,128)(2,1)S(1)}, bf16[512,256]{1,0:T(8,128)(2,1)S(1)}, u32[]{:S(2)}, u32[]{:S(2)}) %collective-permute-start.31) | collective-permute-done | bytes 262176 | tf_op jit(solution)/shard_map/gather_basis/ppermute | solution.py:25
  130.7 3.2 %collective-permute-done.29 = bf16[512,256]{1,0:T(8,128)(2,1)S(1)} collective-permute-done((bf16[512,256]{1,0:T(8,128)(2,1)S(1)}, bf16[512,256]{1,0:T(8,128)(2,1)S(1)}, u32[]{:S(2)}, u32[]{:S(2)}) %collective-permute-start.29) | collective-permute-done | bytes 262176 | tf_op jit(solution)/shard_map/gather_basis/ppermute | solution.py:25
  134.9 2.8 %partial.1.part = f32[512,1024]{1,0:T(8,128)S(1)} custom-call(bf16[512,2048]{1,0:T(8,128)(2,1)S(1)} %lay.1.left, bf16[8,1024,128]{2,1,0:T(8,128)(2,1)} %all-to-all-done.1.mine), custom_call_target="tpu_custom_call" | custom-call | flops 1100000000 | bytes 4194304 | tf_op jit(solution)/shard_map/partial/pallas_call | solution.py:45
  137.8 1.5 %collective-permute-done.32.theirs = bf16[8,1024,128]{2,1,0:T(8,128)(2,1)S(1)} collective-permute-done((bf16[8,1024,128]{2,1,0:T(8,128)(2,1)}, bf16[8,1024,128]{2,1,0:T(8,128)(2,1)S(1)}, u32[]{:S(2)}, u32[]{:S(2)}) %collective-permute-start.32) | collective-permute-done | bytes 2097184 | tf_op jit(solution)/shard_map/gather_coef/ppermute | solution.py:25
  139.3 5.6 %update.1 = (f32[512,1024]{1,0:T(8,128)}, f32[512,1024]{1,0:T(8,128)}) custom-call(f32[512,1024]{1,0:T(8,128)} %params.1, f32[512,1024]{1,0:T(8,128)} %momentum.1, f32[512,1024]{1,0:T(8,128)S(1)} %partial.1.part, bf16[512,2048]{1,0:T(8,128)(2,1)S(1)} %lay.1.left, bf16[8,1024,128]{2,1,0:T(8,128)(2,1)S(1)} %collective-permute-done.32.theirs), custom_call_target="tpu_custom_call" | custom-call | flops 1100000000 | bytes 14000000 | tf_op jit(solution)/shard_map/update/pallas_call | solution.py:221
  (50 shorter events, 4.3 us)
Async XLA Ops:
  0.6 10.8 %collective-permute-start.2 = (bf16[512,256]{1,0:T(8,128)(2,1)}, bf16[512,256]{1,0:T(8,128)(2,1)S(1)}, u32[]{:S(2)}, u32[]{:S(2)}) collective-permute-start(bf16[512,256]{1,0:T(8,128)(2,1)} %refs_0_.1), channel_id=1, source_target_pairs={{0,8},{1,9},{2,10},{3,11},{4,12},{5,13},{6,14},{7,15},{8,0},{9,1},... | collective-permute-start | bytes 786440 | tf_op jit(solution)/shard_map/gather_sketch/ppermute | solution.py:25
  5.1 9.1 %collective-permute-start.7 = (bf16[512,256]{1,0:T(8,128)(2,1)}, bf16[512,256]{1,0:T(8,128)(2,1)S(1)}, u32[]{:S(2)}, u32[]{:S(2)}) collective-permute-start(bf16[512,256]{1,0:T(8,128)(2,1)} %refs_0_.1), channel_id=1, source_target_pairs={{0,2},{1,3},{2,16},{3,17},{4,6},{5,7},{6,20},{7,21},{8,10},{9,11},... | collective-permute-start | bytes 786440 | tf_op jit(solution)/shard_map/gather_sketch/ppermute | solution.py:25
  6.4 11.1 %collective-permute-start.1 = (bf16[512,256]{1,0:T(8,128)(2,1)}, bf16[512,256]{1,0:T(8,128)(2,1)S(1)}, u32[]{:S(2)}, u32[]{:S(2)}) collective-permute-start(bf16[512,256]{1,0:T(8,128)(2,1)} %refs_0_.1), channel_id=1, source_target_pairs={{0,12},{1,13},{2,14},{3,15},{4,0},{5,1},{6,2},{7,3},{8,4},{9,5},{1... | collective-permute-start | bytes 786440 | tf_op jit(solution)/shard_map/gather_sketch/ppermute | solution.py:25
  6.9 12.1 %collective-permute-start = (bf16[512,256]{1,0:T(8,128)(2,1)}, bf16[512,256]{1,0:T(8,128)(2,1)S(1)}, u32[]{:S(2)}, u32[]{:S(2)}) collective-permute-start(bf16[512,256]{1,0:T(8,128)(2,1)} %refs_0_.1), channel_id=1, source_target_pairs={{0,4},{1,5},{2,6},{3,7},{4,8},{5,9},{6,10},{7,11},{8,12},{9,13},{1... | collective-permute-start | bytes 786440 | tf_op jit(solution)/shard_map/gather_sketch/ppermute | solution.py:25
  11.4 7.6 %collective-permute-start.4 = (bf16[256,256]{1,0:T(8,128)(2,1)S(1)}, bf16[256,256]{1,0:T(8,128)(2,1)S(1)}, u32[]{:S(2)}, u32[]{:S(2)}) collective-permute-start(bf16[256,256]{1,0:T(8,128)(2,1)S(1)} %get-tuple-element.72), channel_id=1, source_target_pairs={{0,18},{1,19},{2,0},{3,1},{4,22},{5,23},{6,4},{7,5},{8,26},{9,27},... | collective-permute-start | bytes 393224 | tf_op jit(solution)/shard_map/gather_sketch/ppermute | solution.py:25
  14.2 5.3 %collective-permute-start.3 = (bf16[256,256]{1,0:T(8,128)(2,1)S(1)}, bf16[256,256]{1,0:T(8,128)(2,1)S(1)}, u32[]{:S(2)}, u32[]{:S(2)}) collective-permute-start(bf16[256,256]{1,0:T(8,128)(2,1)S(1)} %get-tuple-element.73), channel_id=1, source_target_pairs={{0,2},{1,3},{2,16},{3,17},{4,6},{5,7},{6,20},{7,21},{8,10},{9,11},... | collective-permute-start | bytes 393224 | tf_op jit(solution)/shard_map/gather_sketch/ppermute | solution.py:25
  14.2 8.5 %collective-permute-start.8 = (bf16[512,256]{1,0:T(8,128)(2,1)}, bf16[512,256]{1,0:T(8,128)(2,1)S(1)}, u32[]{:S(2)}, u32[]{:S(2)}) collective-permute-start(bf16[512,256]{1,0:T(8,128)(2,1)} %refs_0_.1), channel_id=1, source_target_pairs={{0,1},{1,0},{2,3},{3,2},{4,5},{5,4},{6,7},{7,6},{8,9},{9,8},{10,11... | collective-permute-start | bytes 786440 | tf_op jit(solution)/shard_map/gather_sketch/ppermute | solution.py:25
  17.6 5.4 %collective-permute-start.12 = (bf16[512,256]{1,0:T(8,128)(2,1)S(1)}, bf16[512,256]{1,0:T(8,128)(2,1)S(1)}, u32[]{:S(2)}, u32[]{:S(2)}) collective-permute-start(bf16[512,256]{1,0:T(8,128)(2,1)S(1)} %collective-permute-done.2.refs_4_), channel_id=1, source_target_pairs={{0,1},{1,0},{2,3},{3,2},{4,5},{5,4},{6,7},{7,6},{8,9},{9,8},{10,11... | collective-permute-start | bytes 786440 | tf_op jit(solution)/shard_map/gather_sketch/ppermute | solution.py:25
  19.0 3.9 %collective-permute-start.11 = (bf16[512,256]{1,0:T(8,128)(2,1)S(1)}, bf16[512,256]{1,0:T(8,128)(2,1)S(1)}, u32[]{:S(2)}, u32[]{:S(2)}) collective-permute-start(bf16[512,256]{1,0:T(8,128)(2,1)S(1)} %collective-permute-done.7.refs_3_), channel_id=1, source_target_pairs={{0,1},{1,0},{2,3},{3,2},{4,5},{5,4},{6,7},{7,6},{8,9},{9,8},{10,11... | collective-permute-start | bytes 786440 | tf_op jit(solution)/shard_map/gather_sketch/ppermute | solution.py:25
  19.0 6.7 %collective-permute-start.10 = (bf16[512,256]{1,0:T(8,128)(2,1)S(1)}, bf16[512,256]{1,0:T(8,128)(2,1)S(1)}, u32[]{:S(2)}, u32[]{:S(2)}) collective-permute-start(bf16[512,256]{1,0:T(8,128)(2,1)S(1)} %collective-permute-done.1.refs_2_), channel_id=1, source_target_pairs={{0,1},{1,0},{2,3},{3,2},{4,5},{5,4},{6,7},{7,6},{8,9},{9,8},{10,11... | collective-permute-start | bytes 786440 | tf_op jit(solution)/shard_map/gather_sketch/ppermute | solution.py:25
  19.5 6.2 %collective-permute-start.9 = (bf16[512,256]{1,0:T(8,128)(2,1)S(1)}, bf16[512,256]{1,0:T(8,128)(2,1)S(1)}, u32[]{:S(2)}, u32[]{:S(2)}) collective-permute-start(bf16[512,256]{1,0:T(8,128)(2,1)S(1)} %collective-permute-done.refs_1_), channel_id=1, source_target_pairs={{0,1},{1,0},{2,3},{3,2},{4,5},{5,4},{6,7},{7,6},{8,9},{9,8},{10,11... | collective-permute-start | bytes 786440 | tf_op jit(solution)/shard_map/gather_sketch/ppermute | solution.py:25
  22.8 3.0 %collective-permute-start.13 = (bf16[512,256]{1,0:T(8,128)(2,1)S(1)}, bf16[512,256]{1,0:T(8,128)(2,1)S(1)}, u32[]{:S(2)}, u32[]{:S(2)}) collective-permute-start(bf16[512,256]{1,0:T(8,128)(2,1)S(1)} %constant_dynamic-update-slice_fusion.refs_5_), channel_id=1, source_target_pairs={{0,1},{1,0},{2,3},{3,2},{4,5},{5,4},{6,7},{7,6},{8,9},{9,8},{10,11... | collective-permute-start | bytes 786440 | tf_op jit(solution)/shard_map/gather_sketch/ppermute | solution.py:25
  22.9 9.6 %collective-permute-start.5 = (bf16[512,256]{1,0:T(8,128)(2,1)S(1)}, bf16[512,256]{1,0:T(8,128)(2,1)S(1)}, u32[]{:S(2)}, u32[]{:S(2)}) collective-permute-start(bf16[512,256]{1,0:T(8,128)(2,1)S(1)} %collective-permute-done.refs_1_), channel_id=1, source_target_pairs={{0,2},{1,3},{2,16},{3,17},{4,6},{5,7},{6,20},{7,21},{8,10},{9,11},... | collective-permute-start | bytes 786440 | tf_op jit(solution)/shard_map/gather_sketch/ppermute | solution.py:25
  23.0 9.5 %collective-permute-start.6 = (bf16[512,256]{1,0:T(8,128)(2,1)S(1)}, bf16[512,256]{1,0:T(8,128)(2,1)S(1)}, u32[]{:S(2)}, u32[]{:S(2)}) collective-permute-start(bf16[512,256]{1,0:T(8,128)(2,1)S(1)} %collective-permute-done.1.refs_2_), channel_id=1, source_target_pairs={{0,18},{1,19},{2,0},{3,1},{4,22},{5,23},{6,4},{7,5},{8,26},{9,27},... | collective-permute-start | bytes 786440 | tf_op jit(solution)/shard_map/gather_sketch/ppermute | solution.py:25
  25.8 3.4 %copy-start = (bf16[1,512,8192]{2,1,0:T(8,128)(2,1)S(1)}, bf16[1,512,8192]{2,1,0:T(8,128)(2,1)}, u32[]{:S(2)}) copy-start(bf16[1,512,8192]{2,1,0:T(8,128)(2,1)} %param.4) | copy-start | bytes 25165828
  29.2 0.9 copy-start.2
  32.5 6.7 %copy-start.1 = (bf16[1,512,8192]{2,1,0:T(8,128)(2,1)S(1)}, bf16[1,512,8192]{2,1,0:T(8,128)(2,1)}, u32[]{:S(2)}) copy-start(bf16[1,512,8192]{2,1,0:T(8,128)(2,1)} %param.4) | copy-start | bytes 25165828
  32.5 2.2 %collective-permute-start.14 = (bf16[512,256]{1,0:T(8,128)(2,1)S(1)}, bf16[512,256]{1,0:T(8,128)(2,1)S(1)}, u32[]{:S(2)}, u32[]{:S(2)}) collective-permute-start(bf16[512,256]{1,0:T(8,128)(2,1)S(1)} %collective-permute-done.5.refs_0_), channel_id=1, source_target_pairs={{0,1},{1,0},{2,3},{3,2},{4,5},{5,4},{6,7},{7,6},{8,9},{9,8},{10,11... | collective-permute-start | bytes 786440 | tf_op jit(solution)/shard_map/gather_sketch/ppermute | solution.py:25
  33.6 1.5 %collective-permute-start.15 = (bf16[512,256]{1,0:T(8,128)(2,1)S(1)}, bf16[512,256]{1,0:T(8,128)(2,1)S(1)}, u32[]{:S(2)}, u32[]{:S(2)}) collective-permute-start(bf16[512,256]{1,0:T(8,128)(2,1)S(1)} %collective-permute-done.6.refs_1_), channel_id=1, source_target_pairs={{0,1},{1,0},{2,3},{3,2},{4,5},{5,4},{6,7},{7,6},{8,9},{9,8},{10,11... | collective-permute-start | bytes 786440 | tf_op jit(solution)/shard_map/gather_sketch/ppermute | solution.py:25
  37.7 1.4 collective-permute-start.16
  39.1 4.1 %collective-permute-start.17 = (f32[192,128]{1,0:T(8,128)S(1)}, f32[192,128]{1,0:T(8,128)S(1)}, u32[]{:S(2)}, u32[]{:S(2)}) collective-permute-start(f32[192,128]{1,0:T(8,128)S(1)} %add.168), channel_id=1, source_target_pairs={{0,2},{1,3},{2,0},{3,1},{4,6},{5,7},{6,4},{7,5},{8,10},{9,11},{10,... | collective-permute-start | bytes 294920 | tf_op jit(solution)/shard_map/sum_gram/ppermute | solution.py:25
  43.2 6.0 %collective-permute-start.21 = (bf16[8,256,512]{2,1,0:T(8,128)(2,1)S(1)}, bf16[8,256,512]{2,1,0:T(8,128)(2,1)S(1)}, u32[]{:S(2)}, u32[]{:S(2)}) collective-permute-start(bf16[8,256,512]{2,1,0:T(8,128)(2,1)S(1)} %get-tuple-element.53), channel_id=1, source_target_pairs={{0,1},{1,0},{2,3},{3,2},{4,5},{5,4},{6,7},{7,6},{8,9},{9,8},{10,11... | collective-permute-start | bytes 6291464 | tf_op jit(solution)/shard_map/sum_cores/ppermute | solution.py:25
  44.4 6.8 %collective-permute-start.20 = (f32[192,128]{1,0:T(8,128)S(1)}, f32[192,128]{1,0:T(8,128)S(1)}, u32[]{:S(2)}, u32[]{:S(2)}) collective-permute-start(f32[192,128]{1,0:T(8,128)S(1)} %add.169), channel_id=1, source_target_pairs={{0,12},{1,13},{2,14},{3,15},{4,0},{5,1},{6,2},{7,3},{8,4},{9,5},{1... | collective-permute-start | bytes 294920 | tf_op jit(solution)/shard_map/sum_gram/ppermute | solution.py:25
  47.9 7.7 %collective-permute-start.19 = (f32[192,128]{1,0:T(8,128)S(1)}, f32[192,128]{1,0:T(8,128)S(1)}, u32[]{:S(2)}, u32[]{:S(2)}) collective-permute-start(f32[192,128]{1,0:T(8,128)S(1)} %add.169), channel_id=1, source_target_pairs={{0,4},{1,5},{2,6},{3,7},{4,8},{5,9},{6,10},{7,11},{8,12},{9,13},{1... | collective-permute-start | bytes 294920 | tf_op jit(solution)/shard_map/sum_gram/ppermute | solution.py:25
  47.9 7.7 %collective-permute-start.18 = (f32[192,128]{1,0:T(8,128)S(1)}, f32[192,128]{1,0:T(8,128)S(1)}, u32[]{:S(2)}, u32[]{:S(2)}) collective-permute-start(f32[192,128]{1,0:T(8,128)S(1)} %add.169), channel_id=1, source_target_pairs={{0,8},{1,9},{2,10},{3,11},{4,12},{5,13},{6,14},{7,15},{8,0},{9,1},... | collective-permute-start | bytes 294920 | tf_op jit(solution)/shard_map/sum_gram/ppermute | solution.py:25
  55.6 29.7 %all-to-all-start = ((bf16[8,256,512]{2,1,0:T(8,128)(2,1)}), bf16[8,256,512]{2,1,0:T(8,128)(2,1)S(1)}, u32[]{:S(2)}, u32[]{:S(2)}) async-start(bf16[8,256,512]{2,1,0:T(8,128)(2,1)} %add_convert_fusion), calls=%async_computation | async-start | bytes 4194304 | tf_op jit(solution)/shard_map/sum_fsdp/all_to_all | solution.py:316
  59.2 1.9 %collective-permute-start.22 = (f32[192,128]{1,0:T(8,128)S(1)}, f32[192,128]{1,0:T(8,128)S(1)}, u32[]{:S(2)}, u32[]{:S(2)}) collective-permute-start(f32[192,128]{1,0:T(8,128)S(1)} %add_add_fusion.mine), channel_id=1, source_target_pairs={{0,1},{1,0},{2,3},{3,2},{4,5},{5,4},{6,7},{7,6},{8,9},{9,8},{10,11... | collective-permute-start | bytes 294920 | tf_op jit(solution)/shard_map/sum_gram/ppermute | solution.py:25
  73.1 16.5 %collective-permute-start.23 = (bf16[512,256]{1,0:T(8,128)(2,1)S(1)}, bf16[512,256]{1,0:T(8,128)(2,1)S(1)}, u32[]{:S(2)}, u32[]{:S(2)}) collective-permute-start(bf16[512,256]{1,0:T(8,128)(2,1)S(1)} %basis.1), channel_id=1, source_target_pairs={{0,16},{1,17},{2,18},{3,19},{4,20},{5,21},{6,22},{7,23},{8,24},{9,... | collective-permute-start | bytes 786440 | tf_op jit(solution)/shard_map/gather_basis/ppermute | solution.py:25
  89.7 12.4 %collective-permute-start.24 = (bf16[256,128]{1,0:T(8,128)(2,1)S(1)}, bf16[256,128]{1,0:T(8,128)(2,1)S(1)}, u32[]{:S(2)}, u32[]{:S(2)}) collective-permute-start(bf16[256,128]{1,0:T(8,128)(2,1)S(1)} %get-tuple-element.65), channel_id=1, source_target_pairs={{0,0},{1,16},{2,2},{3,18},{4,4},{5,20},{6,6},{7,22},{8,8},{9,24},{... | collective-permute-start | bytes 196616 | tf_op jit(solution)/shard_map/exchange_coef/ppermute | solution.py:25
  94.2 8.0 %collective-permute-start.25 = (bf16[256,128]{1,0:T(8,128)(2,1)S(1)}, bf16[256,128]{1,0:T(8,128)(2,1)S(1)}, u32[]{:S(2)}, u32[]{:S(2)}) collective-permute-start(bf16[256,128]{1,0:T(8,128)(2,1)S(1)} %get-tuple-element.66), channel_id=1, source_target_pairs={{0,32},{1,48},{2,34},{3,50},{4,36},{5,52},{6,38},{7,54},{8,40},{9,... | collective-permute-start | bytes 196616 | tf_op jit(solution)/shard_map/exchange_coef/ppermute | solution.py:25
  95.8 7.6 %collective-permute-start.26 = (bf16[256,128]{1,0:T(8,128)(2,1)S(1)}, bf16[256,128]{1,0:T(8,128)(2,1)S(1)}, u32[]{:S(2)}, u32[]{:S(2)}) collective-permute-start(bf16[256,128]{1,0:T(8,128)(2,1)S(1)} %get-tuple-element.67), channel_id=1, source_target_pairs={{0,64},{1,80},{2,66},{3,82},{4,68},{5,84},{6,70},{7,86},{8,72},{9,... | collective-permute-start | bytes 196616 | tf_op jit(solution)/shard_map/exchange_coef/ppermute | solution.py:25
  100.6 6.1 %collective-permute-start.27 = (bf16[256,128]{1,0:T(8,128)(2,1)S(1)}, bf16[256,128]{1,0:T(8,128)(2,1)S(1)}, u32[]{:S(2)}, u32[]{:S(2)}) collective-permute-start(bf16[256,128]{1,0:T(8,128)(2,1)S(1)} %get-tuple-element.68), channel_id=1, source_target_pairs={{0,96},{1,112},{2,98},{3,114},{4,100},{5,116},{6,102},{7,118},{8,1... | collective-permute-start | bytes 196616 | tf_op jit(solution)/shard_map/exchange_coef/ppermute | solution.py:25
  108.3 26.7 %all-to-all-start.1 = ((bf16[8,1024,128]{2,1,0:T(8,128)(2,1)}), bf16[8,1024,128]{2,1,0:T(8,128)(2,1)}, u32[]{:S(2)}, u32[]{:S(2)}) async-start(bf16[8,1024,128]{2,1,0:T(8,128)(2,1)} %spread.1), calls=%async_computation.1 | async-start | bytes 4194304 | tf_op jit(solution)/shard_map/gather_coef/all_to_all | solution.py:351
  113.8 10.8 %collective-permute-start.30 = (bf16[2,512,256]{2,1,0:T(8,128)(2,1)S(1)}, bf16[2,512,256]{2,1,0:T(8,128)(2,1)S(1)}, u32[]{:S(2)}, u32[]{:S(2)}) collective-permute-start(bf16[2,512,256]{2,1,0:T(8,128)(2,1)S(1)} %pad_maximum_fusion.q0), channel_id=1, source_target_pairs={{0,96},{1,97},{2,98},{3,99},{4,100},{5,101},{6,102},{7,103},{8,104... | collective-permute-start | bytes 1572872 | tf_op jit(solution)/shard_map/gather_basis/ppermute | solution.py:25
  116.3 11.1 %collective-permute-start.28 = (bf16[2,512,256]{2,1,0:T(8,128)(2,1)S(1)}, bf16[2,512,256]{2,1,0:T(8,128)(2,1)S(1)}, u32[]{:S(2)}, u32[]{:S(2)}) collective-permute-start(bf16[2,512,256]{2,1,0:T(8,128)(2,1)S(1)} %pad_maximum_fusion.q0), channel_id=1, source_target_pairs={{0,32},{1,33},{2,34},{3,35},{4,36},{5,37},{6,38},{7,39},{8,40},{9,... | collective-permute-start | bytes 1572872 | tf_op jit(solution)/shard_map/gather_basis/ppermute | solution.py:25
  124.7 6.0 %collective-permute-start.31 = (bf16[512,256]{1,0:T(8,128)(2,1)S(1)}, bf16[512,256]{1,0:T(8,128)(2,1)S(1)}, u32[]{:S(2)}, u32[]{:S(2)}) collective-permute-start(bf16[512,256]{1,0:T(8,128)(2,1)S(1)} %slice_bitcast_fusion), channel_id=1, source_target_pairs={{0,96},{1,97},{2,98},{3,99},{4,100},{5,101},{6,102},{7,103},{8,104... | collective-permute-start | bytes 786440 | tf_op jit(solution)/shard_map/gather_basis/ppermute | solution.py:25
  127.4 6.5 %collective-permute-start.29 = (bf16[512,256]{1,0:T(8,128)(2,1)S(1)}, bf16[512,256]{1,0:T(8,128)(2,1)S(1)}, u32[]{:S(2)}, u32[]{:S(2)}) collective-permute-start(bf16[512,256]{1,0:T(8,128)(2,1)S(1)} %slice_bitcast_fusion.1), channel_id=1, source_target_pairs={{0,32},{1,33},{2,34},{3,35},{4,36},{5,37},{6,38},{7,39},{8,40},{9,... | collective-permute-start | bytes 786440 | tf_op jit(solution)/shard_map/gather_basis/ppermute | solution.py:25
  134.9 4.4 %collective-permute-start.32 = (bf16[8,1024,128]{2,1,0:T(8,128)(2,1)}, bf16[8,1024,128]{2,1,0:T(8,128)(2,1)S(1)}, u32[]{:S(2)}, u32[]{:S(2)}) collective-permute-start(bf16[8,1024,128]{2,1,0:T(8,128)(2,1)} %all-to-all-done.1.mine), channel_id=1, source_target_pairs={{0,1},{1,0},{2,3},{3,2},{4,5},{5,4},{6,7},{7,6},{8,9},{9,8},{10,11... | collective-permute-start | bytes 6291464 | tf_op jit(solution)/shard_map/gather_coef/ppermute | solution.py:25

commit v4 on v3

--- a/solution.py
+++ b/solution.py
@@ -205,41 +205,40 @@
         )
 
 
-def update_kernel(params, momentum, part, left, theirs, new_params, new_momentum):
-    right = jnp.concatenate([theirs[0], theirs[1]], axis=1)
-    rest = jnp.dot(left[...], right, preferred_element_type=F32)
-    average = (part[...] + rest) * (1.0 / ISLANDS)
-    new = 0.9 * momentum[...] + average
-    new_momentum[...] = new
-    new_params[...] = params[...] - 0.7 * (average + 0.9 * new)
+def update_kernel(left, theirs, part, params, momentum, new_params, new_momentum, sums, sems):
+    depth = theirs.shape[1]
+    steps = sems.shape[1]
+    count = left.shape[0] // steps
+    outs = []
+    for n in range(steps):
+        rows = slice(n * count, (n + 1) * count)
+        for t in range(0, 8, 2):
+            at = slice(t * BLK, (t + 2) * BLK)
+            right = jnp.concatenate([theirs[t], theirs[t + 1]], axis=1)
+            rest = jnp.dot(left[rows, depth:], right, preferred_element_type=F32)
+            average = (part[rows, at] + rest) * (1.0 / ISLANDS)
+            new = 0.9 * momentum[rows, at] + average
+            sums[1, rows, at] = new
+            sums[0, rows, at] = params[rows, at] - 0.7 * (average + 0.9 * new)
+        for m, out in enumerate((new_params, new_momentum)):
+            outs.append(pltpu.make_async_copy(sums.at[m, rows], out.at[rows], sems.at[m, n]))
+            outs[-1].start()
+    for out in outs:
+        out.wait()
 
 
 def update_call(params, momentum, part, left, theirs):
-    rows, width = params.shape
-    depth = theirs.shape[1]
-    tile = pl.BlockSpec((rows, 2 * BLK), lambda g: (0, g))
+    shape = params.shape
     return pl.pallas_call(
         update_kernel,
-        grid=(4,),
-        in_specs=[
-            tile,
-            tile,
-            tile,
-            pl.BlockSpec((rows, depth), lambda g: (0, 1)),
-            pl.BlockSpec((2, depth, BLK), lambda g: (g, 0, 0)),
-        ],
-        out_specs=[tile, tile],
-        out_shape=[jax.ShapeDtypeStruct((rows, width), F32)] * 2,
+        in_specs=[VMEM] * 5,
+        out_specs=[FAR, FAR],
+        out_shape=[jax.ShapeDtypeStruct(shape, F32)] * 2,
+        scratch_shapes=[pltpu.VMEM((2,) + shape, F32), pltpu.SemaphoreType.DMA((2, 4))],
         compiler_params=pltpu.CompilerParams(vmem_limit_bytes=16 * 1024 * 1024),
         cost_estimate=pl.CostEstimate(flops=1100000000, bytes_accessed=14000000, transcendentals=0),
         name="update",
-    )(
-        pltpu.with_memory_space_constraint(params, pltpu.HBM),
-        pltpu.with_memory_space_constraint(momentum, pltpu.HBM),
-        part,
-        left,
-        theirs,
-    )
+    )(left, theirs, part, params, momentum)
 
 
 def body(delta, sketch, params, momentum):
@@ -350,7 +349,7 @@
     with jax.named_scope("gather_coef"):
         mine, operand = fence((lax.all_to_all(tiles, ("z", "yl"), 0, 0, tiled=True), operand))
         theirs = shift(mine, dc=1)
-    part = call(partial_kernel, [((rows, 8 * BLK), F32)], 1.1e9, "partial", False)(operand, mine)[0]
+    part = call(partial_kernel, [pltpu.VMEM((rows, 8 * BLK), F32)], 1.1e9, "partial", False)(operand, mine)[0]
     return tuple(update_call(params, momentum, part, operand, theirs))
 
 

time: 146 us -> 143 us (0.979)
  Pallas kernels: 32.2 us -> 29.5 us
    pallas_call x1, Pallas kernels: 5.58 us -> 2.65 us  [update_call(): pl.pallas_call(update_kernel, in_specs=[VMEM] * 5, out_specs=[FAR, FAR],...]
    unnamed x7 -> x11, local copies, waits for them, and re-layouts: 4.34 us -> 4.35 us
where the time goes in v4:
time: 143 us; the launch traced here: 142 us
  starting transfers between devices  57.9 us (40%)
  waiting for transfers between devices  47.1 us (33%)
  Pallas kernels  29.5 us (21%)
  local copies, waits for them, and re-layouts  4.51 us (3%)
  other arithmetic  2.11 us (1%)
    ppermute x33, starting transfers between devices, move(): return lax.ppermute(value, AXES, pairs)  48.8 us
    ppermute x33, waiting for transfers between devices, move(): return lax.ppermute(value, AXES, pairs)  36.8 us
    pallas_call x9, Pallas kernels, run(): pl.pallas_call(kernel, in_specs=[SMEM] * smem + [VMEM] * (len(args) - sme...  26.8 us
    all_to_all x1, waiting for transfers between devices, body(): parts = lax.all_to_all(kept, ('z', 'yl'), 0, 0, tiled=True)  10.1 us
    all_to_all x1, starting transfers between devices, body(): lax.all_to_all(tiles, ('z', 'yl'), 0, 0, tiled=True)  5.51 us
    unnamed x11, local copies, waits for them, and re-layouts  4.35 us
    all_to_all x1, starting transfers between devices, body(): parts = lax.all_to_all(kept, ('z', 'yl'), 0, 0, tiled=True)  3.62 us
  transfers between devices with their start and end apart: 35, of which 17 were waited for; matrix products, arithmetic and copies ran while one was open for 2% of the time, Pallas kernels for 16%

profile of v4, /device:TPU:1, one launch (start us, length us, event | category | flops | bytes accessed | tf_op | source)
XLA Modules:
  0.0 142.2 jit_solution(14768170447972749813)
XLA Ops:
  0.6 4.5 %collective-permute-start.2 = (bf16[512,256]{1,0:T(8,128)(2,1)}, bf16[512,256]{1,0:T(8,128)(2,1)S(1)}, u32[]{:S(2)}, u32[]{:S(2)}) collective-permute-start(bf16[512,256]{1,0:T(8,128)(2,1)} %refs_0_.1), channel_id=1, source_target_pairs={{0,8},{1,9},{2,10},{3,11},{4,12},{5,13},{6,14},{7,15},{8,0},{9,1},... | collective-permute-start | bytes 786440 | tf_op jit(solution)/shard_map/gather_sketch/ppermute | solution.py:25
  5.1 1.3 collective-permute-start.7
  6.9 1.0 collective-permute-start
  7.9 3.5 %collective-permute-done.2.refs_4_ = bf16[512,256]{1,0:T(8,128)(2,1)S(1)} collective-permute-done((bf16[512,256]{1,0:T(8,128)(2,1)}, bf16[512,256]{1,0:T(8,128)(2,1)S(1)}, u32[]{:S(2)}, u32[]{:S(2)}) %collective-permute-start.2) | collective-permute-done | bytes 262176 | tf_op jit(solution)/shard_map/gather_sketch/ppermute | solution.py:25
  11.4 2.8 %collective-permute-start.4 = (bf16[256,256]{1,0:T(8,128)(2,1)S(1)}, bf16[256,256]{1,0:T(8,128)(2,1)S(1)}, u32[]{:S(2)}, u32[]{:S(2)}) collective-permute-start(bf16[256,256]{1,0:T(8,128)(2,1)S(1)} %get-tuple-element.72), channel_id=1, source_target_pairs={{0,18},{1,19},{2,0},{3,1},{4,22},{5,23},{6,4},{7,5},{8,26},{9,27},... | collective-permute-start | bytes 393224 | tf_op jit(solution)/shard_map/gather_sketch/ppermute | solution.py:25
  14.2 2.3 %collective-permute-start.8 = (bf16[512,256]{1,0:T(8,128)(2,1)}, bf16[512,256]{1,0:T(8,128)(2,1)S(1)}, u32[]{:S(2)}, u32[]{:S(2)}) collective-permute-start(bf16[512,256]{1,0:T(8,128)(2,1)} %refs_0_.1), channel_id=1, source_target_pairs={{0,1},{1,0},{2,3},{3,2},{4,5},{5,4},{6,7},{7,6},{8,9},{9,8},{10,11... | collective-permute-start | bytes 786440 | tf_op jit(solution)/shard_map/gather_sketch/ppermute | solution.py:25
  16.6 1.0 collective-permute-done.1.refs_2_
  17.6 1.4 %collective-permute-start.12 = (bf16[512,256]{1,0:T(8,128)(2,1)S(1)}, bf16[512,256]{1,0:T(8,128)(2,1)S(1)}, u32[]{:S(2)}, u32[]{:S(2)}) collective-permute-start(bf16[512,256]{1,0:T(8,128)(2,1)S(1)} %collective-permute-done.2.refs_4_), channel_id=1, source_target_pairs={{0,1},{1,0},{2,3},{3,2},{4,5},{5,4},{6,7},{7,6},{8,9},{9,8},{10,11... | collective-permute-start | bytes 786440 | tf_op jit(solution)/shard_map/gather_sketch/ppermute | solution.py:25
  19.5 3.2 %collective-permute-start.9 = (bf16[512,256]{1,0:T(8,128)(2,1)S(1)}, bf16[512,256]{1,0:T(8,128)(2,1)S(1)}, u32[]{:S(2)}, u32[]{:S(2)}) collective-permute-start(bf16[512,256]{1,0:T(8,128)(2,1)S(1)} %collective-permute-done.refs_1_), channel_id=1, source_target_pairs={{0,1},{1,0},{2,3},{3,2},{4,5},{5,4},{6,7},{7,6},{8,9},{9,8},{10,11... | collective-permute-start | bytes 786440 | tf_op jit(solution)/shard_map/gather_sketch/ppermute | solution.py:25
  23.0 2.7 %collective-permute-start.6 = (bf16[512,256]{1,0:T(8,128)(2,1)S(1)}, bf16[512,256]{1,0:T(8,128)(2,1)S(1)}, u32[]{:S(2)}, u32[]{:S(2)}) collective-permute-start(bf16[512,256]{1,0:T(8,128)(2,1)S(1)} %collective-permute-done.1.refs_2_), channel_id=1, source_target_pairs={{0,18},{1,19},{2,0},{3,1},{4,22},{5,23},{6,4},{7,5},{8,26},{9,27},... | collective-permute-start | bytes 786440 | tf_op jit(solution)/shard_map/gather_sketch/ppermute | solution.py:25
  25.8 3.4 %copy-done = bf16[1,512,8192]{2,1,0:T(8,128)(2,1)S(1)} copy-done((bf16[1,512,8192]{2,1,0:T(8,128)(2,1)S(1)}, bf16[1,512,8192]{2,1,0:T(8,128)(2,1)}, u32[]{:S(2)}) %copy-start) | copy-done | bytes 8388632
  29.2 0.9 copy-done.4
  30.1 2.4 %sketched_early.1.refs_4_ = f32[512,256]{1,0:T(8,128)S(1)} custom-call(s32[20]{0:T(128)S(1)} %stack.97.place, bf16[512,8192]{1,0:T(8,128)(2,1)S(1)} %bitcast.28, bf16[512,256]{1,0:T(8,128)(2,1)S(1)} %copy-done.4, bf16[512,256]{1,0:T(8,128)(2,1)S(1)} %collective-permute-done.refs_1_, bf16[512,256]{1,0:T(8,128)(2,1)S(1)} %collective-permute-done.1.refs_2_, ...), custom_call_target="tpu_custom_call" | custom-call | flops 1600000000 | bytes 4194304 | tf_op jit(solution)/shard_map/sketched_early/pallas_call | solution.py:45
  32.5 1.1 collective-permute-start.14
  33.7 1.1 collective-permute-done.14.refs_2_
  35.1 2.6 %sketched_late.1 = (f32[192,128]{1,0:T(8,128)S(1)}, f32[192,128]{1,0:T(8,128)S(1)}, f32[512,256]{1,0:T(8,128)S(1)}, bf16[256,512]{1,0:T(8,128)(2,1)S(1)}) custom-call(s32[20]{0:T(128)S(1)} %stack.97.place, bf16[512,8192]{1,0:T(8,128)(2,1)S(1)} %bitcast.29, bf16[512,256]{1,0:T(8,128)(2,1)S(1)} %collective-permute-done.5.refs_0_, ...), custom_call_target="tpu_custom_call" | custom-call | flops 800000000 | bytes 4194304 | tf_op jit(solution)/shard_map/sketched_late/pallas_call | solution.py:45
  38.1 0.9 collective-permute-done.16
  39.2 2.9 %product.1 = (bf16[8,256,512]{2,1,0:T(8,128)(2,1)S(1)}, bf16[8,256,512]{2,1,0:T(8,128)(2,1)S(1)}) custom-call(s32[20]{0:T(128)S(1)} %stack.97.place, bf16[512,8192]{1,0:T(8,128)(2,1)S(1)} %bitcast.30, bf16[256,512]{1,0:T(8,128)(2,1)S(1)} %get-tuple-element.48.turned), custom_call_target="tpu_custom_call" | custom-call | flops 2200000000 | bytes 4194304 | tf_op jit(solution)/shard_map/product/pallas_call | solution.py:45
  42.1 1.1 collective-permute-done.17
  43.2 1.2 collective-permute-start.21
  44.4 3.5 %collective-permute-start.20 = (f32[192,128]{1,0:T(8,128)S(1)}, f32[192,128]{1,0:T(8,128)S(1)}, u32[]{:S(2)}, u32[]{:S(2)}) collective-permute-start(f32[192,128]{1,0:T(8,128)S(1)} %add.169), channel_id=1, source_target_pairs={{0,12},{1,13},{2,14},{3,15},{4,0},{5,1},{6,2},{7,3},{8,4},{9,5},{1... | collective-permute-start | bytes 294920 | tf_op jit(solution)/shard_map/sum_gram/ppermute | solution.py:25
  47.9 1.3 collective-permute-start.18
  49.3 2.0 %add_convert_fusion = bf16[8,256,512]{2,1,0:T(8,128)(2,1)} fusion(bf16[8,256,512]{2,1,0:T(8,128)(2,1)S(1)} %collective-permute-done.21, bf16[8,256,512]{2,1,0:T(8,128)(2,1)S(1)} %get-tuple-element.52), kind=kLoop, calls=%fused_computation | loop fusion | flops 4194304 | bytes 6291456 | tf_op jit(solution)/shard_map/sum_cores/convert_element_type | solution.py:310
  51.2 4.3 %collective-permute-done.19 = f32[192,128]{1,0:T(8,128)S(1)} collective-permute-done((f32[192,128]{1,0:T(8,128)S(1)}, f32[192,128]{1,0:T(8,128)S(1)}, u32[]{:S(2)}, u32[]{:S(2)}) %collective-permute-start.19) | collective-permute-done | bytes 98336 | tf_op jit(solution)/shard_map/sum_gram/ppermute | solution.py:25
  55.6 3.6 %all-to-all-start = ((bf16[8,256,512]{2,1,0:T(8,128)(2,1)}), bf16[8,256,512]{2,1,0:T(8,128)(2,1)S(1)}, u32[]{:S(2)}, u32[]{:S(2)}) async-start(bf16[8,256,512]{2,1,0:T(8,128)(2,1)} %add_convert_fusion), calls=%async_computation | async-start | bytes 4194304 | tf_op jit(solution)/shard_map/sum_fsdp/all_to_all | solution.py:315
  59.2 1.0 collective-permute-start.22
  60.2 0.9 collective-permute-done.22.theirs
  61.1 11.3 %inverse.1 = f32[256,256]{1,0:T(8,128)S(1)} custom-call(s32[20]{0:T(128)S(1)} %stack.97.place, f32[192,128]{1,0:T(8,128)S(1)} %add_add_fusion.mine, f32[192,128]{1,0:T(8,128)S(1)} %collective-permute-done.22.theirs), custom_call_target="tpu_custom_call" | custom-call | flops 3000000000 | bytes 4194304 | tf_op jit(solution)/shard_map/inverse/pallas_call | solution.py:45
  73.1 2.0 %collective-permute-start.23 = (bf16[512,256]{1,0:T(8,128)(2,1)S(1)}, bf16[512,256]{1,0:T(8,128)(2,1)S(1)}, u32[]{:S(2)}, u32[]{:S(2)}) collective-permute-start(bf16[512,256]{1,0:T(8,128)(2,1)S(1)} %basis.1), channel_id=1, source_target_pairs={{0,16},{1,17},{2,18},{3,19},{4,20},{5,21},{6,22},{7,23},{8,24},{9,... | collective-permute-start | bytes 786440 | tf_op jit(solution)/shard_map/gather_basis/ppermute | solution.py:25
  75.2 10.1 %all-to-all-done.parts = bf16[8,256,512]{2,1,0:T(8,128)(2,1)S(1)} async-done(((bf16[8,256,512]{2,1,0:T(8,128)(2,1)}), bf16[8,256,512]{2,1,0:T(8,128)(2,1)S(1)}, u32[]{:S(2)}, u32[]{:S(2)}) %all-to-all-start) | async-done | bytes 2097184 | tf_op jit(solution)/shard_map/sum_fsdp/all_to_all | solution.py:315
  85.3 1.5 %coef.1 = (bf16[256,128]{1,0:T(8,128)(2,1)S(1)}, bf16[256,128]{1,0:T(8,128)(2,1)S(1)}, bf16[256,128]{1,0:T(8,128)(2,1)S(1)}, bf16[256,128]{1,0:T(8,128)(2,1)S(1)}) custom-call(s32[20]{0:T(128)S(1)} %stack.97.place, f32[256,256]{1,0:T(8,128)S(1)} %inverse.1, bf16[8,256,512]{2,1,0:T(8,128)(2,1)S(1)} %all-to-all-done.parts), custom_call_target="tpu_custom_call" | custom-call | flops 400000000 | bytes 4194304 | tf_op jit(solution)/shard_map/coef/pallas_call | solution.py:45
  86.8 2.8 %collective-permute-done.23 = bf16[512,256]{1,0:T(8,128)(2,1)S(1)} collective-permute-done((bf16[512,256]{1,0:T(8,128)(2,1)S(1)}, bf16[512,256]{1,0:T(8,128)(2,1)S(1)}, u32[]{:S(2)}, u32[]{:S(2)}) %collective-permute-start.23) | collective-permute-done | bytes 262176 | tf_op jit(solution)/shard_map/gather_basis/ppermute | solution.py:25
  89.7 4.5 %collective-permute-start.24 = (bf16[256,128]{1,0:T(8,128)(2,1)S(1)}, bf16[256,128]{1,0:T(8,128)(2,1)S(1)}, u32[]{:S(2)}, u32[]{:S(2)}) collective-permute-start(bf16[256,128]{1,0:T(8,128)(2,1)S(1)} %get-tuple-element.65), channel_id=1, source_target_pairs={{0,0},{1,16},{2,2},{3,18},{4,4},{5,20},{6,6},{7,22},{8,8},{9,24},{... | collective-permute-start | bytes 196616 | tf_op jit(solution)/shard_map/exchange_coef/ppermute | solution.py:25
  94.2 1.7 %collective-permute-start.25 = (bf16[256,128]{1,0:T(8,128)(2,1)S(1)}, bf16[256,128]{1,0:T(8,128)(2,1)S(1)}, u32[]{:S(2)}, u32[]{:S(2)}) collective-permute-start(bf16[256,128]{1,0:T(8,128)(2,1)S(1)} %get-tuple-element.66), channel_id=1, source_target_pairs={{0,32},{1,48},{2,34},{3,50},{4,36},{5,52},{6,38},{7,54},{8,40},{9,... | collective-permute-start | bytes 196616 | tf_op jit(solution)/shard_map/exchange_coef/ppermute | solution.py:25
  95.8 4.8 %collective-permute-start.26 = (bf16[256,128]{1,0:T(8,128)(2,1)S(1)}, bf16[256,128]{1,0:T(8,128)(2,1)S(1)}, u32[]{:S(2)}, u32[]{:S(2)}) collective-permute-start(bf16[256,128]{1,0:T(8,128)(2,1)S(1)} %get-tuple-element.67), channel_id=1, source_target_pairs={{0,64},{1,80},{2,66},{3,82},{4,68},{5,84},{6,70},{7,86},{8,72},{9,... | collective-permute-start | bytes 196616 | tf_op jit(solution)/shard_map/exchange_coef/ppermute | solution.py:25
  100.6 1.5 %collective-permute-start.27 = (bf16[256,128]{1,0:T(8,128)(2,1)S(1)}, bf16[256,128]{1,0:T(8,128)(2,1)S(1)}, u32[]{:S(2)}, u32[]{:S(2)}) collective-permute-start(bf16[256,128]{1,0:T(8,128)(2,1)S(1)} %get-tuple-element.68), channel_id=1, source_target_pairs={{0,96},{1,112},{2,98},{3,114},{4,100},{5,116},{6,102},{7,118},{8,1... | collective-permute-start | bytes 196616 | tf_op jit(solution)/shard_map/exchange_coef/ppermute | solution.py:25
  102.1 1.3 collective-permute-done.26.t2
  103.4 3.3 %collective-permute-done.27.t3 = bf16[256,128]{1,0:T(8,128)(2,1)S(1)} collective-permute-done((bf16[256,128]{1,0:T(8,128)(2,1)S(1)}, bf16[256,128]{1,0:T(8,128)(2,1)S(1)}, u32[]{:S(2)}, u32[]{:S(2)}) %collective-permute-start.27) | collective-permute-done | bytes 65568 | tf_op jit(solution)/shard_map/exchange_coef/ppermute | solution.py:25
  106.7 1.6 %spread.1 = bf16[8,1024,128]{2,1,0:T(8,128)(2,1)} custom-call(bf16[256,128]{1,0:T(8,128)(2,1)S(1)} %collective-permute-done.24.t0, bf16[256,128]{1,0:T(8,128)(2,1)S(1)} %collective-permute-done.25.t1, bf16[256,128]{1,0:T(8,128)(2,1)S(1)} %collective-permute-done.26.t2, bf16[256,128]{1,0:T(8,128)(2,1)S(1)} %collective-permute-done.27.t3), custom_call_target="tpu_custom_call" | custom-call | bytes 4194304 | tf_op jit(solution)/shard_map/spread/pallas_call | solution.py:45
  108.3 5.5 %all-to-all-start.1 = ((bf16[8,1024,128]{2,1,0:T(8,128)(2,1)}), bf16[8,1024,128]{2,1,0:T(8,128)(2,1)}, u32[]{:S(2)}, u32[]{:S(2)}) async-start(bf16[8,1024,128]{2,1,0:T(8,128)(2,1)} %spread.1), calls=%async_computation.1 | async-start | bytes 4194304 | tf_op jit(solution)/shard_map/gather_coef/all_to_all | solution.py:350
  113.8 2.5 %collective-permute-start.30 = (bf16[2,512,256]{2,1,0:T(8,128)(2,1)S(1)}, bf16[2,512,256]{2,1,0:T(8,128)(2,1)S(1)}, u32[]{:S(2)}, u32[]{:S(2)}) collective-permute-start(bf16[2,512,256]{2,1,0:T(8,128)(2,1)S(1)} %pad_maximum_fusion.q0), channel_id=1, source_target_pairs={{0,96},{1,97},{2,98},{3,99},{4,100},{5,101},{6,102},{7,103},{8,104... | collective-permute-start | bytes 1572872 | tf_op jit(solution)/shard_map/gather_basis/ppermute | solution.py:25
  116.3 8.4 %collective-permute-done.30.q3 = bf16[2,512,256]{2,1,0:T(8,128)(2,1)S(1)} collective-permute-done((bf16[2,512,256]{2,1,0:T(8,128)(2,1)S(1)}, bf16[2,512,256]{2,1,0:T(8,128)(2,1)S(1)}, u32[]{:S(2)}, u32[]{:S(2)}) %collective-permute-start.30) | collective-permute-done | bytes 524320 | tf_op jit(solution)/shard_map/gather_basis/ppermute | solution.py:25
  124.7 2.7 %collective-permute-start.31 = (bf16[512,256]{1,0:T(8,128)(2,1)S(1)}, bf16[512,256]{1,0:T(8,128)(2,1)S(1)}, u32[]{:S(2)}, u32[]{:S(2)}) collective-permute-start(bf16[512,256]{1,0:T(8,128)(2,1)S(1)} %slice_bitcast_fusion), channel_id=1, source_target_pairs={{0,96},{1,97},{2,98},{3,99},{4,100},{5,101},{6,102},{7,103},{8,104... | collective-permute-start | bytes 786440 | tf_op jit(solution)/shard_map/gather_basis/ppermute | solution.py:25
  127.5 3.2 %collective-permute-done.31 = bf16[512,256]{1,0:T(8,128)(2,1)S(1)} collective-permute-done((bf16[512,256]{1,0:T(8,128)(2,1)S(1)}, bf16[512,256]{1,0:T(8,128)(2,1)S(1)}, u32[]{:S(2)}, u32[]{:S(2)}) %collective-permute-start.31) | collective-permute-done | bytes 262176 | tf_op jit(solution)/shard_map/gather_basis/ppermute | solution.py:25
  130.7 3.2 %collective-permute-done.29 = bf16[512,256]{1,0:T(8,128)(2,1)S(1)} collective-permute-done((bf16[512,256]{1,0:T(8,128)(2,1)S(1)}, bf16[512,256]{1,0:T(8,128)(2,1)S(1)}, u32[]{:S(2)}, u32[]{:S(2)}) %collective-permute-start.29) | collective-permute-done | bytes 262176 | tf_op jit(solution)/shard_map/gather_basis/ppermute | solution.py:25
  134.9 3.0 %partial.1.part = f32[512,1024]{1,0:T(8,128)S(1)} custom-call(bf16[512,2048]{1,0:T(8,128)(2,1)S(1)} %lay.1.left, bf16[8,1024,128]{2,1,0:T(8,128)(2,1)} %all-to-all-done.1.mine), custom_call_target="tpu_custom_call" | custom-call | flops 1100000000 | bytes 4194304 | tf_op jit(solution)/shard_map/partial/pallas_call | solution.py:45
  137.9 1.4 collective-permute-done.32.theirs
  139.3 2.7 %update.1 = (f32[512,1024]{1,0:T(8,128)}, f32[512,1024]{1,0:T(8,128)}) custom-call(bf16[512,2048]{1,0:T(8,128)(2,1)S(1)} %lay.1.left, bf16[8,1024,128]{2,1,0:T(8,128)(2,1)S(1)} %collective-permute-done.32.theirs, f32[512,1024]{1,0:T(8,128)S(1)} %partial.1.part, f32[512,1024]{1,0:T(8,128)S(1)} %copy-done.2, f32[512,1024]{1,0:T(8,128)S(1)} %copy-done.3), custom_call_target="tpu_custom_call" | custom-call | flops 1100000000 | bytes 14000000 | tf_op jit(solution)/shard_map/update/pallas_call | solution.py:232
  (54 shorter events, 4.3 us)
Async XLA Ops:
  0.6 10.8 %collective-permute-start.2 = (bf16[512,256]{1,0:T(8,128)(2,1)}, bf16[512,256]{1,0:T(8,128)(2,1)S(1)}, u32[]{:S(2)}, u32[]{:S(2)}) collective-permute-start(bf16[512,256]{1,0:T(8,128)(2,1)} %refs_0_.1), channel_id=1, source_target_pairs={{0,8},{1,9},{2,10},{3,11},{4,12},{5,13},{6,14},{7,15},{8,0},{9,1},... | collective-permute-start | bytes 786440 | tf_op jit(solution)/shard_map/gather_sketch/ppermute | solution.py:25
  5.1 9.1 %collective-permute-start.7 = (bf16[512,256]{1,0:T(8,128)(2,1)}, bf16[512,256]{1,0:T(8,128)(2,1)S(1)}, u32[]{:S(2)}, u32[]{:S(2)}) collective-permute-start(bf16[512,256]{1,0:T(8,128)(2,1)} %refs_0_.1), channel_id=1, source_target_pairs={{0,2},{1,3},{2,16},{3,17},{4,6},{5,7},{6,20},{7,21},{8,10},{9,11},... | collective-permute-start | bytes 786440 | tf_op jit(solution)/shard_map/gather_sketch/ppermute | solution.py:25
  6.4 11.1 %collective-permute-start.1 = (bf16[512,256]{1,0:T(8,128)(2,1)}, bf16[512,256]{1,0:T(8,128)(2,1)S(1)}, u32[]{:S(2)}, u32[]{:S(2)}) collective-permute-start(bf16[512,256]{1,0:T(8,128)(2,1)} %refs_0_.1), channel_id=1, source_target_pairs={{0,12},{1,13},{2,14},{3,15},{4,0},{5,1},{6,2},{7,3},{8,4},{9,5},{1... | collective-permute-start | bytes 786440 | tf_op jit(solution)/shard_map/gather_sketch/ppermute | solution.py:25
  6.9 12.1 %collective-permute-start = (bf16[512,256]{1,0:T(8,128)(2,1)}, bf16[512,256]{1,0:T(8,128)(2,1)S(1)}, u32[]{:S(2)}, u32[]{:S(2)}) collective-permute-start(bf16[512,256]{1,0:T(8,128)(2,1)} %refs_0_.1), channel_id=1, source_target_pairs={{0,4},{1,5},{2,6},{3,7},{4,8},{5,9},{6,10},{7,11},{8,12},{9,13},{1... | collective-permute-start | bytes 786440 | tf_op jit(solution)/shard_map/gather_sketch/ppermute | solution.py:25
  11.4 7.6 %collective-permute-start.4 = (bf16[256,256]{1,0:T(8,128)(2,1)S(1)}, bf16[256,256]{1,0:T(8,128)(2,1)S(1)}, u32[]{:S(2)}, u32[]{:S(2)}) collective-permute-start(bf16[256,256]{1,0:T(8,128)(2,1)S(1)} %get-tuple-element.72), channel_id=1, source_target_pairs={{0,18},{1,19},{2,0},{3,1},{4,22},{5,23},{6,4},{7,5},{8,26},{9,27},... | collective-permute-start | bytes 393224 | tf_op jit(solution)/shard_map/gather_sketch/ppermute | solution.py:25
  14.2 5.3 %collective-permute-start.3 = (bf16[256,256]{1,0:T(8,128)(2,1)S(1)}, bf16[256,256]{1,0:T(8,128)(2,1)S(1)}, u32[]{:S(2)}, u32[]{:S(2)}) collective-permute-start(bf16[256,256]{1,0:T(8,128)(2,1)S(1)} %get-tuple-element.73), channel_id=1, source_target_pairs={{0,2},{1,3},{2,16},{3,17},{4,6},{5,7},{6,20},{7,21},{8,10},{9,11},... | collective-permute-start | bytes 393224 | tf_op jit(solution)/shard_map/gather_sketch/ppermute | solution.py:25
  14.2 8.5 %collective-permute-start.8 = (bf16[512,256]{1,0:T(8,128)(2,1)}, bf16[512,256]{1,0:T(8,128)(2,1)S(1)}, u32[]{:S(2)}, u32[]{:S(2)}) collective-permute-start(bf16[512,256]{1,0:T(8,128)(2,1)} %refs_0_.1), channel_id=1, source_target_pairs={{0,1},{1,0},{2,3},{3,2},{4,5},{5,4},{6,7},{7,6},{8,9},{9,8},{10,11... | collective-permute-start | bytes 786440 | tf_op jit(solution)/shard_map/gather_sketch/ppermute | solution.py:25
  17.6 5.4 %collective-permute-start.12 = (bf16[512,256]{1,0:T(8,128)(2,1)S(1)}, bf16[512,256]{1,0:T(8,128)(2,1)S(1)}, u32[]{:S(2)}, u32[]{:S(2)}) collective-permute-start(bf16[512,256]{1,0:T(8,128)(2,1)S(1)} %collective-permute-done.2.refs_4_), channel_id=1, source_target_pairs={{0,1},{1,0},{2,3},{3,2},{4,5},{5,4},{6,7},{7,6},{8,9},{9,8},{10,11... | collective-permute-start | bytes 786440 | tf_op jit(solution)/shard_map/gather_sketch/ppermute | solution.py:25
  19.0 3.9 %collective-permute-start.11 = (bf16[512,256]{1,0:T(8,128)(2,1)S(1)}, bf16[512,256]{1,0:T(8,128)(2,1)S(1)}, u32[]{:S(2)}, u32[]{:S(2)}) collective-permute-start(bf16[512,256]{1,0:T(8,128)(2,1)S(1)} %collective-permute-done.7.refs_3_), channel_id=1, source_target_pairs={{0,1},{1,0},{2,3},{3,2},{4,5},{5,4},{6,7},{7,6},{8,9},{9,8},{10,11... | collective-permute-start | bytes 786440 | tf_op jit(solution)/shard_map/gather_sketch/ppermute | solution.py:25
  19.0 6.7 %collective-permute-start.10 = (bf16[512,256]{1,0:T(8,128)(2,1)S(1)}, bf16[512,256]{1,0:T(8,128)(2,1)S(1)}, u32[]{:S(2)}, u32[]{:S(2)}) collective-permute-start(bf16[512,256]{1,0:T(8,128)(2,1)S(1)} %collective-permute-done.1.refs_2_), channel_id=1, source_target_pairs={{0,1},{1,0},{2,3},{3,2},{4,5},{5,4},{6,7},{7,6},{8,9},{9,8},{10,11... | collective-permute-start | bytes 786440 | tf_op jit(solution)/shard_map/gather_sketch/ppermute | solution.py:25
  19.5 6.2 %collective-permute-start.9 = (bf16[512,256]{1,0:T(8,128)(2,1)S(1)}, bf16[512,256]{1,0:T(8,128)(2,1)S(1)}, u32[]{:S(2)}, u32[]{:S(2)}) collective-permute-start(bf16[512,256]{1,0:T(8,128)(2,1)S(1)} %collective-permute-done.refs_1_), channel_id=1, source_target_pairs={{0,1},{1,0},{2,3},{3,2},{4,5},{5,4},{6,7},{7,6},{8,9},{9,8},{10,11... | collective-permute-start | bytes 786440 | tf_op jit(solution)/shard_map/gather_sketch/ppermute | solution.py:25
  22.8 3.0 %collective-permute-start.13 = (bf16[512,256]{1,0:T(8,128)(2,1)S(1)}, bf16[512,256]{1,0:T(8,128)(2,1)S(1)}, u32[]{:S(2)}, u32[]{:S(2)}) collective-permute-start(bf16[512,256]{1,0:T(8,128)(2,1)S(1)} %constant_dynamic-update-slice_fusion.refs_5_), channel_id=1, source_target_pairs={{0,1},{1,0},{2,3},{3,2},{4,5},{5,4},{6,7},{7,6},{8,9},{9,8},{10,11... | collective-permute-start | bytes 786440 | tf_op jit(solution)/shard_map/gather_sketch/ppermute | solution.py:25
  22.9 9.6 %collective-permute-start.5 = (bf16[512,256]{1,0:T(8,128)(2,1)S(1)}, bf16[512,256]{1,0:T(8,128)(2,1)S(1)}, u32[]{:S(2)}, u32[]{:S(2)}) collective-permute-start(bf16[512,256]{1,0:T(8,128)(2,1)S(1)} %collective-permute-done.refs_1_), channel_id=1, source_target_pairs={{0,2},{1,3},{2,16},{3,17},{4,6},{5,7},{6,20},{7,21},{8,10},{9,11},... | collective-permute-start | bytes 786440 | tf_op jit(solution)/shard_map/gather_sketch/ppermute | solution.py:25
  23.0 9.5 %collective-permute-start.6 = (bf16[512,256]{1,0:T(8,128)(2,1)S(1)}, bf16[512,256]{1,0:T(8,128)(2,1)S(1)}, u32[]{:S(2)}, u32[]{:S(2)}) collective-permute-start(bf16[512,256]{1,0:T(8,128)(2,1)S(1)} %collective-permute-done.1.refs_2_), channel_id=1, source_target_pairs={{0,18},{1,19},{2,0},{3,1},{4,22},{5,23},{6,4},{7,5},{8,26},{9,27},... | collective-permute-start | bytes 786440 | tf_op jit(solution)/shard_map/gather_sketch/ppermute | solution.py:25
  25.8 3.4 %copy-start = (bf16[1,512,8192]{2,1,0:T(8,128)(2,1)S(1)}, bf16[1,512,8192]{2,1,0:T(8,128)(2,1)}, u32[]{:S(2)}) copy-start(bf16[1,512,8192]{2,1,0:T(8,128)(2,1)} %param.4) | copy-start | bytes 25165828
  29.2 0.9 copy-start.4
  32.5 6.7 %copy-start.1 = (bf16[1,512,8192]{2,1,0:T(8,128)(2,1)S(1)}, bf16[1,512,8192]{2,1,0:T(8,128)(2,1)}, u32[]{:S(2)}) copy-start(bf16[1,512,8192]{2,1,0:T(8,128)(2,1)} %param.4) | copy-start | bytes 25165828
  32.5 2.2 %collective-permute-start.14 = (bf16[512,256]{1,0:T(8,128)(2,1)S(1)}, bf16[512,256]{1,0:T(8,128)(2,1)S(1)}, u32[]{:S(2)}, u32[]{:S(2)}) collective-permute-start(bf16[512,256]{1,0:T(8,128)(2,1)S(1)} %collective-permute-done.5.refs_0_), channel_id=1, source_target_pairs={{0,1},{1,0},{2,3},{3,2},{4,5},{5,4},{6,7},{7,6},{8,9},{9,8},{10,11... | collective-permute-start | bytes 786440 | tf_op jit(solution)/shard_map/gather_sketch/ppermute | solution.py:25
  33.6 1.5 %collective-permute-start.15 = (bf16[512,256]{1,0:T(8,128)(2,1)S(1)}, bf16[512,256]{1,0:T(8,128)(2,1)S(1)}, u32[]{:S(2)}, u32[]{:S(2)}) collective-permute-start(bf16[512,256]{1,0:T(8,128)(2,1)S(1)} %collective-permute-done.6.refs_1_), channel_id=1, source_target_pairs={{0,1},{1,0},{2,3},{3,2},{4,5},{5,4},{6,7},{7,6},{8,9},{9,8},{10,11... | collective-permute-start | bytes 786440 | tf_op jit(solution)/shard_map/gather_sketch/ppermute | solution.py:25
  37.7 1.4 collective-permute-start.16
  39.1 4.1 %collective-permute-start.17 = (f32[192,128]{1,0:T(8,128)S(1)}, f32[192,128]{1,0:T(8,128)S(1)}, u32[]{:S(2)}, u32[]{:S(2)}) collective-permute-start(f32[192,128]{1,0:T(8,128)S(1)} %add.168), channel_id=1, source_target_pairs={{0,2},{1,3},{2,0},{3,1},{4,6},{5,7},{6,4},{7,5},{8,10},{9,11},{10,... | collective-permute-start | bytes 294920 | tf_op jit(solution)/shard_map/sum_gram/ppermute | solution.py:25
  43.2 6.0 %collective-permute-start.21 = (bf16[8,256,512]{2,1,0:T(8,128)(2,1)S(1)}, bf16[8,256,512]{2,1,0:T(8,128)(2,1)S(1)}, u32[]{:S(2)}, u32[]{:S(2)}) collective-permute-start(bf16[8,256,512]{2,1,0:T(8,128)(2,1)S(1)} %get-tuple-element.53), channel_id=1, source_target_pairs={{0,1},{1,0},{2,3},{3,2},{4,5},{5,4},{6,7},{7,6},{8,9},{9,8},{10,11... | collective-permute-start | bytes 6291464 | tf_op jit(solution)/shard_map/sum_cores/ppermute | solution.py:25
  44.4 6.8 %collective-permute-start.20 = (f32[192,128]{1,0:T(8,128)S(1)}, f32[192,128]{1,0:T(8,128)S(1)}, u32[]{:S(2)}, u32[]{:S(2)}) collective-permute-start(f32[192,128]{1,0:T(8,128)S(1)} %add.169), channel_id=1, source_target_pairs={{0,12},{1,13},{2,14},{3,15},{4,0},{5,1},{6,2},{7,3},{8,4},{9,5},{1... | collective-permute-start | bytes 294920 | tf_op jit(solution)/shard_map/sum_gram/ppermute | solution.py:25
  47.9 7.7 %collective-permute-start.19 = (f32[192,128]{1,0:T(8,128)S(1)}, f32[192,128]{1,0:T(8,128)S(1)}, u32[]{:S(2)}, u32[]{:S(2)}) collective-permute-start(f32[192,128]{1,0:T(8,128)S(1)} %add.169), channel_id=1, source_target_pairs={{0,4},{1,5},{2,6},{3,7},{4,8},{5,9},{6,10},{7,11},{8,12},{9,13},{1... | collective-permute-start | bytes 294920 | tf_op jit(solution)/shard_map/sum_gram/ppermute | solution.py:25
  47.9 7.7 %collective-permute-start.18 = (f32[192,128]{1,0:T(8,128)S(1)}, f32[192,128]{1,0:T(8,128)S(1)}, u32[]{:S(2)}, u32[]{:S(2)}) collective-permute-start(f32[192,128]{1,0:T(8,128)S(1)} %add.169), channel_id=1, source_target_pairs={{0,8},{1,9},{2,10},{3,11},{4,12},{5,13},{6,14},{7,15},{8,0},{9,1},... | collective-permute-start | bytes 294920 | tf_op jit(solution)/shard_map/sum_gram/ppermute | solution.py:25
  55.6 29.7 %all-to-all-start = ((bf16[8,256,512]{2,1,0:T(8,128)(2,1)}), bf16[8,256,512]{2,1,0:T(8,128)(2,1)S(1)}, u32[]{:S(2)}, u32[]{:S(2)}) async-start(bf16[8,256,512]{2,1,0:T(8,128)(2,1)} %add_convert_fusion), calls=%async_computation | async-start | bytes 4194304 | tf_op jit(solution)/shard_map/sum_fsdp/all_to_all | solution.py:315
  59.2 1.9 %collective-permute-start.22 = (f32[192,128]{1,0:T(8,128)S(1)}, f32[192,128]{1,0:T(8,128)S(1)}, u32[]{:S(2)}, u32[]{:S(2)}) collective-permute-start(f32[192,128]{1,0:T(8,128)S(1)} %add_add_fusion.mine), channel_id=1, source_target_pairs={{0,1},{1,0},{2,3},{3,2},{4,5},{5,4},{6,7},{7,6},{8,9},{9,8},{10,11... | collective-permute-start | bytes 294920 | tf_op jit(solution)/shard_map/sum_gram/ppermute | solution.py:25
  73.1 16.5 %collective-permute-start.23 = (bf16[512,256]{1,0:T(8,128)(2,1)S(1)}, bf16[512,256]{1,0:T(8,128)(2,1)S(1)}, u32[]{:S(2)}, u32[]{:S(2)}) collective-permute-start(bf16[512,256]{1,0:T(8,128)(2,1)S(1)} %basis.1), channel_id=1, source_target_pairs={{0,16},{1,17},{2,18},{3,19},{4,20},{5,21},{6,22},{7,23},{8,24},{9,... | collective-permute-start | bytes 786440 | tf_op jit(solution)/shard_map/gather_basis/ppermute | solution.py:25
  89.7 12.4 %collective-permute-start.24 = (bf16[256,128]{1,0:T(8,128)(2,1)S(1)}, bf16[256,128]{1,0:T(8,128)(2,1)S(1)}, u32[]{:S(2)}, u32[]{:S(2)}) collective-permute-start(bf16[256,128]{1,0:T(8,128)(2,1)S(1)} %get-tuple-element.65), channel_id=1, source_target_pairs={{0,0},{1,16},{2,2},{3,18},{4,4},{5,20},{6,6},{7,22},{8,8},{9,24},{... | collective-permute-start | bytes 196616 | tf_op jit(solution)/shard_map/exchange_coef/ppermute | solution.py:25
  94.2 8.0 %collective-permute-start.25 = (bf16[256,128]{1,0:T(8,128)(2,1)S(1)}, bf16[256,128]{1,0:T(8,128)(2,1)S(1)}, u32[]{:S(2)}, u32[]{:S(2)}) collective-permute-start(bf16[256,128]{1,0:T(8,128)(2,1)S(1)} %get-tuple-element.66), channel_id=1, source_target_pairs={{0,32},{1,48},{2,34},{3,50},{4,36},{5,52},{6,38},{7,54},{8,40},{9,... | collective-permute-start | bytes 196616 | tf_op jit(solution)/shard_map/exchange_coef/ppermute | solution.py:25
  95.8 7.6 %collective-permute-start.26 = (bf16[256,128]{1,0:T(8,128)(2,1)S(1)}, bf16[256,128]{1,0:T(8,128)(2,1)S(1)}, u32[]{:S(2)}, u32[]{:S(2)}) collective-permute-start(bf16[256,128]{1,0:T(8,128)(2,1)S(1)} %get-tuple-element.67), channel_id=1, source_target_pairs={{0,64},{1,80},{2,66},{3,82},{4,68},{5,84},{6,70},{7,86},{8,72},{9,... | collective-permute-start | bytes 196616 | tf_op jit(solution)/shard_map/exchange_coef/ppermute | solution.py:25
  100.6 6.1 %collective-permute-start.27 = (bf16[256,128]{1,0:T(8,128)(2,1)S(1)}, bf16[256,128]{1,0:T(8,128)(2,1)S(1)}, u32[]{:S(2)}, u32[]{:S(2)}) collective-permute-start(bf16[256,128]{1,0:T(8,128)(2,1)S(1)} %get-tuple-element.68), channel_id=1, source_target_pairs={{0,96},{1,112},{2,98},{3,114},{4,100},{5,116},{6,102},{7,118},{8,1... | collective-permute-start | bytes 196616 | tf_op jit(solution)/shard_map/exchange_coef/ppermute | solution.py:25
  108.3 26.7 %all-to-all-start.1 = ((bf16[8,1024,128]{2,1,0:T(8,128)(2,1)}), bf16[8,1024,128]{2,1,0:T(8,128)(2,1)}, u32[]{:S(2)}, u32[]{:S(2)}) async-start(bf16[8,1024,128]{2,1,0:T(8,128)(2,1)} %spread.1), calls=%async_computation.1 | async-start | bytes 4194304 | tf_op jit(solution)/shard_map/gather_coef/all_to_all | solution.py:350
  113.8 10.8 %collective-permute-start.30 = (bf16[2,512,256]{2,1,0:T(8,128)(2,1)S(1)}, bf16[2,512,256]{2,1,0:T(8,128)(2,1)S(1)}, u32[]{:S(2)}, u32[]{:S(2)}) collective-permute-start(bf16[2,512,256]{2,1,0:T(8,128)(2,1)S(1)} %pad_maximum_fusion.q0), channel_id=1, source_target_pairs={{0,96},{1,97},{2,98},{3,99},{4,100},{5,101},{6,102},{7,103},{8,104... | collective-permute-start | bytes 1572872 | tf_op jit(solution)/shard_map/gather_basis/ppermute | solution.py:25
  116.3 11.1 %collective-permute-start.28 = (bf16[2,512,256]{2,1,0:T(8,128)(2,1)S(1)}, bf16[2,512,256]{2,1,0:T(8,128)(2,1)S(1)}, u32[]{:S(2)}, u32[]{:S(2)}) collective-permute-start(bf16[2,512,256]{2,1,0:T(8,128)(2,1)S(1)} %pad_maximum_fusion.q0), channel_id=1, source_target_pairs={{0,32},{1,33},{2,34},{3,35},{4,36},{5,37},{6,38},{7,39},{8,40},{9,... | collective-permute-start | bytes 1572872 | tf_op jit(solution)/shard_map/gather_basis/ppermute | solution.py:25
  124.7 6.0 %collective-permute-start.31 = (bf16[512,256]{1,0:T(8,128)(2,1)S(1)}, bf16[512,256]{1,0:T(8,128)(2,1)S(1)}, u32[]{:S(2)}, u32[]{:S(2)}) collective-permute-start(bf16[512,256]{1,0:T(8,128)(2,1)S(1)} %slice_bitcast_fusion), channel_id=1, source_target_pairs={{0,96},{1,97},{2,98},{3,99},{4,100},{5,101},{6,102},{7,103},{8,104... | collective-permute-start | bytes 786440 | tf_op jit(solution)/shard_map/gather_basis/ppermute | solution.py:25
  127.4 6.5 %collective-permute-start.29 = (bf16[512,256]{1,0:T(8,128)(2,1)S(1)}, bf16[512,256]{1,0:T(8,128)(2,1)S(1)}, u32[]{:S(2)}, u32[]{:S(2)}) collective-permute-start(bf16[512,256]{1,0:T(8,128)(2,1)S(1)} %slice_bitcast_fusion.1), channel_id=1, source_target_pairs={{0,32},{1,33},{2,34},{3,35},{4,36},{5,37},{6,38},{7,39},{8,40},{9,... | collective-permute-start | bytes 786440 | tf_op jit(solution)/shard_map/gather_basis/ppermute | solution.py:25
  134.9 4.4 %copy-start.2 = (f32[512,1024]{1,0:T(8,128)S(1)}, f32[512,1024]{1,0:T(8,128)}, u32[]{:S(2)}) copy-start(f32[512,1024]{1,0:T(8,128)} %params.1) | copy-start | bytes 6291460
  134.9 4.4 %copy-start.3 = (f32[512,1024]{1,0:T(8,128)S(1)}, f32[512,1024]{1,0:T(8,128)}, u32[]{:S(2)}) copy-start(f32[512,1024]{1,0:T(8,128)} %momentum.1) | copy-start | bytes 6291460
  134.9 4.4 %collective-permute-start.32 = (bf16[8,1024,128]{2,1,0:T(8,128)(2,1)}, bf16[8,1024,128]{2,1,0:T(8,128)(2,1)S(1)}, u32[]{:S(2)}, u32[]{:S(2)}) collective-permute-start(bf16[8,1024,128]{2,1,0:T(8,128)(2,1)} %all-to-all-done.1.mine), channel_id=1, source_target_pairs={{0,1},{1,0},{2,3},{3,2},{4,5},{5,4},{6,7},{7,6},{8,9},{9,8},{10,11... | collective-permute-start | bytes 6291464 | tf_op jit(solution)/shard_map/gather_coef/ppermute | solution.py:25

commit v5 on v4

--- a/solution.py
+++ b/solution.py
@@ -79,12 +79,12 @@
 
 def late_kernel(layout, place, delta, *refs):
     pieces, part = refs[: len(layout)], refs[len(layout)]
-    mine, theirs, sketched, turned, out = refs[len(layout) + 1 :]
+    mine, theirs, rounded, turned, out = refs[len(layout) + 1 :]
     add_products(layout, place, delta, pieces, out)
     total = out[...] + part[...]
     flipped = total.T
     gram = jnp.dot(flipped, total, precision=HIGH, preferred_element_type=F32)
-    sketched[...] = total
+    rounded[...] = total.astype(BF16)
     turned[...] = flipped.astype(BF16)
     for core, to in ((0, (mine, theirs)), (1, (theirs, mine))):
 
@@ -109,11 +109,35 @@
                     out[4 * q + u, :, g * BLK : (g + 1) * BLK] = tile[:, u * BLK : (u + 1) * BLK]
 
 
-def spread_kernel(t0, t1, t2, t3, out):
-    rank = t0.shape[0]
-    for n in range(out.shape[0]):
-        for d, tile in enumerate((t0, t1, t2, t3)):
-            out[n, d * rank : (d + 1) * rank] = tile[...]
+def spread_kernel(first, *refs):
+    tiles, (out, sems) = refs[:2], refs[-2:]
+    rank = tiles[0].shape[0]
+    copies = [
+        pltpu.make_async_copy(
+            tile, out.at[n, (first + d) * rank : (first + d + 1) * rank], sems.at[d, n]
+        )
+        for n in range(out.shape[0])
+        for d, tile in enumerate(tiles)
+    ]
+    for copy in copies:
+        copy.start()
+    for copy in copies:
+        copy.wait()
+
+
+def spread_call(first, tiles, before=()):
+    rank = tiles[0].shape[0]
+    return pl.pallas_call(
+        functools.partial(spread_kernel, first),
+        in_specs=[VMEM, VMEM] + [FAR] * len(before),
+        out_specs=FAR,
+        out_shape=jax.ShapeDtypeStruct((8, 4 * rank, BLK), BF16),
+        scratch_shapes=[pltpu.SemaphoreType.DMA((2, 8))],
+        input_output_aliases={2: 0} if before else {},
+        compiler_params=pltpu.CompilerParams(vmem_limit_bytes=4 * 1024 * 1024),
+        cost_estimate=pl.CostEstimate(flops=0, bytes_accessed=1000000, transcendentals=0),
+        name="spread",
+    )(*tiles, *before)
 
 
 def inverse_kernel(place, mine, theirs, out, left):
@@ -177,23 +201,18 @@
         outs[d][...] = columns(held, (place[2] + d) % 4 * BLK, BLK)[...]
 
 
-def basis_kernel(sketched, inverse, out):
-    basis = lax.dot_general(
-        sketched[...],
-        inverse[...],
-        (((1,), (1,)), ((), ())),
-        precision=HIGH,
-        preferred_element_type=F32,
-    )
-    for b in range(2):
-        out[:, b * BLK : (b + 1) * BLK] = recode(basis[:, b * BLK : (b + 1) * BLK], 1)
-
-
-def lay_kernel(place, q0, q1, q2, q3, left):
-    rank = q0.shape[2]
-    for d, q in enumerate((q0, q1, q2, q3)):
-        left[:, d * rank : (d + 1) * rank] = q[place[3]]
-        left[:, (4 + d) * rank : (5 + d) * rank] = q[1 - place[3]]
+def basis_kernel(place, s0, s1, s2, s3, mine, theirs, left):
+    for d, sketched in enumerate((s0, s1, s2, s3)):
+        for n, yh in enumerate((place[3], 1 - place[3])):
+            for core, inverse in ((place[0], mine), (1 - place[0], theirs)):
+                basis = lax.dot_general(
+                    sketched[yh],
+                    inverse[d, yh],
+                    (((1,), (1,)), ((), ())),
+                    preferred_element_type=F32,
+                )
+                start = pl.multiple_of((2 * (4 * n + d) + core) * BLK, BLK)
+                left[:, pl.ds(start, BLK)] = recode(basis, 1)
 
 
 def partial_kernel(left, mine, out):
@@ -282,9 +301,9 @@
         pieces = [y1, y3]
         pieces += swap(pieces)
     gram_part = ((BLK + BLK // 2, BLK), F32)
-    mine, theirs, sketched, turned = call(
+    mine, theirs, rounded, turned = call(
         functools.partial(late_kernel, range(16, 20)),
-        [gram_part, gram_part, ((rows, rank), F32), ((rank, rows), BF16)],
+        [gram_part, gram_part, ((rows, rank), BF16), ((rank, rows), BF16)],
         8e8,
         "sketched_late",
         scratch=[pltpu.VMEM((rows, rank), F32)],
@@ -308,9 +327,14 @@
         got = [shift(mine, dz=d) for d in (2, 1, 3)]
     with jax.named_scope("sum_cores"):
         kept = (kept.astype(F32) + shift(sent, dc=1).astype(F32)).astype(BF16)
-    *got, kept = fence((*got, kept))
+    with jax.named_scope("gather_sketched"):
+        across = shift(rounded, dh=1)
+    *got, kept, across = fence((*got, kept, across))
     mine = (mine + got[0]) + (got[1] + got[2])
     mine, kept = fence((mine, kept))
+    with jax.named_scope("gather_sketched"):
+        both = jnp.stack([rounded, across])
+        right, left = shift(both, dx=1), shift(both, dx=-1)
     with jax.named_scope("sum_fsdp"):
         parts = lax.all_to_all(kept, ("z", "yl"), 0, 0, tiled=True)
 
@@ -323,9 +347,12 @@
         "inverse",
         scratch=[pltpu.VMEM((rank, rank), F32)],
     )(place, mine, theirs)[0]
-    basis = call(basis_kernel, [((rows, rank), BF16)], 4e8, "basis", False)(sketched, inverse)[0]
-    with jax.named_scope("gather_basis"):
-        across = shift(basis, dh=1)
+    inverse, right, left = fence((inverse, right, left))
+    with jax.named_scope("gather_sketched"):
+        far = [shift(right[0], dx=1), shift(left[1], dx=-1)]
+    with jax.named_scope("gather_inverse"):
+        half_inverse = lax.dynamic_slice_in_dim(inverse, core * BLK, BLK, 0).astype(BF16)
+        across = shift(half_inverse, dh=1)
     tiles = call(
         coef_kernel,
         [((rank, BLK), BF16)] * 4,
@@ -333,19 +360,21 @@
         "coef",
         scratch=[pltpu.VMEM((rank, 4 * BLK), BF16)],
     )(place, inverse, parts)
-    *tiles, across = fence((*tiles, across))
-    both = jnp.stack([basis, across])
-    with jax.named_scope("gather_basis"):
-        right, left = shift(both, dx=1), shift(both, dx=-1)
-        far = jnp.stack([shift(right[0], dx=1), shift(left[1], dx=-1)])
-    operand = call(lay_kernel, [((rows, 8 * rank), BF16)], 1e8, "lay")(
-        place, both, right, far, left
+    *tiles, across, far[0], far[1] = fence((*tiles, across, *far))
+    with jax.named_scope("gather_inverse"):
+        pair = jnp.stack([half_inverse, across])
+        inverses = jnp.stack([pair] + [shift(pair, dx=d) for d in range(1, 4)])
+        other = shift(inverses, dc=1)
+    operand = call(basis_kernel, [((rows, 8 * rank), BF16)], 5.4e8, "basis")(
+        place, both, right, jnp.stack(far), left, inverses, other
     )[0]
     with jax.named_scope("exchange_coef"):
         tiles = [
             move(v, lambda x, h, z, l, c, d=d: (x + d, c, z, l, h)) for d, v in enumerate(tiles)
         ]
-    tiles = call(spread_kernel, [pltpu.VMEM((8, 4 * rank, BLK), BF16)], 0, "spread", False)(*tiles)[0]
+    half = spread_call(0, tiles[:2])
+    *rest, half = fence((*tiles[2:], half))
+    tiles = spread_call(2, rest, (half,))
     with jax.named_scope("gather_coef"):
         mine, operand = fence((lax.all_to_all(tiles, ("z", "yl"), 0, 0, tiled=True), operand))
         theirs = shift(mine, dc=1)

time: 143 us -> 143 us (level)
  waiting for transfers between devices: 47.1 us -> 37.9 us
  local copies, waits for them, and re-layouts: 4.51 us -> 7.34 us
  starting transfers between devices: 57.9 us -> 60.7 us
  other arithmetic: 2.11 us -> 4.12 us
  Pallas kernels: 29.5 us -> 31 us
    ppermute x33 -> x38, waiting for transfers between devices: 36.8 us -> 24.5 us  [move(): return lax.ppermute(value, AXES, pairs)]
    all_to_all x1, waiting for transfers between devices: 0.18 us -> 10.7 us  [body(): lax.all_to_all(tiles, ('z', 'yl'), 0, 0, tiled=True)]
    all_to_all x1, waiting for transfers between devices: 10.1 us -> 2.71 us  [body(): parts = lax.all_to_all(kept, ('z', 'yl'), 0, 0, tiled=True)]
    ppermute x33 -> x38, starting transfers between devices: 48.8 us -> 52.6 us  [move(): return lax.ppermute(value, AXES, pairs)]
    pallas_call x0 -> x2, Pallas kernels: none -> 2.17 us  [spread_call(): pl.pallas_call(functools.partial(spread_kernel, first), in_specs=[VMEM, V...]
    another operation x2 -> x4, other arithmetic: 0.1 us -> 2.11 us  [the longest x1 1.08 us: body(): jnp.stack(far)]
    unnamed x11 -> x15, local copies, waits for them, and re-layouts: 4.35 us -> 5.15 us
    pallas_call x9 -> x7, Pallas kernels: 26.8 us -> 26.2 us  [run(): pl.pallas_call(kernel, in_specs=[SMEM] * smem + [VMEM] * (len(args) - sme...]
  transfers between devices with their start and end apart: 35 -> 40, of which waited for: 17 -> 18; matrix products, arithmetic and copies ran while one was open for 2% -> 4% of each run, Pallas kernels for 16% -> 17%
where the time goes in v5:
time: 143 us; the launch traced here: 142 us
  starting transfers between devices  60.7 us (42%)
  waiting for transfers between devices  37.9 us (27%)
  Pallas kernels  31 us (22%)
  local copies, waits for them, and re-layouts  7.34 us (5%)
  other arithmetic  4.12 us (3%)
    ppermute x38, starting transfers between devices, move(): return lax.ppermute(value, AXES, pairs)  52.6 us
    pallas_call x7, Pallas kernels, run(): pl.pallas_call(kernel, in_specs=[SMEM] * smem + [VMEM] * (len(args) - sme...  26.2 us
    ppermute x38, waiting for transfers between devices, move(): return lax.ppermute(value, AXES, pairs)  24.5 us
    all_to_all x1, waiting for transfers between devices, body(): lax.all_to_all(tiles, ('z', 'yl'), 0, 0, tiled=True)  10.7 us
    unnamed x15, local copies, waits for them, and re-layouts  5.15 us
    all_to_all x1, starting transfers between devices, body(): lax.all_to_all(tiles, ('z', 'yl'), 0, 0, tiled=True)  4.48 us
    all_to_all x1, starting transfers between devices, body(): parts = lax.all_to_all(kept, ('z', 'yl'), 0, 0, tiled=True)  3.62 us
  transfers between devices with their start and end apart: 40, of which 18 were waited for; matrix products, arithmetic and copies ran while one was open for 4% of the time, Pallas kernels for 17%

profile of v5, /device:TPU:1, one launch (start us, length us, event | category | flops | bytes accessed | tf_op | source)
XLA Modules:
  0.0 142.2 jit_solution(5085695754604847511)
XLA Ops:
  0.6 4.5 %collective-permute-start.2 = (bf16[512,256]{1,0:T(8,128)(2,1)}, bf16[512,256]{1,0:T(8,128)(2,1)S(1)}, u32[]{:S(2)}, u32[]{:S(2)}) collective-permute-start(bf16[512,256]{1,0:T(8,128)(2,1)} %refs_0_.1), channel_id=1, source_target_pairs={{0,8},{1,9},{2,10},{3,11},{4,12},{5,13},{6,14},{7,15},{8,0},{9,1},... | collective-permute-start | bytes 786440 | tf_op jit(solution)/shard_map/gather_sketch/ppermute | solution.py:25
  5.1 1.3 collective-permute-start.7
  7.9 3.5 %collective-permute-done.2.refs_4_ = bf16[512,256]{1,0:T(8,128)(2,1)S(1)} collective-permute-done((bf16[512,256]{1,0:T(8,128)(2,1)}, bf16[512,256]{1,0:T(8,128)(2,1)S(1)}, u32[]{:S(2)}, u32[]{:S(2)}) %collective-permute-start.2) | collective-permute-done | bytes 262176 | tf_op jit(solution)/shard_map/gather_sketch/ppermute | solution.py:25
  11.4 2.8 %collective-permute-start.4 = (bf16[256,256]{1,0:T(8,128)(2,1)S(1)}, bf16[256,256]{1,0:T(8,128)(2,1)S(1)}, u32[]{:S(2)}, u32[]{:S(2)}) collective-permute-start(bf16[256,256]{1,0:T(8,128)(2,1)S(1)} %get-tuple-element.90), channel_id=1, source_target_pairs={{0,18},{1,19},{2,0},{3,1},{4,22},{5,23},{6,4},{7,5},{8,26},{9,27},... | collective-permute-start | bytes 393224 | tf_op jit(solution)/shard_map/gather_sketch/ppermute | solution.py:25
  14.2 2.3 %collective-permute-start.8 = (bf16[512,256]{1,0:T(8,128)(2,1)}, bf16[512,256]{1,0:T(8,128)(2,1)S(1)}, u32[]{:S(2)}, u32[]{:S(2)}) collective-permute-start(bf16[512,256]{1,0:T(8,128)(2,1)} %refs_0_.1), channel_id=1, source_target_pairs={{0,1},{1,0},{2,3},{3,2},{4,5},{5,4},{6,7},{7,6},{8,9},{9,8},{10,11... | collective-permute-start | bytes 786440 | tf_op jit(solution)/shard_map/gather_sketch/ppermute | solution.py:25
  17.6 1.4 %collective-permute-start.12 = (bf16[512,256]{1,0:T(8,128)(2,1)S(1)}, bf16[512,256]{1,0:T(8,128)(2,1)S(1)}, u32[]{:S(2)}, u32[]{:S(2)}) collective-permute-start(bf16[512,256]{1,0:T(8,128)(2,1)S(1)} %collective-permute-done.2.refs_4_), channel_id=1, source_target_pairs={{0,1},{1,0},{2,3},{3,2},{4,5},{5,4},{6,7},{7,6},{8,9},{9,8},{10,11... | collective-permute-start | bytes 786440 | tf_op jit(solution)/shard_map/gather_sketch/ppermute | solution.py:25
  19.5 3.2 %collective-permute-start.9 = (bf16[512,256]{1,0:T(8,128)(2,1)S(1)}, bf16[512,256]{1,0:T(8,128)(2,1)S(1)}, u32[]{:S(2)}, u32[]{:S(2)}) collective-permute-start(bf16[512,256]{1,0:T(8,128)(2,1)S(1)} %collective-permute-done.refs_1_), channel_id=1, source_target_pairs={{0,1},{1,0},{2,3},{3,2},{4,5},{5,4},{6,7},{7,6},{8,9},{9,8},{10,11... | collective-permute-start | bytes 786440 | tf_op jit(solution)/shard_map/gather_sketch/ppermute | solution.py:25
  23.0 2.7 %collective-permute-start.6 = (bf16[512,256]{1,0:T(8,128)(2,1)S(1)}, bf16[512,256]{1,0:T(8,128)(2,1)S(1)}, u32[]{:S(2)}, u32[]{:S(2)}) collective-permute-start(bf16[512,256]{1,0:T(8,128)(2,1)S(1)} %collective-permute-done.1.refs_2_), channel_id=1, source_target_pairs={{0,18},{1,19},{2,0},{3,1},{4,22},{5,23},{6,4},{7,5},{8,26},{9,27},... | collective-permute-start | bytes 786440 | tf_op jit(solution)/shard_map/gather_sketch/ppermute | solution.py:25
  25.8 3.4 %copy-done = bf16[1,512,8192]{2,1,0:T(8,128)(2,1)S(1)} copy-done((bf16[1,512,8192]{2,1,0:T(8,128)(2,1)S(1)}, bf16[1,512,8192]{2,1,0:T(8,128)(2,1)}, u32[]{:S(2)}) %copy-start) | copy-done | bytes 8388632
  30.1 2.4 %sketched_early.1.refs_4_ = f32[512,256]{1,0:T(8,128)S(1)} custom-call(s32[20]{0:T(128)S(1)} %stack.121.place, bf16[512,8192]{1,0:T(8,128)(2,1)S(1)} %bitcast.36, bf16[512,256]{1,0:T(8,128)(2,1)S(1)} %copy-done.6, bf16[512,256]{1,0:T(8,128)(2,1)S(1)} %collective-permute-done.refs_1_, bf16[512,256]{1,0:T(8,128)(2,1)S(1)} %collective-permute-done.1.refs_2_, ...), custom_call_target="tpu_custom_call" | custom-call | flops 1600000000 | bytes 4194304 | tf_op jit(solution)/shard_map/sketched_early/pallas_call | solution.py:45
  32.5 1.1 collective-permute-start.14
  33.7 1.1 collective-permute-done.14.refs_2_
  35.1 2.6 %sketched_late.1 = (f32[192,128]{1,0:T(8,128)S(1)}, f32[192,128]{1,0:T(8,128)S(1)}, bf16[512,256]{1,0:T(8,128)(2,1)S(1)}, bf16[256,512]{1,0:T(8,128)(2,1)S(1)}) custom-call(s32[20]{0:T(128)S(1)} %stack.121.place, bf16[512,8192]{1,0:T(8,128)(2,1)S(1)} %bitcast.37, bf16[512,256]{1,0:T(8,128)(2,1)S(1)} %collective-permute-done.5.refs_0_, ...), custom_call_target="tpu_custom_call" | custom-call | flops 800000000 | bytes 4194304 | tf_op jit(solution)/shard_map/sketched_late/pallas_call | solution.py:45
  39.2 2.9 %product.1 = (bf16[8,256,512]{2,1,0:T(8,128)(2,1)S(1)}, bf16[8,256,512]{2,1,0:T(8,128)(2,1)S(1)}) custom-call(s32[20]{0:T(128)S(1)} %stack.121.place, bf16[512,8192]{1,0:T(8,128)(2,1)S(1)} %bitcast.38, bf16[256,512]{1,0:T(8,128)(2,1)S(1)} %get-tuple-element.57.turned), custom_call_target="tpu_custom_call" | custom-call | flops 2200000000 | bytes 4194304 | tf_op jit(solution)/shard_map/product/pallas_call | solution.py:45
  42.1 1.1 collective-permute-done.17
  43.2 1.2 collective-permute-start.21
  44.4 1.7 %collective-permute-start.22 = (bf16[512,256]{1,0:T(8,128)(2,1)S(1)}, bf16[512,256]{1,0:T(8,128)(2,1)S(1)}, u32[]{:S(2)}, u32[]{:S(2)}) collective-permute-start(bf16[512,256]{1,0:T(8,128)(2,1)S(1)} %get-tuple-element.63), channel_id=1, source_target_pairs={{0,16},{1,17},{2,18},{3,19},{4,20},{5,21},{6,22},{7,23},{8,24},{9,... | collective-permute-start | bytes 786440 | tf_op jit(solution)/shard_map/gather_sketched/ppermute | solution.py:25
  46.1 3.5 %collective-permute-start.20 = (f32[192,128]{1,0:T(8,128)S(1)}, f32[192,128]{1,0:T(8,128)S(1)}, u32[]{:S(2)}, u32[]{:S(2)}) collective-permute-start(f32[192,128]{1,0:T(8,128)S(1)} %add.172), channel_id=1, source_target_pairs={{0,12},{1,13},{2,14},{3,15},{4,0},{5,1},{6,2},{7,3},{8,4},{9,5},{1... | collective-permute-start | bytes 294920 | tf_op jit(solution)/shard_map/sum_gram/ppermute | solution.py:25
  49.6 1.3 collective-permute-start.18
  51.0 2.0 %add_convert_fusion = bf16[8,256,512]{2,1,0:T(8,128)(2,1)} fusion(bf16[8,256,512]{2,1,0:T(8,128)(2,1)S(1)} %collective-permute-done.21, bf16[8,256,512]{2,1,0:T(8,128)(2,1)S(1)} %get-tuple-element.61), kind=kLoop, calls=%fused_computation | loop fusion | flops 4194304 | bytes 6291456 | tf_op jit(solution)/shard_map/sum_cores/convert_element_type | solution.py:329
  53.8 3.3 %collective-permute-done.19 = f32[192,128]{1,0:T(8,128)S(1)} collective-permute-done((f32[192,128]{1,0:T(8,128)S(1)}, f32[192,128]{1,0:T(8,128)S(1)}, u32[]{:S(2)}, u32[]{:S(2)}) %collective-permute-start.19) | collective-permute-done | bytes 98336 | tf_op jit(solution)/shard_map/sum_gram/ppermute | solution.py:25
  57.2 3.6 %all-to-all-start = ((bf16[8,256,512]{2,1,0:T(8,128)(2,1)}), bf16[8,256,512]{2,1,0:T(8,128)(2,1)S(1)}, u32[]{:S(2)}, u32[]{:S(2)}) async-start(bf16[8,256,512]{2,1,0:T(8,128)(2,1)} %add_convert_fusion), calls=%async_computation | async-start | bytes 4194304 | tf_op jit(solution)/shard_map/sum_fsdp/all_to_all | solution.py:339
  60.8 2.5 %collective-permute-start.25 = (bf16[2,512,256]{2,1,0:T(8,128)(2,1)S(1)}, bf16[2,512,256]{2,1,0:T(8,128)(2,1)S(1)}, u32[]{:S(2)}, u32[]{:S(2)}) collective-permute-start(bf16[2,512,256]{2,1,0:T(8,128)(2,1)S(1)} %pad_maximum_fusion.s0), channel_id=1, source_target_pairs={{0,96},{1,97},{2,98},{3,99},{4,100},{5,101},{6,102},{7,103},{8,104... | collective-permute-start | bytes 1572872 | tf_op jit(solution)/shard_map/gather_sketched/ppermute | solution.py:25
  63.4 1.3 collective-permute-start.23
  65.6 11.3 %inverse.1 = f32[256,256]{1,0:T(8,128)S(1)} custom-call(s32[20]{0:T(128)S(1)} %stack.121.place, f32[192,128]{1,0:T(8,128)S(1)} %add_add_fusion.mine, f32[192,128]{1,0:T(8,128)S(1)} %collective-permute-done.23.theirs), custom_call_target="tpu_custom_call" | custom-call | flops 3000000000 | bytes 4194304 | tf_op jit(solution)/shard_map/inverse/pallas_call | solution.py:45
  79.2 3.0 %collective-permute-start.28 = (bf16[512,256]{1,0:T(8,128)(2,1)}, bf16[512,256]{1,0:T(8,128)(2,1)}, u32[]{:S(2)}, u32[]{:S(2)}) collective-permute-start(bf16[512,256]{1,0:T(8,128)(2,1)} %slice_bitcast_fusion), channel_id=1, source_target_pairs={{0,96},{1,97},{2,98},{3,99},{4,100},{5,101},{6,102},{7,103},{8,104... | collective-permute-start | bytes 786440 | tf_op jit(solution)/shard_map/gather_sketched/ppermute | solution.py:25
  82.8 1.2 collective-permute-start.26
  84.0 2.7 %all-to-all-done.parts = bf16[8,256,512]{2,1,0:T(8,128)(2,1)S(1)} async-done(((bf16[8,256,512]{2,1,0:T(8,128)(2,1)}), bf16[8,256,512]{2,1,0:T(8,128)(2,1)S(1)}, u32[]{:S(2)}, u32[]{:S(2)}) %all-to-all-start) | async-done | bytes 2097184 | tf_op jit(solution)/shard_map/sum_fsdp/all_to_all | solution.py:339
  86.7 1.5 %coef.1 = (bf16[256,128]{1,0:T(8,128)(2,1)S(1)}, bf16[256,128]{1,0:T(8,128)(2,1)S(1)}, bf16[256,128]{1,0:T(8,128)(2,1)S(1)}, bf16[256,128]{1,0:T(8,128)(2,1)S(1)}) custom-call(s32[20]{0:T(128)S(1)} %stack.121.place, f32[256,256]{1,0:T(8,128)S(1)} %inverse.1, bf16[8,256,512]{2,1,0:T(8,128)(2,1)S(1)} %all-to-all-done.parts), custom_call_target="tpu_custom_call" | custom-call | flops 400000000 | bytes 4194304 | tf_op jit(solution)/shard_map/coef/pallas_call | solution.py:45
  88.2 2.6 %collective-permute-done.27 = bf16[512,256]{1,0:T(8,128)(2,1)} collective-permute-done((bf16[512,256]{1,0:T(8,128)(2,1)}, bf16[512,256]{1,0:T(8,128)(2,1)}, u32[]{:S(2)}, u32[]{:S(2)}) %collective-permute-start.27) | collective-permute-done | bytes 262176 | tf_op jit(solution)/shard_map/gather_sketched/ppermute | solution.py:25
  90.9 4.5 %collective-permute-start.31 = (bf16[256,128]{1,0:T(8,128)(2,1)S(1)}, bf16[256,128]{1,0:T(8,128)(2,1)S(1)}, u32[]{:S(2)}, u32[]{:S(2)}) collective-permute-start(bf16[256,128]{1,0:T(8,128)(2,1)S(1)} %get-tuple-element.80), channel_id=1, source_target_pairs={{0,0},{1,16},{2,2},{3,18},{4,4},{5,20},{6,6},{7,22},{8,8},{9,24},{... | collective-permute-start | bytes 196616 | tf_op jit(solution)/shard_map/exchange_coef/ppermute | solution.py:25
  95.5 4.2 %collective-permute-start.29 = (bf16[256,128]{1,0:T(8,128)(2,1)S(1)}, bf16[256,128]{1,0:T(8,128)(2,1)S(1)}, u32[]{:S(2)}, u32[]{:S(2)}) collective-permute-start(bf16[256,128]{1,0:T(8,128)(2,1)S(1)} %get-tuple-element.78), channel_id=1, source_target_pairs={{0,64},{1,80},{2,66},{3,82},{4,68},{5,84},{6,70},{7,86},{8,72},{9,... | collective-permute-start | bytes 196616 | tf_op jit(solution)/shard_map/exchange_coef/ppermute | solution.py:25
  99.7 1.2 collective-permute-start.30
  100.8 2.6 %collective-permute-done.32.refs_1_ = bf16[256,128]{1,0:T(8,128)(2,1)S(1)} collective-permute-done((bf16[256,128]{1,0:T(8,128)(2,1)S(1)}, bf16[256,128]{1,0:T(8,128)(2,1)S(1)}, u32[]{:S(2)}, u32[]{:S(2)}) %collective-permute-start.32) | collective-permute-done | bytes 65568 | tf_op jit(solution)/shard_map/exchange_coef/ppermute | solution.py:25
  103.5 1.1 spread.2.refs_2_
  104.6 1.2 collective-permute-done.30.refs_1_
  105.8 1.1 spread.3
  106.9 4.5 %all-to-all-start.1 = ((bf16[8,1024,128]{2,1,0:T(8,128)(2,1)}), bf16[8,1024,128]{2,1,0:T(8,128)(2,1)}, u32[]{:S(2)}, u32[]{:S(2)}) async-start(bf16[8,1024,128]{2,1,0:T(8,128)(2,1)} %spread.3), calls=%async_computation.1 | async-start | bytes 4194304 | tf_op jit(solution)/shard_map/gather_coef/all_to_all | solution.py:379
  113.1 2.1 %collective-permute-start.33 = (bf16[2,128,256]{2,1,0:T(8,128)(2,1)S(1)}, bf16[2,128,256]{2,1,0:T(8,128)(2,1)S(1)}, u32[]{:S(2)}, u32[]{:S(2)}) collective-permute-start(bf16[2,128,256]{2,1,0:T(8,128)(2,1)S(1)} %get-tuple-element.93), channel_id=1, source_target_pairs={{0,32},{1,33},{2,34},{3,35},{4,36},{5,37},{6,38},{7,39},{8,40},{9,... | collective-permute-start | bytes 393224 | tf_op jit(solution)/shard_map/gather_inverse/ppermute | solution.py:25
  115.2 1.7 %collective-permute-start.35 = (bf16[2,128,256]{2,1,0:T(8,128)(2,1)S(1)}, bf16[2,128,256]{2,1,0:T(8,128)(2,1)S(1)}, u32[]{:S(2)}, u32[]{:S(2)}) collective-permute-start(bf16[2,128,256]{2,1,0:T(8,128)(2,1)S(1)} %get-tuple-element.93), channel_id=1, source_target_pairs={{0,96},{1,97},{2,98},{3,99},{4,100},{5,101},{6,102},{7,103},{8,104... | collective-permute-start | bytes 393224 | tf_op jit(solution)/shard_map/gather_inverse/ppermute | solution.py:25
  116.9 1.2 collective-permute-done.34
  118.1 1.5 %collective-permute-done.33 = bf16[2,128,256]{2,1,0:T(8,128)(2,1)S(1)} collective-permute-done((bf16[2,128,256]{2,1,0:T(8,128)(2,1)S(1)}, bf16[2,128,256]{2,1,0:T(8,128)(2,1)S(1)}, u32[]{:S(2)}, u32[]{:S(2)}) %collective-permute-start.33) | collective-permute-done | bytes 131104 | tf_op jit(solution)/shard_map/gather_inverse/ppermute | solution.py:25
  119.8 1.1 pad_maximum_fusion.1.s2
  121.7 2.5 %basis.1.left = bf16[512,2048]{1,0:T(8,128)(2,1)S(1)} custom-call(s32[20]{0:T(128)S(1)} %stack.121.place, bf16[2,512,256]{2,1,0:T(8,128)(2,1)S(1)} %pad_maximum_fusion.s0, bf16[2,512,256]{2,1,0:T(8,128)(2,1)S(1)} %copy-done.5, bf16[2,512,256]{2,1,0:T(8,128)(2,1)S(1)} %pad_maximum_fusion.1.s2, bf16[2,512,256]{2,1,0:T(8,128)(2,1)S(1)} %collective-permute-done.25.s3, ...), custom_call_target="tpu_custom_call" | custom-call | flops 540000000 | bytes 4194304 | tf_op jit(solution)/shard_map/basis/pallas_call | solution.py:45
  124.2 10.7 %all-to-all-done.1.mine = bf16[8,1024,128]{2,1,0:T(8,128)(2,1)} async-done(((bf16[8,1024,128]{2,1,0:T(8,128)(2,1)}), bf16[8,1024,128]{2,1,0:T(8,128)(2,1)}, u32[]{:S(2)}, u32[]{:S(2)}) %all-to-all-start.1) | async-done | bytes 2097184 | tf_op jit(solution)/shard_map/gather_coef/all_to_all | solution.py:379
  134.9 3.0 %partial.1.part = f32[512,1024]{1,0:T(8,128)S(1)} custom-call(bf16[512,2048]{1,0:T(8,128)(2,1)S(1)} %basis.1.left, bf16[8,1024,128]{2,1,0:T(8,128)(2,1)} %all-to-all-done.1.mine), custom_call_target="tpu_custom_call" | custom-call | flops 1100000000 | bytes 4194304 | tf_op jit(solution)/shard_map/partial/pallas_call | solution.py:45
  137.9 1.4 collective-permute-done.37.theirs
  139.3 2.7 %update.1 = (f32[512,1024]{1,0:T(8,128)}, f32[512,1024]{1,0:T(8,128)}) custom-call(bf16[512,2048]{1,0:T(8,128)(2,1)S(1)} %basis.1.left, bf16[8,1024,128]{2,1,0:T(8,128)(2,1)S(1)} %collective-permute-done.37.theirs, f32[512,1024]{1,0:T(8,128)S(1)} %partial.1.part, f32[512,1024]{1,0:T(8,128)S(1)} %copy-done.2, f32[512,1024]{1,0:T(8,128)S(1)} %copy-done.3), custom_call_target="tpu_custom_call" | custom-call | flops 1100000000 | bytes 14000000 | tf_op jit(solution)/shard_map/update/pallas_call | solution.py:251
  (72 shorter events, 13.8 us)
Async XLA Ops:
  0.6 10.8 %collective-permute-start.2 = (bf16[512,256]{1,0:T(8,128)(2,1)}, bf16[512,256]{1,0:T(8,128)(2,1)S(1)}, u32[]{:S(2)}, u32[]{:S(2)}) collective-permute-start(bf16[512,256]{1,0:T(8,128)(2,1)} %refs_0_.1), channel_id=1, source_target_pairs={{0,8},{1,9},{2,10},{3,11},{4,12},{5,13},{6,14},{7,15},{8,0},{9,1},... | collective-permute-start | bytes 786440 | tf_op jit(solution)/shard_map/gather_sketch/ppermute | solution.py:25
  5.1 9.1 %collective-permute-start.7 = (bf16[512,256]{1,0:T(8,128)(2,1)}, bf16[512,256]{1,0:T(8,128)(2,1)S(1)}, u32[]{:S(2)}, u32[]{:S(2)}) collective-permute-start(bf16[512,256]{1,0:T(8,128)(2,1)} %refs_0_.1), channel_id=1, source_target_pairs={{0,2},{1,3},{2,16},{3,17},{4,6},{5,7},{6,20},{7,21},{8,10},{9,11},... | collective-permute-start | bytes 786440 | tf_op jit(solution)/shard_map/gather_sketch/ppermute | solution.py:25
  6.4 11.1 %collective-permute-start.1 = (bf16[512,256]{1,0:T(8,128)(2,1)}, bf16[512,256]{1,0:T(8,128)(2,1)S(1)}, u32[]{:S(2)}, u32[]{:S(2)}) collective-permute-start(bf16[512,256]{1,0:T(8,128)(2,1)} %refs_0_.1), channel_id=1, source_target_pairs={{0,12},{1,13},{2,14},{3,15},{4,0},{5,1},{6,2},{7,3},{8,4},{9,5},{1... | collective-permute-start | bytes 786440 | tf_op jit(solution)/shard_map/gather_sketch/ppermute | solution.py:25
  6.9 12.1 %collective-permute-start = (bf16[512,256]{1,0:T(8,128)(2,1)}, bf16[512,256]{1,0:T(8,128)(2,1)S(1)}, u32[]{:S(2)}, u32[]{:S(2)}) collective-permute-start(bf16[512,256]{1,0:T(8,128)(2,1)} %refs_0_.1), channel_id=1, source_target_pairs={{0,4},{1,5},{2,6},{3,7},{4,8},{5,9},{6,10},{7,11},{8,12},{9,13},{1... | collective-permute-start | bytes 786440 | tf_op jit(solution)/shard_map/gather_sketch/ppermute | solution.py:25
  11.4 7.6 %collective-permute-start.4 = (bf16[256,256]{1,0:T(8,128)(2,1)S(1)}, bf16[256,256]{1,0:T(8,128)(2,1)S(1)}, u32[]{:S(2)}, u32[]{:S(2)}) collective-permute-start(bf16[256,256]{1,0:T(8,128)(2,1)S(1)} %get-tuple-element.90), channel_id=1, source_target_pairs={{0,18},{1,19},{2,0},{3,1},{4,22},{5,23},{6,4},{7,5},{8,26},{9,27},... | collective-permute-start | bytes 393224 | tf_op jit(solution)/shard_map/gather_sketch/ppermute | solution.py:25
  14.2 5.3 %collective-permute-start.3 = (bf16[256,256]{1,0:T(8,128)(2,1)S(1)}, bf16[256,256]{1,0:T(8,128)(2,1)S(1)}, u32[]{:S(2)}, u32[]{:S(2)}) collective-permute-start(bf16[256,256]{1,0:T(8,128)(2,1)S(1)} %get-tuple-element.91), channel_id=1, source_target_pairs={{0,2},{1,3},{2,16},{3,17},{4,6},{5,7},{6,20},{7,21},{8,10},{9,11},... | collective-permute-start | bytes 393224 | tf_op jit(solution)/shard_map/gather_sketch/ppermute | solution.py:25
  14.2 8.5 %collective-permute-start.8 = (bf16[512,256]{1,0:T(8,128)(2,1)}, bf16[512,256]{1,0:T(8,128)(2,1)S(1)}, u32[]{:S(2)}, u32[]{:S(2)}) collective-permute-start(bf16[512,256]{1,0:T(8,128)(2,1)} %refs_0_.1), channel_id=1, source_target_pairs={{0,1},{1,0},{2,3},{3,2},{4,5},{5,4},{6,7},{7,6},{8,9},{9,8},{10,11... | collective-permute-start | bytes 786440 | tf_op jit(solution)/shard_map/gather_sketch/ppermute | solution.py:25
  17.6 5.4 %collective-permute-start.12 = (bf16[512,256]{1,0:T(8,128)(2,1)S(1)}, bf16[512,256]{1,0:T(8,128)(2,1)S(1)}, u32[]{:S(2)}, u32[]{:S(2)}) collective-permute-start(bf16[512,256]{1,0:T(8,128)(2,1)S(1)} %collective-permute-done.2.refs_4_), channel_id=1, source_target_pairs={{0,1},{1,0},{2,3},{3,2},{4,5},{5,4},{6,7},{7,6},{8,9},{9,8},{10,11... | collective-permute-start | bytes 786440 | tf_op jit(solution)/shard_map/gather_sketch/ppermute | solution.py:25
  19.0 3.9 %collective-permute-start.11 = (bf16[512,256]{1,0:T(8,128)(2,1)S(1)}, bf16[512,256]{1,0:T(8,128)(2,1)S(1)}, u32[]{:S(2)}, u32[]{:S(2)}) collective-permute-start(bf16[512,256]{1,0:T(8,128)(2,1)S(1)} %collective-permute-done.7.refs_3_), channel_id=1, source_target_pairs={{0,1},{1,0},{2,3},{3,2},{4,5},{5,4},{6,7},{7,6},{8,9},{9,8},{10,11... | collective-permute-start | bytes 786440 | tf_op jit(solution)/shard_map/gather_sketch/ppermute | solution.py:25
  19.0 6.7 %collective-permute-start.10 = (bf16[512,256]{1,0:T(8,128)(2,1)S(1)}, bf16[512,256]{1,0:T(8,128)(2,1)S(1)}, u32[]{:S(2)}, u32[]{:S(2)}) collective-permute-start(bf16[512,256]{1,0:T(8,128)(2,1)S(1)} %collective-permute-done.1.refs_2_), channel_id=1, source_target_pairs={{0,1},{1,0},{2,3},{3,2},{4,5},{5,4},{6,7},{7,6},{8,9},{9,8},{10,11... | collective-permute-start | bytes 786440 | tf_op jit(solution)/shard_map/gather_sketch/ppermute | solution.py:25
  19.5 6.2 %collective-permute-start.9 = (bf16[512,256]{1,0:T(8,128)(2,1)S(1)}, bf16[512,256]{1,0:T(8,128)(2,1)S(1)}, u32[]{:S(2)}, u32[]{:S(2)}) collective-permute-start(bf16[512,256]{1,0:T(8,128)(2,1)S(1)} %collective-permute-done.refs_1_), channel_id=1, source_target_pairs={{0,1},{1,0},{2,3},{3,2},{4,5},{5,4},{6,7},{7,6},{8,9},{9,8},{10,11... | collective-permute-start | bytes 786440 | tf_op jit(solution)/shard_map/gather_sketch/ppermute | solution.py:25
  22.8 3.0 %collective-permute-start.13 = (bf16[512,256]{1,0:T(8,128)(2,1)S(1)}, bf16[512,256]{1,0:T(8,128)(2,1)S(1)}, u32[]{:S(2)}, u32[]{:S(2)}) collective-permute-start(bf16[512,256]{1,0:T(8,128)(2,1)S(1)} %constant_dynamic-update-slice_fusion.refs_5_), channel_id=1, source_target_pairs={{0,1},{1,0},{2,3},{3,2},{4,5},{5,4},{6,7},{7,6},{8,9},{9,8},{10,11... | collective-permute-start | bytes 786440 | tf_op jit(solution)/shard_map/gather_sketch/ppermute | solution.py:25
  22.9 9.6 %collective-permute-start.5 = (bf16[512,256]{1,0:T(8,128)(2,1)S(1)}, bf16[512,256]{1,0:T(8,128)(2,1)S(1)}, u32[]{:S(2)}, u32[]{:S(2)}) collective-permute-start(bf16[512,256]{1,0:T(8,128)(2,1)S(1)} %collective-permute-done.refs_1_), channel_id=1, source_target_pairs={{0,2},{1,3},{2,16},{3,17},{4,6},{5,7},{6,20},{7,21},{8,10},{9,11},... | collective-permute-start | bytes 786440 | tf_op jit(solution)/shard_map/gather_sketch/ppermute | solution.py:25
  23.0 9.5 %collective-permute-start.6 = (bf16[512,256]{1,0:T(8,128)(2,1)S(1)}, bf16[512,256]{1,0:T(8,128)(2,1)S(1)}, u32[]{:S(2)}, u32[]{:S(2)}) collective-permute-start(bf16[512,256]{1,0:T(8,128)(2,1)S(1)} %collective-permute-done.1.refs_2_), channel_id=1, source_target_pairs={{0,18},{1,19},{2,0},{3,1},{4,22},{5,23},{6,4},{7,5},{8,26},{9,27},... | collective-permute-start | bytes 786440 | tf_op jit(solution)/shard_map/gather_sketch/ppermute | solution.py:25
  25.8 3.4 %copy-start = (bf16[1,512,8192]{2,1,0:T(8,128)(2,1)S(1)}, bf16[1,512,8192]{2,1,0:T(8,128)(2,1)}, u32[]{:S(2)}) copy-start(bf16[1,512,8192]{2,1,0:T(8,128)(2,1)} %param.4) | copy-start | bytes 25165828
  29.2 0.9 copy-start.6
  32.5 6.7 %copy-start.1 = (bf16[1,512,8192]{2,1,0:T(8,128)(2,1)S(1)}, bf16[1,512,8192]{2,1,0:T(8,128)(2,1)}, u32[]{:S(2)}) copy-start(bf16[1,512,8192]{2,1,0:T(8,128)(2,1)} %param.4) | copy-start | bytes 25165828
  32.5 2.2 %collective-permute-start.14 = (bf16[512,256]{1,0:T(8,128)(2,1)S(1)}, bf16[512,256]{1,0:T(8,128)(2,1)S(1)}, u32[]{:S(2)}, u32[]{:S(2)}) collective-permute-start(bf16[512,256]{1,0:T(8,128)(2,1)S(1)} %collective-permute-done.5.refs_0_), channel_id=1, source_target_pairs={{0,1},{1,0},{2,3},{3,2},{4,5},{5,4},{6,7},{7,6},{8,9},{9,8},{10,11... | collective-permute-start | bytes 786440 | tf_op jit(solution)/shard_map/gather_sketch/ppermute | solution.py:25
  33.6 1.5 %collective-permute-start.15 = (bf16[512,256]{1,0:T(8,128)(2,1)S(1)}, bf16[512,256]{1,0:T(8,128)(2,1)S(1)}, u32[]{:S(2)}, u32[]{:S(2)}) collective-permute-start(bf16[512,256]{1,0:T(8,128)(2,1)S(1)} %collective-permute-done.6.refs_1_), channel_id=1, source_target_pairs={{0,1},{1,0},{2,3},{3,2},{4,5},{5,4},{6,7},{7,6},{8,9},{9,8},{10,11... | collective-permute-start | bytes 786440 | tf_op jit(solution)/shard_map/gather_sketch/ppermute | solution.py:25
  37.7 1.4 collective-permute-start.16
  39.1 4.1 %collective-permute-start.17 = (f32[192,128]{1,0:T(8,128)S(1)}, f32[192,128]{1,0:T(8,128)S(1)}, u32[]{:S(2)}, u32[]{:S(2)}) collective-permute-start(f32[192,128]{1,0:T(8,128)S(1)} %add.171), channel_id=1, source_target_pairs={{0,2},{1,3},{2,0},{3,1},{4,6},{5,7},{6,4},{7,5},{8,10},{9,11},{10,... | collective-permute-start | bytes 294920 | tf_op jit(solution)/shard_map/sum_gram/ppermute | solution.py:25
  43.2 7.8 %collective-permute-start.21 = (bf16[8,256,512]{2,1,0:T(8,128)(2,1)S(1)}, bf16[8,256,512]{2,1,0:T(8,128)(2,1)S(1)}, u32[]{:S(2)}, u32[]{:S(2)}) collective-permute-start(bf16[8,256,512]{2,1,0:T(8,128)(2,1)S(1)} %get-tuple-element.62), channel_id=1, source_target_pairs={{0,1},{1,0},{2,3},{3,2},{4,5},{5,4},{6,7},{7,6},{8,9},{9,8},{10,11... | collective-permute-start | bytes 6291464 | tf_op jit(solution)/shard_map/sum_cores/ppermute | solution.py:25
  44.4 9.4 %collective-permute-start.22 = (bf16[512,256]{1,0:T(8,128)(2,1)S(1)}, bf16[512,256]{1,0:T(8,128)(2,1)S(1)}, u32[]{:S(2)}, u32[]{:S(2)}) collective-permute-start(bf16[512,256]{1,0:T(8,128)(2,1)S(1)} %get-tuple-element.63), channel_id=1, source_target_pairs={{0,16},{1,17},{2,18},{3,19},{4,20},{5,21},{6,22},{7,23},{8,24},{9,... | collective-permute-start | bytes 786440 | tf_op jit(solution)/shard_map/gather_sketched/ppermute | solution.py:25
  46.1 7.7 %collective-permute-start.20 = (f32[192,128]{1,0:T(8,128)S(1)}, f32[192,128]{1,0:T(8,128)S(1)}, u32[]{:S(2)}, u32[]{:S(2)}) collective-permute-start(f32[192,128]{1,0:T(8,128)S(1)} %add.172), channel_id=1, source_target_pairs={{0,12},{1,13},{2,14},{3,15},{4,0},{5,1},{6,2},{7,3},{8,4},{9,5},{1... | collective-permute-start | bytes 294920 | tf_op jit(solution)/shard_map/sum_gram/ppermute | solution.py:25
  49.6 7.5 %collective-permute-start.19 = (f32[192,128]{1,0:T(8,128)S(1)}, f32[192,128]{1,0:T(8,128)S(1)}, u32[]{:S(2)}, u32[]{:S(2)}) collective-permute-start(f32[192,128]{1,0:T(8,128)S(1)} %add.172), channel_id=1, source_target_pairs={{0,4},{1,5},{2,6},{3,7},{4,8},{5,9},{6,10},{7,11},{8,12},{9,13},{1... | collective-permute-start | bytes 294920 | tf_op jit(solution)/shard_map/sum_gram/ppermute | solution.py:25
  49.6 7.5 %collective-permute-start.18 = (f32[192,128]{1,0:T(8,128)S(1)}, f32[192,128]{1,0:T(8,128)S(1)}, u32[]{:S(2)}, u32[]{:S(2)}) collective-permute-start(f32[192,128]{1,0:T(8,128)S(1)} %add.172), channel_id=1, source_target_pairs={{0,8},{1,9},{2,10},{3,11},{4,12},{5,13},{6,14},{7,15},{8,0},{9,1},... | collective-permute-start | bytes 294920 | tf_op jit(solution)/shard_map/sum_gram/ppermute | solution.py:25
  57.2 29.5 %all-to-all-start = ((bf16[8,256,512]{2,1,0:T(8,128)(2,1)}), bf16[8,256,512]{2,1,0:T(8,128)(2,1)S(1)}, u32[]{:S(2)}, u32[]{:S(2)}) async-start(bf16[8,256,512]{2,1,0:T(8,128)(2,1)} %add_convert_fusion), calls=%async_computation | async-start | bytes 4194304 | tf_op jit(solution)/shard_map/sum_fsdp/all_to_all | solution.py:339
  60.8 16.1 %collective-permute-start.25 = (bf16[2,512,256]{2,1,0:T(8,128)(2,1)S(1)}, bf16[2,512,256]{2,1,0:T(8,128)(2,1)S(1)}, u32[]{:S(2)}, u32[]{:S(2)}) collective-permute-start(bf16[2,512,256]{2,1,0:T(8,128)(2,1)S(1)} %pad_maximum_fusion.s0), channel_id=1, source_target_pairs={{0,96},{1,97},{2,98},{3,99},{4,100},{5,101},{6,102},{7,103},{8,104... | collective-permute-start | bytes 1572872 | tf_op jit(solution)/shard_map/gather_sketched/ppermute | solution.py:25
  63.4 13.5 %collective-permute-start.24 = (bf16[2,512,256]{2,1,0:T(8,128)(2,1)S(1)}, bf16[2,512,256]{2,1,0:T(8,128)(2,1)S(1)}, u32[]{:S(2)}, u32[]{:S(2)}) collective-permute-start(bf16[2,512,256]{2,1,0:T(8,128)(2,1)S(1)} %pad_maximum_fusion.s0), channel_id=1, source_target_pairs={{0,32},{1,33},{2,34},{3,35},{4,36},{5,37},{6,38},{7,39},{8,40},{9,... | collective-permute-start | bytes 1572872 | tf_op jit(solution)/shard_map/gather_sketched/ppermute | solution.py:25
  63.4 2.3 %collective-permute-start.23 = (f32[192,128]{1,0:T(8,128)S(1)}, f32[192,128]{1,0:T(8,128)S(1)}, u32[]{:S(2)}, u32[]{:S(2)}) collective-permute-start(f32[192,128]{1,0:T(8,128)S(1)} %add_add_fusion.mine), channel_id=1, source_target_pairs={{0,1},{1,0},{2,3},{3,2},{4,5},{5,4},{6,7},{7,6},{8,9},{9,8},{10,11... | collective-permute-start | bytes 294920 | tf_op jit(solution)/shard_map/sum_gram/ppermute | solution.py:25
  77.7 0.8 copy-start.4
  79.2 9.1 %collective-permute-start.28 = (bf16[512,256]{1,0:T(8,128)(2,1)}, bf16[512,256]{1,0:T(8,128)(2,1)}, u32[]{:S(2)}, u32[]{:S(2)}) collective-permute-start(bf16[512,256]{1,0:T(8,128)(2,1)} %slice_bitcast_fusion), channel_id=1, source_target_pairs={{0,96},{1,97},{2,98},{3,99},{4,100},{5,101},{6,102},{7,103},{8,104... | collective-permute-start | bytes 786440 | tf_op jit(solution)/shard_map/gather_sketched/ppermute | solution.py:25
  82.1 8.7 %collective-permute-start.27 = (bf16[512,256]{1,0:T(8,128)(2,1)}, bf16[512,256]{1,0:T(8,128)(2,1)}, u32[]{:S(2)}, u32[]{:S(2)}) collective-permute-start(bf16[512,256]{1,0:T(8,128)(2,1)} %slice_bitcast_fusion.1), channel_id=1, source_target_pairs={{0,32},{1,33},{2,34},{3,35},{4,36},{5,37},{6,38},{7,39},{8,40},{9,... | collective-permute-start | bytes 786440 | tf_op jit(solution)/shard_map/gather_sketched/ppermute | solution.py:25
  82.8 5.5 %collective-permute-start.26 = (bf16[128,256]{1,0:T(8,128)(2,1)}, bf16[128,256]{1,0:T(8,128)(2,1)}, u32[]{:S(2)}, u32[]{:S(2)}) collective-permute-start(bf16[128,256]{1,0:T(8,128)(2,1)} %dynamic-slice_convert_fusion), channel_id=1, source_target_pairs={{0,16},{1,17},{2,18},{3,19},{4,20},{5,21},{6,22},{7,23},{8,24},{9,... | collective-permute-start | bytes 196616 | tf_op jit(solution)/shard_map/gather_inverse/ppermute | solution.py:25
  90.9 10.0 %collective-permute-start.31 = (bf16[256,128]{1,0:T(8,128)(2,1)S(1)}, bf16[256,128]{1,0:T(8,128)(2,1)S(1)}, u32[]{:S(2)}, u32[]{:S(2)}) collective-permute-start(bf16[256,128]{1,0:T(8,128)(2,1)S(1)} %get-tuple-element.80), channel_id=1, source_target_pairs={{0,0},{1,16},{2,2},{3,18},{4,4},{5,20},{6,6},{7,22},{8,8},{9,24},{... | collective-permute-start | bytes 196616 | tf_op jit(solution)/shard_map/exchange_coef/ppermute | solution.py:25
  95.4 8.1 %collective-permute-start.32 = (bf16[256,128]{1,0:T(8,128)(2,1)S(1)}, bf16[256,128]{1,0:T(8,128)(2,1)S(1)}, u32[]{:S(2)}, u32[]{:S(2)}) collective-permute-start(bf16[256,128]{1,0:T(8,128)(2,1)S(1)} %get-tuple-element.81), channel_id=1, source_target_pairs={{0,32},{1,48},{2,34},{3,50},{4,36},{5,52},{6,38},{7,54},{8,40},{9,... | collective-permute-start | bytes 196616 | tf_op jit(solution)/shard_map/exchange_coef/ppermute | solution.py:25
  95.5 9.1 %collective-permute-start.29 = (bf16[256,128]{1,0:T(8,128)(2,1)S(1)}, bf16[256,128]{1,0:T(8,128)(2,1)S(1)}, u32[]{:S(2)}, u32[]{:S(2)}) collective-permute-start(bf16[256,128]{1,0:T(8,128)(2,1)S(1)} %get-tuple-element.78), channel_id=1, source_target_pairs={{0,64},{1,80},{2,66},{3,82},{4,68},{5,84},{6,70},{7,86},{8,72},{9,... | collective-permute-start | bytes 196616 | tf_op jit(solution)/shard_map/exchange_coef/ppermute | solution.py:25
  99.7 6.1 %collective-permute-start.30 = (bf16[256,128]{1,0:T(8,128)(2,1)S(1)}, bf16[256,128]{1,0:T(8,128)(2,1)S(1)}, u32[]{:S(2)}, u32[]{:S(2)}) collective-permute-start(bf16[256,128]{1,0:T(8,128)(2,1)S(1)} %get-tuple-element.79), channel_id=1, source_target_pairs={{0,96},{1,112},{2,98},{3,114},{4,100},{5,116},{6,102},{7,118},{8,1... | collective-permute-start | bytes 196616 | tf_op jit(solution)/shard_map/exchange_coef/ppermute | solution.py:25
  106.9 28.1 %all-to-all-start.1 = ((bf16[8,1024,128]{2,1,0:T(8,128)(2,1)}), bf16[8,1024,128]{2,1,0:T(8,128)(2,1)}, u32[]{:S(2)}, u32[]{:S(2)}) async-start(bf16[8,1024,128]{2,1,0:T(8,128)(2,1)} %spread.3), calls=%async_computation.1 | async-start | bytes 4194304 | tf_op jit(solution)/shard_map/gather_coef/all_to_all | solution.py:379
  111.3 10.4 %copy-start.5 = (bf16[2,512,256]{2,1,0:T(8,128)(2,1)S(1)}, bf16[2,512,256]{2,1,0:T(8,128)(2,1)}, u32[]{:S(2)}) copy-start(bf16[2,512,256]{2,1,0:T(8,128)(2,1)} %copy-done.4) | copy-start | bytes 1572868
  112.3 5.8 %collective-permute-start.34 = (bf16[2,128,256]{2,1,0:T(8,128)(2,1)S(1)}, bf16[2,128,256]{2,1,0:T(8,128)(2,1)S(1)}, u32[]{:S(2)}, u32[]{:S(2)}) collective-permute-start(bf16[2,128,256]{2,1,0:T(8,128)(2,1)S(1)} %get-tuple-element.93), channel_id=1, source_target_pairs={{0,64},{1,65},{2,66},{3,67},{4,68},{5,69},{6,70},{7,71},{8,72},{9,... | collective-permute-start | bytes 393224 | tf_op jit(solution)/shard_map/gather_inverse/ppermute | solution.py:25
  113.1 6.5 %collective-permute-start.33 = (bf16[2,128,256]{2,1,0:T(8,128)(2,1)S(1)}, bf16[2,128,256]{2,1,0:T(8,128)(2,1)S(1)}, u32[]{:S(2)}, u32[]{:S(2)}) collective-permute-start(bf16[2,128,256]{2,1,0:T(8,128)(2,1)S(1)} %get-tuple-element.93), channel_id=1, source_target_pairs={{0,32},{1,33},{2,34},{3,35},{4,36},{5,37},{6,38},{7,39},{8,40},{9,... | collective-permute-start | bytes 393224 | tf_op jit(solution)/shard_map/gather_inverse/ppermute | solution.py:25
  115.2 4.4 %collective-permute-start.35 = (bf16[2,128,256]{2,1,0:T(8,128)(2,1)S(1)}, bf16[2,128,256]{2,1,0:T(8,128)(2,1)S(1)}, u32[]{:S(2)}, u32[]{:S(2)}) collective-permute-start(bf16[2,128,256]{2,1,0:T(8,128)(2,1)S(1)} %get-tuple-element.93), channel_id=1, source_target_pairs={{0,96},{1,97},{2,98},{3,99},{4,100},{5,101},{6,102},{7,103},{8,104... | collective-permute-start | bytes 393224 | tf_op jit(solution)/shard_map/gather_inverse/ppermute | solution.py:25
  119.7 2.0 %collective-permute-start.36 = (bf16[4,2,128,256]{3,2,1,0:T(8,128)(2,1)S(1)}, bf16[4,2,128,256]{3,2,1,0:T(8,128)(2,1)S(1)}, u32[]{:S(2)}, u32[]{:S(2)}) collective-permute-start(bf16[4,2,128,256]{3,2,1,0:T(8,128)(2,1)S(1)} %pad_maximum_fusion.2.mine), channel_id=1, source_target_pairs={{0,1},{1,0},{2,3},{3,2},{4,5},{5,4},{6,7},{7,6},{8,9},{9,8},{10,11... | collective-permute-start | bytes 1572872 | tf_op jit(solution)/shard_map/gather_inverse/ppermute | solution.py:25
  134.9 4.4 %copy-start.2 = (f32[512,1024]{1,0:T(8,128)S(1)}, f32[512,1024]{1,0:T(8,128)}, u32[]{:S(2)}) copy-start(f32[512,1024]{1,0:T(8,128)} %params.1) | copy-start | bytes 6291460
  134.9 4.4 %copy-start.3 = (f32[512,1024]{1,0:T(8,128)S(1)}, f32[512,1024]{1,0:T(8,128)}, u32[]{:S(2)}) copy-start(f32[512,1024]{1,0:T(8,128)} %momentum.1) | copy-start | bytes 6291460
  134.9 4.4 %collective-permute-start.37 = (bf16[8,1024,128]{2,1,0:T(8,128)(2,1)}, bf16[8,1024,128]{2,1,0:T(8,128)(2,1)S(1)}, u32[]{:S(2)}, u32[]{:S(2)}) collective-permute-start(bf16[8,1024,128]{2,1,0:T(8,128)(2,1)} %all-to-all-done.1.mine), channel_id=1, source_target_pairs={{0,1},{1,0},{2,3},{3,2},{4,5},{5,4},{6,7},{7,6},{8,9},{9,8},{10,11... | collective-permute-start | bytes 6291464 | tf_op jit(solution)/shard_map/gather_coef/ppermute | solution.py:25

commit v6 on v4

--- a/solution.py
+++ b/solution.py
@@ -109,11 +109,35 @@
                     out[4 * q + u, :, g * BLK : (g + 1) * BLK] = tile[:, u * BLK : (u + 1) * BLK]
 
 
-def spread_kernel(t0, t1, t2, t3, out):
-    rank = t0.shape[0]
-    for n in range(out.shape[0]):
-        for d, tile in enumerate((t0, t1, t2, t3)):
-            out[n, d * rank : (d + 1) * rank] = tile[...]
+def spread_kernel(first, *refs):
+    tiles, (out, sems) = refs[:2], refs[-2:]
+    rank = tiles[0].shape[0]
+    copies = [
+        pltpu.make_async_copy(
+            tile, out.at[n, (first + d) * rank : (first + d + 1) * rank], sems.at[d, n]
+        )
+        for n in range(out.shape[0])
+        for d, tile in enumerate(tiles)
+    ]
+    for copy in copies:
+        copy.start()
+    for copy in copies:
+        copy.wait()
+
+
+def spread_call(first, tiles, before=()):
+    rank = tiles[0].shape[0]
+    return pl.pallas_call(
+        functools.partial(spread_kernel, first),
+        in_specs=[VMEM, VMEM] + [FAR] * len(before),
+        out_specs=FAR,
+        out_shape=jax.ShapeDtypeStruct((8, 4 * rank, BLK), BF16),
+        scratch_shapes=[pltpu.SemaphoreType.DMA((2, 8))],
+        input_output_aliases={2: 0} if before else {},
+        compiler_params=pltpu.CompilerParams(vmem_limit_bytes=4 * 1024 * 1024),
+        cost_estimate=pl.CostEstimate(flops=0, bytes_accessed=1000000, transcendentals=0),
+        name="spread",
+    )(*tiles, *before)
 
 
 def inverse_kernel(place, mine, theirs, out, left):
@@ -345,7 +369,9 @@
         tiles = [
             move(v, lambda x, h, z, l, c, d=d: (x + d, c, z, l, h)) for d, v in enumerate(tiles)
         ]
-    tiles = call(spread_kernel, [pltpu.VMEM((8, 4 * rank, BLK), BF16)], 0, "spread", False)(*tiles)[0]
+    half = spread_call(0, tiles[:2])
+    *rest, half = fence((*tiles[2:], half))
+    tiles = spread_call(2, rest, (half,))
     with jax.named_scope("gather_coef"):
         mine, operand = fence((lax.all_to_all(tiles, ("z", "yl"), 0, 0, tiled=True), operand))
         theirs = shift(mine, dc=1)

time: 143 us -> 143 us (level)
    pallas_call x0 -> x2, Pallas kernels: none -> 2.18 us  [spread_call(): pl.pallas_call(functools.partial(spread_kernel, first), in_specs=[VMEM, V...]
    pallas_call x9 -> x8, Pallas kernels: 26.8 us -> 25.2 us  [run(): pl.pallas_call(kernel, in_specs=[SMEM] * smem + [VMEM] * (len(args) - sme...]
  transfers between devices with their start and end apart: 35 -> 35, of which waited for: 17 -> 17; matrix products, arithmetic and copies ran while one was open for 2% -> 2% of each run, Pallas kernels for 16% -> 17%
where the time goes in v6:
time: 143 us; the launch traced here: 142 us
  starting transfers between devices  57.9 us (40%)
  waiting for transfers between devices  46 us (32%)
  Pallas kernels  30 us (21%)
  local copies, waits for them, and re-layouts  4.51 us (3%)
  other arithmetic  2.11 us (1%)
    ppermute x33, starting transfers between devices, move(): return lax.ppermute(value, AXES, pairs)  48.7 us
    ppermute x33, waiting for transfers between devices, move(): return lax.ppermute(value, AXES, pairs)  35.8 us
    pallas_call x8, Pallas kernels, run(): pl.pallas_call(kernel, in_specs=[SMEM] * smem + [VMEM] * (len(args) - sme...  25.2 us
    all_to_all x1, waiting for transfers between devices, body(): parts = lax.all_to_all(kept, ('z', 'yl'), 0, 0, tiled=True)  10.1 us
    all_to_all x1, starting transfers between devices, body(): lax.all_to_all(tiles, ('z', 'yl'), 0, 0, tiled=True)  5.59 us
    unnamed x11, local copies, waits for them, and re-layouts  4.35 us
    all_to_all x1, starting transfers between devices, body(): parts = lax.all_to_all(kept, ('z', 'yl'), 0, 0, tiled=True)  3.62 us
  transfers between devices with their start and end apart: 35, of which 17 were waited for; matrix products, arithmetic and copies ran while one was open for 2% of the time, Pallas kernels for 17%

profile of v6, /device:TPU:1, one launch (start us, length us, event | category | flops | bytes accessed | tf_op | source)
XLA Modules:
  0.0 141.7 jit_solution(3763069391665808504)
XLA Ops:
  0.6 4.5 %collective-permute-start.2 = (bf16[512,256]{1,0:T(8,128)(2,1)}, bf16[512,256]{1,0:T(8,128)(2,1)S(1)}, u32[]{:S(2)}, u32[]{:S(2)}) collective-permute-start(bf16[512,256]{1,0:T(8,128)(2,1)} %refs_0_.1), channel_id=1, source_target_pairs={{0,8},{1,9},{2,10},{3,11},{4,12},{5,13},{6,14},{7,15},{8,0},{9,1},... | collective-permute-start | bytes 786440 | tf_op jit(solution)/shard_map/gather_sketch/ppermute | solution.py:25
  5.1 1.3 collective-permute-start.7
  6.9 1.0 collective-permute-start
  7.9 3.5 %collective-permute-done.2.refs_4_ = bf16[512,256]{1,0:T(8,128)(2,1)S(1)} collective-permute-done((bf16[512,256]{1,0:T(8,128)(2,1)}, bf16[512,256]{1,0:T(8,128)(2,1)S(1)}, u32[]{:S(2)}, u32[]{:S(2)}) %collective-permute-start.2) | collective-permute-done | bytes 262176 | tf_op jit(solution)/shard_map/gather_sketch/ppermute | solution.py:25
  11.4 2.8 %collective-permute-start.4 = (bf16[256,256]{1,0:T(8,128)(2,1)S(1)}, bf16[256,256]{1,0:T(8,128)(2,1)S(1)}, u32[]{:S(2)}, u32[]{:S(2)}) collective-permute-start(bf16[256,256]{1,0:T(8,128)(2,1)S(1)} %get-tuple-element.78), channel_id=1, source_target_pairs={{0,18},{1,19},{2,0},{3,1},{4,22},{5,23},{6,4},{7,5},{8,26},{9,27},... | collective-permute-start | bytes 393224 | tf_op jit(solution)/shard_map/gather_sketch/ppermute | solution.py:25
  14.2 2.3 %collective-permute-start.8 = (bf16[512,256]{1,0:T(8,128)(2,1)}, bf16[512,256]{1,0:T(8,128)(2,1)S(1)}, u32[]{:S(2)}, u32[]{:S(2)}) collective-permute-start(bf16[512,256]{1,0:T(8,128)(2,1)} %refs_0_.1), channel_id=1, source_target_pairs={{0,1},{1,0},{2,3},{3,2},{4,5},{5,4},{6,7},{7,6},{8,9},{9,8},{10,11... | collective-permute-start | bytes 786440 | tf_op jit(solution)/shard_map/gather_sketch/ppermute | solution.py:25
  16.6 1.0 collective-permute-done.1.refs_2_
  17.6 1.4 %collective-permute-start.12 = (bf16[512,256]{1,0:T(8,128)(2,1)S(1)}, bf16[512,256]{1,0:T(8,128)(2,1)S(1)}, u32[]{:S(2)}, u32[]{:S(2)}) collective-permute-start(bf16[512,256]{1,0:T(8,128)(2,1)S(1)} %collective-permute-done.2.refs_4_), channel_id=1, source_target_pairs={{0,1},{1,0},{2,3},{3,2},{4,5},{5,4},{6,7},{7,6},{8,9},{9,8},{10,11... | collective-permute-start | bytes 786440 | tf_op jit(solution)/shard_map/gather_sketch/ppermute | solution.py:25
  19.5 3.2 %collective-permute-start.9 = (bf16[512,256]{1,0:T(8,128)(2,1)S(1)}, bf16[512,256]{1,0:T(8,128)(2,1)S(1)}, u32[]{:S(2)}, u32[]{:S(2)}) collective-permute-start(bf16[512,256]{1,0:T(8,128)(2,1)S(1)} %collective-permute-done.refs_1_), channel_id=1, source_target_pairs={{0,1},{1,0},{2,3},{3,2},{4,5},{5,4},{6,7},{7,6},{8,9},{9,8},{10,11... | collective-permute-start | bytes 786440 | tf_op jit(solution)/shard_map/gather_sketch/ppermute | solution.py:25
  23.0 2.7 %collective-permute-start.6 = (bf16[512,256]{1,0:T(8,128)(2,1)S(1)}, bf16[512,256]{1,0:T(8,128)(2,1)S(1)}, u32[]{:S(2)}, u32[]{:S(2)}) collective-permute-start(bf16[512,256]{1,0:T(8,128)(2,1)S(1)} %collective-permute-done.1.refs_2_), channel_id=1, source_target_pairs={{0,18},{1,19},{2,0},{3,1},{4,22},{5,23},{6,4},{7,5},{8,26},{9,27},... | collective-permute-start | bytes 786440 | tf_op jit(solution)/shard_map/gather_sketch/ppermute | solution.py:25
  25.8 3.4 %copy-done = bf16[1,512,8192]{2,1,0:T(8,128)(2,1)S(1)} copy-done((bf16[1,512,8192]{2,1,0:T(8,128)(2,1)S(1)}, bf16[1,512,8192]{2,1,0:T(8,128)(2,1)}, u32[]{:S(2)}) %copy-start) | copy-done | bytes 8388632
  29.2 0.9 copy-done.4
  30.1 2.4 %sketched_early.1.refs_4_ = f32[512,256]{1,0:T(8,128)S(1)} custom-call(s32[20]{0:T(128)S(1)} %stack.97.place, bf16[512,8192]{1,0:T(8,128)(2,1)S(1)} %bitcast.28, bf16[512,256]{1,0:T(8,128)(2,1)S(1)} %copy-done.4, bf16[512,256]{1,0:T(8,128)(2,1)S(1)} %collective-permute-done.refs_1_, bf16[512,256]{1,0:T(8,128)(2,1)S(1)} %collective-permute-done.1.refs_2_, ...), custom_call_target="tpu_custom_call" | custom-call | flops 1600000000 | bytes 4194304 | tf_op jit(solution)/shard_map/sketched_early/pallas_call | solution.py:45
  32.5 1.1 collective-permute-start.14
  33.7 1.1 collective-permute-done.14.refs_2_
  35.1 2.6 %sketched_late.1 = (f32[192,128]{1,0:T(8,128)S(1)}, f32[192,128]{1,0:T(8,128)S(1)}, f32[512,256]{1,0:T(8,128)S(1)}, bf16[256,512]{1,0:T(8,128)(2,1)S(1)}) custom-call(s32[20]{0:T(128)S(1)} %stack.97.place, bf16[512,8192]{1,0:T(8,128)(2,1)S(1)} %bitcast.29, bf16[512,256]{1,0:T(8,128)(2,1)S(1)} %collective-permute-done.5.refs_0_, ...), custom_call_target="tpu_custom_call" | custom-call | flops 800000000 | bytes 4194304 | tf_op jit(solution)/shard_map/sketched_late/pallas_call | solution.py:45
  38.1 0.9 collective-permute-done.16
  39.2 2.9 %product.1 = (bf16[8,256,512]{2,1,0:T(8,128)(2,1)S(1)}, bf16[8,256,512]{2,1,0:T(8,128)(2,1)S(1)}) custom-call(s32[20]{0:T(128)S(1)} %stack.97.place, bf16[512,8192]{1,0:T(8,128)(2,1)S(1)} %bitcast.30, bf16[256,512]{1,0:T(8,128)(2,1)S(1)} %get-tuple-element.51.turned), custom_call_target="tpu_custom_call" | custom-call | flops 2200000000 | bytes 4194304 | tf_op jit(solution)/shard_map/product/pallas_call | solution.py:45
  42.1 1.1 collective-permute-done.17
  43.2 1.2 collective-permute-start.21
  44.4 3.5 %collective-permute-start.20 = (f32[192,128]{1,0:T(8,128)S(1)}, f32[192,128]{1,0:T(8,128)S(1)}, u32[]{:S(2)}, u32[]{:S(2)}) collective-permute-start(f32[192,128]{1,0:T(8,128)S(1)} %add.169), channel_id=1, source_target_pairs={{0,12},{1,13},{2,14},{3,15},{4,0},{5,1},{6,2},{7,3},{8,4},{9,5},{1... | collective-permute-start | bytes 294920 | tf_op jit(solution)/shard_map/sum_gram/ppermute | solution.py:25
  47.9 1.3 collective-permute-start.18
  49.3 2.0 %add_convert_fusion = bf16[8,256,512]{2,1,0:T(8,128)(2,1)} fusion(bf16[8,256,512]{2,1,0:T(8,128)(2,1)S(1)} %collective-permute-done.21, bf16[8,256,512]{2,1,0:T(8,128)(2,1)S(1)} %get-tuple-element.55), kind=kLoop, calls=%fused_computation | loop fusion | flops 4194304 | bytes 6291456 | tf_op jit(solution)/shard_map/sum_cores/convert_element_type | solution.py:334
  51.2 4.3 %collective-permute-done.19 = f32[192,128]{1,0:T(8,128)S(1)} collective-permute-done((f32[192,128]{1,0:T(8,128)S(1)}, f32[192,128]{1,0:T(8,128)S(1)}, u32[]{:S(2)}, u32[]{:S(2)}) %collective-permute-start.19) | collective-permute-done | bytes 98336 | tf_op jit(solution)/shard_map/sum_gram/ppermute | solution.py:25
  55.6 3.6 %all-to-all-start = ((bf16[8,256,512]{2,1,0:T(8,128)(2,1)}), bf16[8,256,512]{2,1,0:T(8,128)(2,1)S(1)}, u32[]{:S(2)}, u32[]{:S(2)}) async-start(bf16[8,256,512]{2,1,0:T(8,128)(2,1)} %add_convert_fusion), calls=%async_computation | async-start | bytes 4194304 | tf_op jit(solution)/shard_map/sum_fsdp/all_to_all | solution.py:339
  59.2 1.0 collective-permute-start.22
  60.2 0.9 collective-permute-done.22.theirs
  61.1 11.3 %inverse.1 = f32[256,256]{1,0:T(8,128)S(1)} custom-call(s32[20]{0:T(128)S(1)} %stack.97.place, f32[192,128]{1,0:T(8,128)S(1)} %add_add_fusion.mine, f32[192,128]{1,0:T(8,128)S(1)} %collective-permute-done.22.theirs), custom_call_target="tpu_custom_call" | custom-call | flops 3000000000 | bytes 4194304 | tf_op jit(solution)/shard_map/inverse/pallas_call | solution.py:45
  73.1 2.0 %collective-permute-start.23 = (bf16[512,256]{1,0:T(8,128)(2,1)S(1)}, bf16[512,256]{1,0:T(8,128)(2,1)S(1)}, u32[]{:S(2)}, u32[]{:S(2)}) collective-permute-start(bf16[512,256]{1,0:T(8,128)(2,1)S(1)} %basis.1), channel_id=1, source_target_pairs={{0,16},{1,17},{2,18},{3,19},{4,20},{5,21},{6,22},{7,23},{8,24},{9,... | collective-permute-start | bytes 786440 | tf_op jit(solution)/shard_map/gather_basis/ppermute | solution.py:25
  75.2 10.1 %all-to-all-done.parts = bf16[8,256,512]{2,1,0:T(8,128)(2,1)S(1)} async-done(((bf16[8,256,512]{2,1,0:T(8,128)(2,1)}), bf16[8,256,512]{2,1,0:T(8,128)(2,1)S(1)}, u32[]{:S(2)}, u32[]{:S(2)}) %all-to-all-start) | async-done | bytes 2097184 | tf_op jit(solution)/shard_map/sum_fsdp/all_to_all | solution.py:339
  85.3 1.5 %coef.1 = (bf16[256,128]{1,0:T(8,128)(2,1)S(1)}, bf16[256,128]{1,0:T(8,128)(2,1)S(1)}, bf16[256,128]{1,0:T(8,128)(2,1)S(1)}, bf16[256,128]{1,0:T(8,128)(2,1)S(1)}) custom-call(s32[20]{0:T(128)S(1)} %stack.97.place, f32[256,256]{1,0:T(8,128)S(1)} %inverse.1, bf16[8,256,512]{2,1,0:T(8,128)(2,1)S(1)} %all-to-all-done.parts), custom_call_target="tpu_custom_call" | custom-call | flops 400000000 | bytes 4194304 | tf_op jit(solution)/shard_map/coef/pallas_call | solution.py:45
  86.8 2.8 %collective-permute-done.23 = bf16[512,256]{1,0:T(8,128)(2,1)S(1)} collective-permute-done((bf16[512,256]{1,0:T(8,128)(2,1)S(1)}, bf16[512,256]{1,0:T(8,128)(2,1)S(1)}, u32[]{:S(2)}, u32[]{:S(2)}) %collective-permute-start.23) | collective-permute-done | bytes 262176 | tf_op jit(solution)/shard_map/gather_basis/ppermute | solution.py:25
  89.7 4.5 %collective-permute-start.26 = (bf16[256,128]{1,0:T(8,128)(2,1)S(1)}, bf16[256,128]{1,0:T(8,128)(2,1)S(1)}, u32[]{:S(2)}, u32[]{:S(2)}) collective-permute-start(bf16[256,128]{1,0:T(8,128)(2,1)S(1)} %get-tuple-element.70), channel_id=1, source_target_pairs={{0,0},{1,16},{2,2},{3,18},{4,4},{5,20},{6,6},{7,22},{8,8},{9,24},{... | collective-permute-start | bytes 196616 | tf_op jit(solution)/shard_map/exchange_coef/ppermute | solution.py:25
  94.2 1.7 %collective-permute-start.27 = (bf16[256,128]{1,0:T(8,128)(2,1)S(1)}, bf16[256,128]{1,0:T(8,128)(2,1)S(1)}, u32[]{:S(2)}, u32[]{:S(2)}) collective-permute-start(bf16[256,128]{1,0:T(8,128)(2,1)S(1)} %get-tuple-element.71), channel_id=1, source_target_pairs={{0,32},{1,48},{2,34},{3,50},{4,36},{5,52},{6,38},{7,54},{8,40},{9,... | collective-permute-start | bytes 196616 | tf_op jit(solution)/shard_map/exchange_coef/ppermute | solution.py:25
  95.8 4.8 %collective-permute-start.24 = (bf16[256,128]{1,0:T(8,128)(2,1)S(1)}, bf16[256,128]{1,0:T(8,128)(2,1)S(1)}, u32[]{:S(2)}, u32[]{:S(2)}) collective-permute-start(bf16[256,128]{1,0:T(8,128)(2,1)S(1)} %get-tuple-element.68), channel_id=1, source_target_pairs={{0,64},{1,80},{2,66},{3,82},{4,68},{5,84},{6,70},{7,86},{8,72},{9,... | collective-permute-start | bytes 196616 | tf_op jit(solution)/shard_map/exchange_coef/ppermute | solution.py:25
  100.6 1.5 %collective-permute-start.25 = (bf16[256,128]{1,0:T(8,128)(2,1)S(1)}, bf16[256,128]{1,0:T(8,128)(2,1)S(1)}, u32[]{:S(2)}, u32[]{:S(2)}) collective-permute-start(bf16[256,128]{1,0:T(8,128)(2,1)S(1)} %get-tuple-element.69), channel_id=1, source_target_pairs={{0,96},{1,112},{2,98},{3,114},{4,100},{5,116},{6,102},{7,118},{8,1... | collective-permute-start | bytes 196616 | tf_op jit(solution)/shard_map/exchange_coef/ppermute | solution.py:25
  102.1 1.1 spread.2.refs_2_
  103.4 3.3 %collective-permute-done.25.refs_1_ = bf16[256,128]{1,0:T(8,128)(2,1)S(1)} collective-permute-done((bf16[256,128]{1,0:T(8,128)(2,1)S(1)}, bf16[256,128]{1,0:T(8,128)(2,1)S(1)}, u32[]{:S(2)}, u32[]{:S(2)}) %collective-permute-start.25) | collective-permute-done | bytes 65568 | tf_op jit(solution)/shard_map/exchange_coef/ppermute | solution.py:25
  106.7 1.1 spread.3
  107.8 5.6 %all-to-all-start.1 = ((bf16[8,1024,128]{2,1,0:T(8,128)(2,1)}), bf16[8,1024,128]{2,1,0:T(8,128)(2,1)}, u32[]{:S(2)}, u32[]{:S(2)}) async-start(bf16[8,1024,128]{2,1,0:T(8,128)(2,1)} %spread.3), calls=%async_computation.1 | async-start | bytes 4194304 | tf_op jit(solution)/shard_map/gather_coef/all_to_all | solution.py:376
  113.4 2.4 %collective-permute-start.30 = (bf16[2,512,256]{2,1,0:T(8,128)(2,1)S(1)}, bf16[2,512,256]{2,1,0:T(8,128)(2,1)S(1)}, u32[]{:S(2)}, u32[]{:S(2)}) collective-permute-start(bf16[2,512,256]{2,1,0:T(8,128)(2,1)S(1)} %pad_maximum_fusion.q0), channel_id=1, source_target_pairs={{0,96},{1,97},{2,98},{3,99},{4,100},{5,101},{6,102},{7,103},{8,104... | collective-permute-start | bytes 1572872 | tf_op jit(solution)/shard_map/gather_basis/ppermute | solution.py:25
  115.8 8.5 %collective-permute-done.30.q3 = bf16[2,512,256]{2,1,0:T(8,128)(2,1)S(1)} collective-permute-done((bf16[2,512,256]{2,1,0:T(8,128)(2,1)S(1)}, bf16[2,512,256]{2,1,0:T(8,128)(2,1)S(1)}, u32[]{:S(2)}, u32[]{:S(2)}) %collective-permute-start.30) | collective-permute-done | bytes 524320 | tf_op jit(solution)/shard_map/gather_basis/ppermute | solution.py:25
  124.3 2.6 %collective-permute-start.31 = (bf16[512,256]{1,0:T(8,128)(2,1)S(1)}, bf16[512,256]{1,0:T(8,128)(2,1)S(1)}, u32[]{:S(2)}, u32[]{:S(2)}) collective-permute-start(bf16[512,256]{1,0:T(8,128)(2,1)S(1)} %slice_bitcast_fusion), channel_id=1, source_target_pairs={{0,96},{1,97},{2,98},{3,99},{4,100},{5,101},{6,102},{7,103},{8,104... | collective-permute-start | bytes 786440 | tf_op jit(solution)/shard_map/gather_basis/ppermute | solution.py:25
  127.0 3.2 %collective-permute-done.31 = bf16[512,256]{1,0:T(8,128)(2,1)S(1)} collective-permute-done((bf16[512,256]{1,0:T(8,128)(2,1)S(1)}, bf16[512,256]{1,0:T(8,128)(2,1)S(1)}, u32[]{:S(2)}, u32[]{:S(2)}) %collective-permute-start.31) | collective-permute-done | bytes 262176 | tf_op jit(solution)/shard_map/gather_basis/ppermute | solution.py:25
  130.2 3.2 %collective-permute-done.29 = bf16[512,256]{1,0:T(8,128)(2,1)S(1)} collective-permute-done((bf16[512,256]{1,0:T(8,128)(2,1)S(1)}, bf16[512,256]{1,0:T(8,128)(2,1)S(1)}, u32[]{:S(2)}, u32[]{:S(2)}) %collective-permute-start.29) | collective-permute-done | bytes 262176 | tf_op jit(solution)/shard_map/gather_basis/ppermute | solution.py:25
  134.5 3.0 %partial.1.part = f32[512,1024]{1,0:T(8,128)S(1)} custom-call(bf16[512,2048]{1,0:T(8,128)(2,1)S(1)} %lay.1.left, bf16[8,1024,128]{2,1,0:T(8,128)(2,1)} %all-to-all-done.1.mine), custom_call_target="tpu_custom_call" | custom-call | flops 1100000000 | bytes 4194304 | tf_op jit(solution)/shard_map/partial/pallas_call | solution.py:45
  137.5 1.4 collective-permute-done.32.theirs
  138.8 2.6 %update.1 = (f32[512,1024]{1,0:T(8,128)}, f32[512,1024]{1,0:T(8,128)}) custom-call(bf16[512,2048]{1,0:T(8,128)(2,1)S(1)} %lay.1.left, bf16[8,1024,128]{2,1,0:T(8,128)(2,1)S(1)} %collective-permute-done.32.theirs, f32[512,1024]{1,0:T(8,128)S(1)} %partial.1.part, f32[512,1024]{1,0:T(8,128)S(1)} %copy-done.2, f32[512,1024]{1,0:T(8,128)S(1)} %copy-done.3), custom_call_target="tpu_custom_call" | custom-call | flops 1100000000 | bytes 14000000 | tf_op jit(solution)/shard_map/update/pallas_call | solution.py:256
  (55 shorter events, 4.5 us)
Async XLA Ops:
  0.6 10.8 %collective-permute-start.2 = (bf16[512,256]{1,0:T(8,128)(2,1)}, bf16[512,256]{1,0:T(8,128)(2,1)S(1)}, u32[]{:S(2)}, u32[]{:S(2)}) collective-permute-start(bf16[512,256]{1,0:T(8,128)(2,1)} %refs_0_.1), channel_id=1, source_target_pairs={{0,8},{1,9},{2,10},{3,11},{4,12},{5,13},{6,14},{7,15},{8,0},{9,1},... | collective-permute-start | bytes 786440 | tf_op jit(solution)/shard_map/gather_sketch/ppermute | solution.py:25
  5.1 9.1 %collective-permute-start.7 = (bf16[512,256]{1,0:T(8,128)(2,1)}, bf16[512,256]{1,0:T(8,128)(2,1)S(1)}, u32[]{:S(2)}, u32[]{:S(2)}) collective-permute-start(bf16[512,256]{1,0:T(8,128)(2,1)} %refs_0_.1), channel_id=1, source_target_pairs={{0,2},{1,3},{2,16},{3,17},{4,6},{5,7},{6,20},{7,21},{8,10},{9,11},... | collective-permute-start | bytes 786440 | tf_op jit(solution)/shard_map/gather_sketch/ppermute | solution.py:25
  6.4 11.1 %collective-permute-start.1 = (bf16[512,256]{1,0:T(8,128)(2,1)}, bf16[512,256]{1,0:T(8,128)(2,1)S(1)}, u32[]{:S(2)}, u32[]{:S(2)}) collective-permute-start(bf16[512,256]{1,0:T(8,128)(2,1)} %refs_0_.1), channel_id=1, source_target_pairs={{0,12},{1,13},{2,14},{3,15},{4,0},{5,1},{6,2},{7,3},{8,4},{9,5},{1... | collective-permute-start | bytes 786440 | tf_op jit(solution)/shard_map/gather_sketch/ppermute | solution.py:25
  6.9 12.1 %collective-permute-start = (bf16[512,256]{1,0:T(8,128)(2,1)}, bf16[512,256]{1,0:T(8,128)(2,1)S(1)}, u32[]{:S(2)}, u32[]{:S(2)}) collective-permute-start(bf16[512,256]{1,0:T(8,128)(2,1)} %refs_0_.1), channel_id=1, source_target_pairs={{0,4},{1,5},{2,6},{3,7},{4,8},{5,9},{6,10},{7,11},{8,12},{9,13},{1... | collective-permute-start | bytes 786440 | tf_op jit(solution)/shard_map/gather_sketch/ppermute | solution.py:25
  11.4 7.6 %collective-permute-start.4 = (bf16[256,256]{1,0:T(8,128)(2,1)S(1)}, bf16[256,256]{1,0:T(8,128)(2,1)S(1)}, u32[]{:S(2)}, u32[]{:S(2)}) collective-permute-start(bf16[256,256]{1,0:T(8,128)(2,1)S(1)} %get-tuple-element.78), channel_id=1, source_target_pairs={{0,18},{1,19},{2,0},{3,1},{4,22},{5,23},{6,4},{7,5},{8,26},{9,27},... | collective-permute-start | bytes 393224 | tf_op jit(solution)/shard_map/gather_sketch/ppermute | solution.py:25
  14.2 5.3 %collective-permute-start.3 = (bf16[256,256]{1,0:T(8,128)(2,1)S(1)}, bf16[256,256]{1,0:T(8,128)(2,1)S(1)}, u32[]{:S(2)}, u32[]{:S(2)}) collective-permute-start(bf16[256,256]{1,0:T(8,128)(2,1)S(1)} %get-tuple-element.79), channel_id=1, source_target_pairs={{0,2},{1,3},{2,16},{3,17},{4,6},{5,7},{6,20},{7,21},{8,10},{9,11},... | collective-permute-start | bytes 393224 | tf_op jit(solution)/shard_map/gather_sketch/ppermute | solution.py:25
  14.2 8.5 %collective-permute-start.8 = (bf16[512,256]{1,0:T(8,128)(2,1)}, bf16[512,256]{1,0:T(8,128)(2,1)S(1)}, u32[]{:S(2)}, u32[]{:S(2)}) collective-permute-start(bf16[512,256]{1,0:T(8,128)(2,1)} %refs_0_.1), channel_id=1, source_target_pairs={{0,1},{1,0},{2,3},{3,2},{4,5},{5,4},{6,7},{7,6},{8,9},{9,8},{10,11... | collective-permute-start | bytes 786440 | tf_op jit(solution)/shard_map/gather_sketch/ppermute | solution.py:25
  17.6 5.4 %collective-permute-start.12 = (bf16[512,256]{1,0:T(8,128)(2,1)S(1)}, bf16[512,256]{1,0:T(8,128)(2,1)S(1)}, u32[]{:S(2)}, u32[]{:S(2)}) collective-permute-start(bf16[512,256]{1,0:T(8,128)(2,1)S(1)} %collective-permute-done.2.refs_4_), channel_id=1, source_target_pairs={{0,1},{1,0},{2,3},{3,2},{4,5},{5,4},{6,7},{7,6},{8,9},{9,8},{10,11... | collective-permute-start | bytes 786440 | tf_op jit(solution)/shard_map/gather_sketch/ppermute | solution.py:25
  19.0 3.9 %collective-permute-start.11 = (bf16[512,256]{1,0:T(8,128)(2,1)S(1)}, bf16[512,256]{1,0:T(8,128)(2,1)S(1)}, u32[]{:S(2)}, u32[]{:S(2)}) collective-permute-start(bf16[512,256]{1,0:T(8,128)(2,1)S(1)} %collective-permute-done.7.refs_3_), channel_id=1, source_target_pairs={{0,1},{1,0},{2,3},{3,2},{4,5},{5,4},{6,7},{7,6},{8,9},{9,8},{10,11... | collective-permute-start | bytes 786440 | tf_op jit(solution)/shard_map/gather_sketch/ppermute | solution.py:25
  19.0 6.7 %collective-permute-start.10 = (bf16[512,256]{1,0:T(8,128)(2,1)S(1)}, bf16[512,256]{1,0:T(8,128)(2,1)S(1)}, u32[]{:S(2)}, u32[]{:S(2)}) collective-permute-start(bf16[512,256]{1,0:T(8,128)(2,1)S(1)} %collective-permute-done.1.refs_2_), channel_id=1, source_target_pairs={{0,1},{1,0},{2,3},{3,2},{4,5},{5,4},{6,7},{7,6},{8,9},{9,8},{10,11... | collective-permute-start | bytes 786440 | tf_op jit(solution)/shard_map/gather_sketch/ppermute | solution.py:25
  19.5 6.2 %collective-permute-start.9 = (bf16[512,256]{1,0:T(8,128)(2,1)S(1)}, bf16[512,256]{1,0:T(8,128)(2,1)S(1)}, u32[]{:S(2)}, u32[]{:S(2)}) collective-permute-start(bf16[512,256]{1,0:T(8,128)(2,1)S(1)} %collective-permute-done.refs_1_), channel_id=1, source_target_pairs={{0,1},{1,0},{2,3},{3,2},{4,5},{5,4},{6,7},{7,6},{8,9},{9,8},{10,11... | collective-permute-start | bytes 786440 | tf_op jit(solution)/shard_map/gather_sketch/ppermute | solution.py:25
  22.8 3.0 %collective-permute-start.13 = (bf16[512,256]{1,0:T(8,128)(2,1)S(1)}, bf16[512,256]{1,0:T(8,128)(2,1)S(1)}, u32[]{:S(2)}, u32[]{:S(2)}) collective-permute-start(bf16[512,256]{1,0:T(8,128)(2,1)S(1)} %constant_dynamic-update-slice_fusion.refs_5_), channel_id=1, source_target_pairs={{0,1},{1,0},{2,3},{3,2},{4,5},{5,4},{6,7},{7,6},{8,9},{9,8},{10,11... | collective-permute-start | bytes 786440 | tf_op jit(solution)/shard_map/gather_sketch/ppermute | solution.py:25
  22.9 9.6 %collective-permute-start.5 = (bf16[512,256]{1,0:T(8,128)(2,1)S(1)}, bf16[512,256]{1,0:T(8,128)(2,1)S(1)}, u32[]{:S(2)}, u32[]{:S(2)}) collective-permute-start(bf16[512,256]{1,0:T(8,128)(2,1)S(1)} %collective-permute-done.refs_1_), channel_id=1, source_target_pairs={{0,2},{1,3},{2,16},{3,17},{4,6},{5,7},{6,20},{7,21},{8,10},{9,11},... | collective-permute-start | bytes 786440 | tf_op jit(solution)/shard_map/gather_sketch/ppermute | solution.py:25
  23.0 9.5 %collective-permute-start.6 = (bf16[512,256]{1,0:T(8,128)(2,1)S(1)}, bf16[512,256]{1,0:T(8,128)(2,1)S(1)}, u32[]{:S(2)}, u32[]{:S(2)}) collective-permute-start(bf16[512,256]{1,0:T(8,128)(2,1)S(1)} %collective-permute-done.1.refs_2_), channel_id=1, source_target_pairs={{0,18},{1,19},{2,0},{3,1},{4,22},{5,23},{6,4},{7,5},{8,26},{9,27},... | collective-permute-start | bytes 786440 | tf_op jit(solution)/shard_map/gather_sketch/ppermute | solution.py:25
  25.8 3.4 %copy-start = (bf16[1,512,8192]{2,1,0:T(8,128)(2,1)S(1)}, bf16[1,512,8192]{2,1,0:T(8,128)(2,1)}, u32[]{:S(2)}) copy-start(bf16[1,512,8192]{2,1,0:T(8,128)(2,1)} %param.4) | copy-start | bytes 25165828
  29.2 0.9 copy-start.4
  32.5 6.7 %copy-start.1 = (bf16[1,512,8192]{2,1,0:T(8,128)(2,1)S(1)}, bf16[1,512,8192]{2,1,0:T(8,128)(2,1)}, u32[]{:S(2)}) copy-start(bf16[1,512,8192]{2,1,0:T(8,128)(2,1)} %param.4) | copy-start | bytes 25165828
  32.5 2.2 %collective-permute-start.14 = (bf16[512,256]{1,0:T(8,128)(2,1)S(1)}, bf16[512,256]{1,0:T(8,128)(2,1)S(1)}, u32[]{:S(2)}, u32[]{:S(2)}) collective-permute-start(bf16[512,256]{1,0:T(8,128)(2,1)S(1)} %collective-permute-done.5.refs_0_), channel_id=1, source_target_pairs={{0,1},{1,0},{2,3},{3,2},{4,5},{5,4},{6,7},{7,6},{8,9},{9,8},{10,11... | collective-permute-start | bytes 786440 | tf_op jit(solution)/shard_map/gather_sketch/ppermute | solution.py:25
  33.6 1.5 %collective-permute-start.15 = (bf16[512,256]{1,0:T(8,128)(2,1)S(1)}, bf16[512,256]{1,0:T(8,128)(2,1)S(1)}, u32[]{:S(2)}, u32[]{:S(2)}) collective-permute-start(bf16[512,256]{1,0:T(8,128)(2,1)S(1)} %collective-permute-done.6.refs_1_), channel_id=1, source_target_pairs={{0,1},{1,0},{2,3},{3,2},{4,5},{5,4},{6,7},{7,6},{8,9},{9,8},{10,11... | collective-permute-start | bytes 786440 | tf_op jit(solution)/shard_map/gather_sketch/ppermute | solution.py:25
  37.7 1.4 collective-permute-start.16
  39.1 4.1 %collective-permute-start.17 = (f32[192,128]{1,0:T(8,128)S(1)}, f32[192,128]{1,0:T(8,128)S(1)}, u32[]{:S(2)}, u32[]{:S(2)}) collective-permute-start(f32[192,128]{1,0:T(8,128)S(1)} %add.168), channel_id=1, source_target_pairs={{0,2},{1,3},{2,0},{3,1},{4,6},{5,7},{6,4},{7,5},{8,10},{9,11},{10,... | collective-permute-start | bytes 294920 | tf_op jit(solution)/shard_map/sum_gram/ppermute | solution.py:25
  43.2 6.0 %collective-permute-start.21 = (bf16[8,256,512]{2,1,0:T(8,128)(2,1)S(1)}, bf16[8,256,512]{2,1,0:T(8,128)(2,1)S(1)}, u32[]{:S(2)}, u32[]{:S(2)}) collective-permute-start(bf16[8,256,512]{2,1,0:T(8,128)(2,1)S(1)} %get-tuple-element.56), channel_id=1, source_target_pairs={{0,1},{1,0},{2,3},{3,2},{4,5},{5,4},{6,7},{7,6},{8,9},{9,8},{10,11... | collective-permute-start | bytes 6291464 | tf_op jit(solution)/shard_map/sum_cores/ppermute | solution.py:25
  44.4 6.8 %collective-permute-start.20 = (f32[192,128]{1,0:T(8,128)S(1)}, f32[192,128]{1,0:T(8,128)S(1)}, u32[]{:S(2)}, u32[]{:S(2)}) collective-permute-start(f32[192,128]{1,0:T(8,128)S(1)} %add.169), channel_id=1, source_target_pairs={{0,12},{1,13},{2,14},{3,15},{4,0},{5,1},{6,2},{7,3},{8,4},{9,5},{1... | collective-permute-start | bytes 294920 | tf_op jit(solution)/shard_map/sum_gram/ppermute | solution.py:25
  47.9 7.7 %collective-permute-start.19 = (f32[192,128]{1,0:T(8,128)S(1)}, f32[192,128]{1,0:T(8,128)S(1)}, u32[]{:S(2)}, u32[]{:S(2)}) collective-permute-start(f32[192,128]{1,0:T(8,128)S(1)} %add.169), channel_id=1, source_target_pairs={{0,4},{1,5},{2,6},{3,7},{4,8},{5,9},{6,10},{7,11},{8,12},{9,13},{1... | collective-permute-start | bytes 294920 | tf_op jit(solution)/shard_map/sum_gram/ppermute | solution.py:25
  47.9 7.7 %collective-permute-start.18 = (f32[192,128]{1,0:T(8,128)S(1)}, f32[192,128]{1,0:T(8,128)S(1)}, u32[]{:S(2)}, u32[]{:S(2)}) collective-permute-start(f32[192,128]{1,0:T(8,128)S(1)} %add.169), channel_id=1, source_target_pairs={{0,8},{1,9},{2,10},{3,11},{4,12},{5,13},{6,14},{7,15},{8,0},{9,1},... | collective-permute-start | bytes 294920 | tf_op jit(solution)/shard_map/sum_gram/ppermute | solution.py:25
  55.6 29.7 %all-to-all-start = ((bf16[8,256,512]{2,1,0:T(8,128)(2,1)}), bf16[8,256,512]{2,1,0:T(8,128)(2,1)S(1)}, u32[]{:S(2)}, u32[]{:S(2)}) async-start(bf16[8,256,512]{2,1,0:T(8,128)(2,1)} %add_convert_fusion), calls=%async_computation | async-start | bytes 4194304 | tf_op jit(solution)/shard_map/sum_fsdp/all_to_all | solution.py:339
  59.2 1.9 %collective-permute-start.22 = (f32[192,128]{1,0:T(8,128)S(1)}, f32[192,128]{1,0:T(8,128)S(1)}, u32[]{:S(2)}, u32[]{:S(2)}) collective-permute-start(f32[192,128]{1,0:T(8,128)S(1)} %add_add_fusion.mine), channel_id=1, source_target_pairs={{0,1},{1,0},{2,3},{3,2},{4,5},{5,4},{6,7},{7,6},{8,9},{9,8},{10,11... | collective-permute-start | bytes 294920 | tf_op jit(solution)/shard_map/sum_gram/ppermute | solution.py:25
  73.1 16.5 %collective-permute-start.23 = (bf16[512,256]{1,0:T(8,128)(2,1)S(1)}, bf16[512,256]{1,0:T(8,128)(2,1)S(1)}, u32[]{:S(2)}, u32[]{:S(2)}) collective-permute-start(bf16[512,256]{1,0:T(8,128)(2,1)S(1)} %basis.1), channel_id=1, source_target_pairs={{0,16},{1,17},{2,18},{3,19},{4,20},{5,21},{6,22},{7,23},{8,24},{9,... | collective-permute-start | bytes 786440 | tf_op jit(solution)/shard_map/gather_basis/ppermute | solution.py:25
  89.7 12.4 %collective-permute-start.26 = (bf16[256,128]{1,0:T(8,128)(2,1)S(1)}, bf16[256,128]{1,0:T(8,128)(2,1)S(1)}, u32[]{:S(2)}, u32[]{:S(2)}) collective-permute-start(bf16[256,128]{1,0:T(8,128)(2,1)S(1)} %get-tuple-element.70), channel_id=1, source_target_pairs={{0,0},{1,16},{2,2},{3,18},{4,4},{5,20},{6,6},{7,22},{8,8},{9,24},{... | collective-permute-start | bytes 196616 | tf_op jit(solution)/shard_map/exchange_coef/ppermute | solution.py:25
  94.2 8.0 %collective-permute-start.27 = (bf16[256,128]{1,0:T(8,128)(2,1)S(1)}, bf16[256,128]{1,0:T(8,128)(2,1)S(1)}, u32[]{:S(2)}, u32[]{:S(2)}) collective-permute-start(bf16[256,128]{1,0:T(8,128)(2,1)S(1)} %get-tuple-element.71), channel_id=1, source_target_pairs={{0,32},{1,48},{2,34},{3,50},{4,36},{5,52},{6,38},{7,54},{8,40},{9,... | collective-permute-start | bytes 196616 | tf_op jit(solution)/shard_map/exchange_coef/ppermute | solution.py:25
  95.8 7.6 %collective-permute-start.24 = (bf16[256,128]{1,0:T(8,128)(2,1)S(1)}, bf16[256,128]{1,0:T(8,128)(2,1)S(1)}, u32[]{:S(2)}, u32[]{:S(2)}) collective-permute-start(bf16[256,128]{1,0:T(8,128)(2,1)S(1)} %get-tuple-element.68), channel_id=1, source_target_pairs={{0,64},{1,80},{2,66},{3,82},{4,68},{5,84},{6,70},{7,86},{8,72},{9,... | collective-permute-start | bytes 196616 | tf_op jit(solution)/shard_map/exchange_coef/ppermute | solution.py:25
  100.6 6.1 %collective-permute-start.25 = (bf16[256,128]{1,0:T(8,128)(2,1)S(1)}, bf16[256,128]{1,0:T(8,128)(2,1)S(1)}, u32[]{:S(2)}, u32[]{:S(2)}) collective-permute-start(bf16[256,128]{1,0:T(8,128)(2,1)S(1)} %get-tuple-element.69), channel_id=1, source_target_pairs={{0,96},{1,112},{2,98},{3,114},{4,100},{5,116},{6,102},{7,118},{8,1... | collective-permute-start | bytes 196616 | tf_op jit(solution)/shard_map/exchange_coef/ppermute | solution.py:25
  107.8 26.7 %all-to-all-start.1 = ((bf16[8,1024,128]{2,1,0:T(8,128)(2,1)}), bf16[8,1024,128]{2,1,0:T(8,128)(2,1)}, u32[]{:S(2)}, u32[]{:S(2)}) async-start(bf16[8,1024,128]{2,1,0:T(8,128)(2,1)} %spread.3), calls=%async_computation.1 | async-start | bytes 4194304 | tf_op jit(solution)/shard_map/gather_coef/all_to_all | solution.py:376
  113.4 10.9 %collective-permute-start.30 = (bf16[2,512,256]{2,1,0:T(8,128)(2,1)S(1)}, bf16[2,512,256]{2,1,0:T(8,128)(2,1)S(1)}, u32[]{:S(2)}, u32[]{:S(2)}) collective-permute-start(bf16[2,512,256]{2,1,0:T(8,128)(2,1)S(1)} %pad_maximum_fusion.q0), channel_id=1, source_target_pairs={{0,96},{1,97},{2,98},{3,99},{4,100},{5,101},{6,102},{7,103},{8,104... | collective-permute-start | bytes 1572872 | tf_op jit(solution)/shard_map/gather_basis/ppermute | solution.py:25
  115.8 11.1 %collective-permute-start.28 = (bf16[2,512,256]{2,1,0:T(8,128)(2,1)S(1)}, bf16[2,512,256]{2,1,0:T(8,128)(2,1)S(1)}, u32[]{:S(2)}, u32[]{:S(2)}) collective-permute-start(bf16[2,512,256]{2,1,0:T(8,128)(2,1)S(1)} %pad_maximum_fusion.q0), channel_id=1, source_target_pairs={{0,32},{1,33},{2,34},{3,35},{4,36},{5,37},{6,38},{7,39},{8,40},{9,... | collective-permute-start | bytes 1572872 | tf_op jit(solution)/shard_map/gather_basis/ppermute | solution.py:25
  124.3 5.9 %collective-permute-start.31 = (bf16[512,256]{1,0:T(8,128)(2,1)S(1)}, bf16[512,256]{1,0:T(8,128)(2,1)S(1)}, u32[]{:S(2)}, u32[]{:S(2)}) collective-permute-start(bf16[512,256]{1,0:T(8,128)(2,1)S(1)} %slice_bitcast_fusion), channel_id=1, source_target_pairs={{0,96},{1,97},{2,98},{3,99},{4,100},{5,101},{6,102},{7,103},{8,104... | collective-permute-start | bytes 786440 | tf_op jit(solution)/shard_map/gather_basis/ppermute | solution.py:25
  127.0 6.5 %collective-permute-start.29 = (bf16[512,256]{1,0:T(8,128)(2,1)S(1)}, bf16[512,256]{1,0:T(8,128)(2,1)S(1)}, u32[]{:S(2)}, u32[]{:S(2)}) collective-permute-start(bf16[512,256]{1,0:T(8,128)(2,1)S(1)} %slice_bitcast_fusion.1), channel_id=1, source_target_pairs={{0,32},{1,33},{2,34},{3,35},{4,36},{5,37},{6,38},{7,39},{8,40},{9,... | collective-permute-start | bytes 786440 | tf_op jit(solution)/shard_map/gather_basis/ppermute | solution.py:25
  134.5 4.4 %copy-start.2 = (f32[512,1024]{1,0:T(8,128)S(1)}, f32[512,1024]{1,0:T(8,128)}, u32[]{:S(2)}) copy-start(f32[512,1024]{1,0:T(8,128)} %params.1) | copy-start | bytes 6291460
  134.5 4.4 %copy-start.3 = (f32[512,1024]{1,0:T(8,128)S(1)}, f32[512,1024]{1,0:T(8,128)}, u32[]{:S(2)}) copy-start(f32[512,1024]{1,0:T(8,128)} %momentum.1) | copy-start | bytes 6291460
  134.5 4.4 %collective-permute-start.32 = (bf16[8,1024,128]{2,1,0:T(8,128)(2,1)}, bf16[8,1024,128]{2,1,0:T(8,128)(2,1)S(1)}, u32[]{:S(2)}, u32[]{:S(2)}) collective-permute-start(bf16[8,1024,128]{2,1,0:T(8,128)(2,1)} %all-to-all-done.1.mine), channel_id=1, source_target_pairs={{0,1},{1,0},{2,3},{3,2},{4,5},{5,4},{6,7},{7,6},{8,9},{9,8},{10,11... | collective-permute-start | bytes 6291464 | tf_op jit(solution)/shard_map/gather_coef/ppermute | solution.py:25
